TPU v7x, 32 devices: a whole 2x2x4 slice. The times are simulated.
32 devices in a mesh: rep: 2 (over y), fsdp: 16 (over z, x, core).
Axes of the slice: x: 2, y: 2, z: 4, core: 2. Of those that a mesh axis runs over, the one named last changes fastest.
Arguments:
- tokens: bfloat16 [37632, 768], P(('rep', 'fsdp')), may hold values from -6 to 6
- mask_flags: int32 [192, 196], P(('rep', 'fsdp')), may hold values 0 or 1
- mask_token: bfloat16 [768], P('fsdp'), may hold values from -4 to 4
- norm1_gain: bfloat16 [768], P('fsdp'), may hold values from 0.099609375 to 1.8984375
- norm1_bias: bfloat16 [768], P('fsdp'), may hold values from -1.5 to 1.5
- qkv_weight: bfloat16 [768, 2304], P('fsdp'), may hold values from -0.21875 to 0.21875
- query_bias: bfloat16 [768], P('fsdp'), may hold values from -1.5 to 1.5
- value_bias: bfloat16 [768], P('fsdp'), may hold values from -1.5 to 1.5
- proj_weight: bfloat16 [768, 768], P('fsdp'), may hold values from -1.75 to 1.75
- proj_bias: bfloat16 [768], P('fsdp'), may hold values from -1.5 to 1.5
- norm2_gain: bfloat16 [768], P('fsdp'), may hold values from 0.099609375 to 1.8984375
- norm2_bias: bfloat16 [768], P('fsdp'), may hold values from -1.5 to 1.5
- fc1_weight: bfloat16 [768, 3072], P('fsdp'), may hold values from -0.21875 to 0.21875
- fc1_bias: bfloat16 [3072], P('fsdp'), may hold values from -1.5 to 1.5
- fc2_weight: bfloat16 [3072, 768], P('fsdp'), may hold values from -0.109375 to 0.109375
- fc2_bias: bfloat16 [768], P('fsdp'), may hold values from -1.5 to 1.5
- out_grad: bfloat16 [37632, 768], P(('rep', 'fsdp')), may hold values from -6 to 6
Outputs:
- block_out: bfloat16 [37632, 768], P(('rep', 'fsdp'))
- input_grad: float32 [37632, 768], P(('rep', 'fsdp'))
- grad_mask_token: float32 [768], P('fsdp')
- grad_norm1_gain: float32 [768], P('fsdp')
- grad_norm1_bias: float32 [768], P('fsdp')
- grad_qkv_weight: float32 [768, 2304], P('fsdp')
- grad_query_bias: float32 [768], P('fsdp')
- grad_value_bias: float32 [768], P('fsdp')
- grad_proj_weight: float32 [768, 768], P('fsdp')
- grad_proj_bias: float32 [768], P('fsdp')
- grad_norm2_gain: float32 [768], P('fsdp')
- grad_norm2_bias: float32 [768], P('fsdp')
- grad_fc1_weight: float32 [768, 3072], P('fsdp')
- grad_fc1_bias: float32 [3072], P('fsdp')
- grad_fc2_weight: float32 [3072, 768], P('fsdp')
- grad_fc2_bias: float32 [768], P('fsdp')
Inputs may be any that keep to these rules, and one draw needn't show every extreme that they name: `mask_flags`: 1 marks a patch replaced by the mask token.
All inputs are finite; a program needn't handle non-finite values. No bound on the sum of `mask_flags` on one device may be relied on, other than what follows from the above.
Results may differ from a plain program's by a relative error of at most 0.012.
Values may be sent and summed in bfloat16 or wider, within the bound.
No kernel may reach another device: no remote copies, remote signals or barrier semaphores. Data moves between devices by JAX's collectives and lax.ppermute only.
A program may use at most 256 MiB of HBM per device.

v0:
```python
import functools
import math

import jax
import jax.numpy as jnp
from jax import lax
from jax.experimental import pallas as pl
from jax.experimental.pallas import tpu as pltpu
from jax.sharding import PartitionSpec as P

F32 = jnp.float32
BF16 = jnp.bfloat16
HEAD = 64
GROUP = 256
NEG = -1e30
VMEM = 56 * 2**20


def dot(a, b):
    return lax.dot_general(a, b, (((1,), (0,)), ((), ())), preferred_element_type=F32)


def dot_rows(a, b):
    return lax.dot_general(a, b, (((0,), (0,)), ((), ())), preferred_element_type=F32)


def dot_cols(a, b):
    return lax.dot_general(a, b, (((1,), (1,)), ((), ())), preferred_element_type=F32)


FAR = 4


class Place:
    def __init__(self, count):
        self.count = count

    def own(self):
        index = lax.axis_index("fsdp")
        return index // 4, (index // 2) % 2, index % 2

    def swap(self, bits):
        return [(i, i ^ bits) for i in range(self.count)]

    def core(self, v):
        return lax.ppermute(v, "fsdp", self.swap(1))

    def along_x(self, v):
        return lax.ppermute(v, "fsdp", self.swap(2))

    def along_z(self, d):
        return lambda v: lax.ppermute(v, "fsdp", self.swap(4 * d))

    def along_y(self, v):
        return lax.ppermute(v, "rep", [(0, 1), (1, 0)])

    def along_xy(self, v):
        n = self.count
        return lax.ppermute(
            v, ("rep", "fsdp"), [(y * n + i, (1 - y) * n + (i ^ 2)) for y in range(2) for i in range(n)]
        )


def shard_at(own, dc, dx, dz):
    z, x, c = own
    return (lax.bitwise_xor(z, dz) * 2 + lax.bitwise_xor(x, dx)) * 2 + lax.bitwise_xor(c, dc)


def add_low(*terms):
    total = terms[0].astype(F32)
    for term in terms[1:]:
        total = total + term.astype(F32)
    return total


def low(v):
    return v.astype(BF16)


def by_side(side, first, second, axis):
    return jnp.where(side == 0, jnp.concatenate([first, second], axis), jnp.concatenate([second, first], axis))


class Weight:
    def __init__(self, kind, arrays):
        self.kind = kind
        self.arrays = arrays


def gather_fast(place, stack):
    came = yield [(place.along_z(d), stack) for d in range(1, FAR)]
    own = jnp.stack([stack] + came)
    beside, own_core = yield [(place.along_x, own), (place.core, own)]
    (beside_core,) = yield [(place.core, beside)]
    return Weight("rows", [own, beside, own_core, beside_core])


def half_columns(stack):
    half = stack.shape[2] // 2
    return lax.dynamic_slice_in_dim(stack, lax.axis_index("rep") * half, half, axis=2)


def gather_wide(place, stack):
    mine = half_columns(stack)
    came = yield [(place.along_z(d), mine) for d in range(1, FAR)]
    own = jnp.stack([mine] + came)
    came = yield [(place.along_x, own), (place.along_y, own), (place.along_xy, own)]
    here = jnp.stack([own] + came)
    (across,) = yield [(place.core, here)]
    return Weight("halves", [here, across])


def gather_even(place, stack):
    mine = half_columns(stack)
    came = yield [(place.along_z(d), mine) for d in range(1, FAR)]
    own = jnp.stack([mine] + came)
    beside, twin = yield [(place.along_x, own), (place.along_y, own)]
    corner = yield [(place.along_y, beside[:2]), (place.along_x, twin[2:])]
    here = jnp.stack([own, beside, twin, jnp.concatenate(corner)])
    (across,) = yield [(place.core, here)]
    return Weight("halves", [here, across])


def gather_late_y(place, stack):
    mine = half_columns(stack)
    came = yield [(place.along_z(d), mine) for d in range(1, FAR)]
    own = jnp.stack([mine] + came)
    (beside,) = yield [(place.along_x, own)]
    side = jnp.stack([own, beside])
    (twin,) = yield [(place.along_y, side)]
    here = jnp.concatenate([side, twin])
    (across,) = yield [(place.core, here)]
    return Weight("halves", [here, across])


def scatter_early_y(place, keep, send):
    (came,) = yield [(place.core, send)]
    (came_y,) = yield [(place.along_y, low(add_low(keep[1], came[1])))]
    (came_x,) = yield [(place.along_x, low(add_low(keep[0, 1], came[0, 1], came_y[1])))]
    total = low(add_low(keep[0, 0], came[0, 0], came_y[0], came_x))
    came = yield [(place.along_z(d), total[d]) for d in range(1, FAR)]
    return low(add_low(total[0], *came))


def scatter_wide(place, keep, send):
    (came,) = yield [(place.core, send)]

    def pair(dy, dx):
        return low(add_low(keep[dy, dx], came[dy, dx]))

    came_xy = yield [(place.along_x, pair(0, 1)), (place.along_y, pair(1, 0)), (place.along_xy, pair(1, 1))]
    total = low(add_low(keep[0, 0], came[0, 0], *came_xy))
    came = yield [(place.along_z(d), total[d]) for d in range(1, FAR)]
    return low(add_low(total[0], *came))


def send_twin(place, *mine):
    twins = yield [(place.along_y, v) for v in mine]
    return list(mine), twins


class Flow:
    def __init__(self):
        self.live = {}
        self.done = {}

    def begin(self, name, steps):
        self.live[name] = (steps, next(steps), None)

    def send(self, *arrays):
        waiting = [name for name, (_, pairs, sent) in self.live.items() if sent is None]
        flat = [v for name in waiting for _, v in self.live[name][1]]
        flat = list(lax.optimization_barrier(tuple(flat) + tuple(arrays)))
        for name in waiting:
            steps, pairs, _ = self.live[name]
            sent = [move(v) for (move, _), v in zip(pairs, flat)]
            flat = flat[len(pairs) :]
            self.live[name] = (steps, pairs, sent)
        return flat

    def meet(self, names, *arrays):
        names = [name for name in names if name in self.live]
        flat = [v for name in names for v in self.live[name][2]]
        flat = list(lax.optimization_barrier(tuple(flat) + tuple(arrays)))
        for name in names:
            steps, pairs, _ = self.live[name]
            mine, flat = flat[: len(pairs)], flat[len(pairs) :]
            try:
                self.live[name] = (steps, steps.send(mine), None)
            except StopIteration as stop:
                del self.live[name]
                self.done[name] = stop.value
        return flat

    def turn(self, names, *arrays):
        return self.send(*self.meet(names, *arrays))


def half_at(dy, width):
    at = lax.bitwise_xor(lax.axis_index("rep"), dy) * width
    return pl.ds(pl.multiple_of(at, 128), width)


def load_weight(place, kind, rows, refs, spot, lead=0):
    own = place.own()
    for dc in range(2):
        for dx in range(2):
            for d in range(FAR):
                at = pl.ds(pl.multiple_of(shard_at(own, dc, dx, d) * rows, 16), rows)
                if kind == "rows":
                    spot[at, :] = refs[2 * dc + dx][d, lead, :rows]
                else:
                    for dy in range(2):
                        spot[at, half_at(dy, refs[0].shape[-1])] = refs[dc][2 * dy + dx, d, lead]


def store_grad(place, spot, keep, send, lead=0):
    own = place.own()
    rows, width = keep.shape[-2:]
    for dc, ref in enumerate((keep, send)):
        for dx in range(2):
            for d in range(FAR):
                at = pl.ds(pl.multiple_of(shard_at(own, dc, dx, d) * rows, 16), rows)
                if len(keep.shape) == 5:
                    ref[dx, d, lead] = spot[at, :]
                else:
                    for dy in range(2):
                        ref[dy, dx, d, lead] = spot[at, half_at(dy, width)]


def norm_stats(v):
    mean = jnp.mean(v, axis=-1, keepdims=True)
    centred = v - mean
    spread = jnp.mean(centred * centred, axis=-1, keepdims=True)
    scale = lax.rsqrt(spread + 1e-06)
    return centred * scale, scale


def norm_back(up, xhat, scale, gain):
    e = up * gain
    return (e - jnp.mean(e, axis=-1, keepdims=True) - xhat * jnp.mean(e * xhat, axis=-1, keepdims=True)) * scale


ERF_P = 0.3275911 / math.sqrt(2.0)
ERF_A = (0.254829592, -0.284496736, 1.421413741, -1.453152027, 1.061405429)


def gelu_and_slope(z):
    t = 1.0 / (1.0 + ERF_P * jnp.abs(z))
    e = jnp.exp(-0.5 * (z * z))
    poly = 0.5 * ERF_A[4]
    for a in ERF_A[3::-1]:
        poly = poly * t + 0.5 * a
    q = poly * t * e
    phi = jnp.where(z > 0, 1.0 - q, q)
    return z * phi, phi + z * (e * (1.0 / math.sqrt(2.0 * math.pi)))


class Rows:
    def __init__(self, images, patches):
        self.images = images
        self.patches = patches
        self.pad = -(-patches // 16) * 16
        self.all = images * self.pad
        self.raw = images * patches

    def block(self, width, count=1):
        return pl.BlockSpec((self.pad * count, width), lambda j: (j, 0))


def flag_column(rows, flags):
    wide = flags[...].astype(F32)
    wide = jnp.concatenate([wide, jnp.zeros((8 - rows.images, rows.patches), F32)], axis=0)
    gap = -rows.patches % 128
    return jnp.concatenate([wide, jnp.zeros((8, gap), F32)], axis=1).T


def padded_image(rows, ref, i):
    lo = rows.patches * i
    first = lo // 16 * 16
    last = min(-(-(lo + rows.patches) // 16) * 16, rows.raw)
    part = ref[first:last, :].astype(F32)[lo - first : lo - first + rows.patches]
    return jnp.concatenate([part, jnp.zeros((rows.pad - rows.patches, ref.shape[1]), F32)], axis=0)


def pad_kernel(rows, tokens, grads, base_o, grad_o):
    j = pl.program_id(0)

    def image(i):
        base_o[...] = padded_image(rows, tokens, i).astype(BF16)
        grad_o[...] = padded_image(rows, grads, i).astype(BF16)

    for i in range(rows.images):
        pl.when(j == i)(functools.partial(image, i))


def norm_one_kernel(rows, tokens, flags, vec, base_o, norm_o):
    cols = flag_column(rows, flags)
    row = lax.broadcasted_iota(jnp.int32, (rows.pad, 1), 0)
    for i in range(rows.images):
        at = pl.ds(i * rows.pad, rows.pad)
        masked = jnp.logical_and(cols[: rows.pad, i : i + 1] > 0.5, row < rows.patches)
        base = jnp.where(masked, vec[0:1, :], tokens[at, :].astype(F32))
        base_o[at, :] = base.astype(BF16)
        xhat, _ = norm_stats(base)
        norm_o[at, :] = (xhat * vec[1:2, :] + vec[2:3, :]).astype(BF16)


def whole(shape):
    return pl.BlockSpec(shape, lambda *j: (0,) * len(shape))


def params():
    return pltpu.CompilerParams(vmem_limit_bytes=VMEM)


SCALE = 0.01


def cost(micros):
    return pl.CostEstimate(flops=int(micros * SCALE * 1.15e9), bytes_accessed=int(micros * SCALE * 3e6), transcendentals=0)


def pad_call(rows, tokens, grads):
    width = tokens.shape[1]
    out = jax.ShapeDtypeStruct((rows.all, width), BF16)
    return pl.pallas_call(
        functools.partial(pad_kernel, rows),
        grid=(rows.images,),
        in_specs=[whole(tokens.shape), whole(grads.shape)],
        out_specs=[rows.block(width)] * 2,
        out_shape=[out, out],
        compiler_params=params(),
        cost_estimate=cost(5),
        name="pad_rows",
    )(tokens, grads)


def norm_one_call(rows, tokens, flags, vec):
    out = jax.ShapeDtypeStruct(tokens.shape, BF16)
    return pl.pallas_call(
        functools.partial(norm_one_kernel, rows),
        out_shape=[out, out],
        compiler_params=params(),
        cost_estimate=cost(5),
        name="norm_one",
    )(tokens, flags, vec)


def pack_kernel(count, quarter, *refs):
    *vectors, wide, qkv, proj, up, down = refs[: -2 - quarter // 2]
    first_o, second_o, *ff_o = refs[-2 - quarter // 2 :]
    r, width = proj.shape

    def group(g):
        return [qkv[:, i * width + g * GROUP : i * width + (g + 1) * GROUP] for i in range(3)]

    for i, part in enumerate(group(0)):
        first_o[0, :r, i * GROUP : (i + 1) * GROUP] = part
    small = [v[...].astype(F32) for v in vectors]
    small += [wide[:, r * i : r * (i + 1)].astype(F32) for i in range(quarter)]
    small = jnp.concatenate(small + [jnp.zeros((16 - len(small), r), F32)], axis=0)
    first_o[0, r:, :] = jnp.concatenate([small, jnp.zeros((16, width - r), F32)], axis=1).astype(BF16)
    for g in (1, 2):
        for i, part in enumerate(group(g)):
            second_o[g - 1, :, i * GROUP : (i + 1) * GROUP] = part
    second_o[2] = proj[...]
    for t in range(quarter):
        out = ff_o[t // 2]
        cols = [up[:, (k * quarter + t) * r : (k * quarter + t + 1) * r] for k in range(count)]
        out[t % 2 * 2] = jnp.concatenate(cols, axis=1)
        out[t % 2 * 2 + 1] = down[t * r : (t + 1) * r, :]


def pack_call(count, vectors, wide, qkv, proj, up, down):
    r, width = proj.shape
    quarter = up.shape[1] // width
    shapes = [(1, r + 16, width), (3, r, width)] + [(4, r, width)] * (quarter // 2)
    return pl.pallas_call(
        functools.partial(pack_kernel, count, quarter),
        out_shape=[jax.ShapeDtypeStruct(shape, BF16) for shape in shapes],
        compiler_params=params(),
        cost_estimate=cost(2.5),
        name="pack",
    )(*[v[None] for v in vectors], wide[None], qkv, proj, up, down)


def unpack_kernel(count, quarter, *refs):
    sums, (qkv_o, proj_o, up_o, down_o) = refs[:6], refs[6:]
    r = proj_o.shape[0]
    width = proj_o.shape[1]

    def added(k):
        return [sums[2 * k][b].astype(F32) + sums[2 * k + 1][b].astype(F32) for b in range(sums[2 * k].shape[0])]

    def joined(k):
        out = []
        for b in range(sums[2 * k].shape[0]):
            mine, twin = sums[2 * k][b].astype(F32), sums[2 * k + 1][b].astype(F32)
            here = jnp.concatenate([mine, twin], axis=1)
            there = jnp.concatenate([twin, mine], axis=1)
            out.append(jnp.where(lax.axis_index("rep") == 0, here, there))
        return out

    ff = added(0) + joined(1)
    heads = joined(2)
    proj_o[...] = heads[0]
    for g in range(3):
        for i in range(3):
            qkv_o[:, i * width + g * GROUP : i * width + (g + 1) * GROUP] = heads[1 + g][:, i * GROUP : (i + 1) * GROUP]
    ups = [ff[2 * t] for t in range(quarter)]
    up_o[...] = jnp.concatenate([ups[t][:, k * r : (k + 1) * r] for k in range(count) for t in range(quarter)], axis=1)
    for t in range(quarter):
        down_o[t * r : (t + 1) * r, :] = ff[2 * t + 1]


def unpack_call(count, quarter, sums):
    r, width = sums[0].shape[1:]
    shapes = [(r, 3 * width), (r, width), (r, quarter * width), (quarter * r, width)]
    return pl.pallas_call(
        functools.partial(unpack_kernel, count, quarter),
        out_shape=[jax.ShapeDtypeStruct(shape, F32) for shape in shapes],
        compiler_params=params(),
        cost_estimate=cost(3),
        name="unpack",
    )(*sums)


def halves(x, first):
    zero = jnp.zeros_like(x)
    return jnp.concatenate([jnp.where(first, x, zero), jnp.where(first, zero, x)], axis=0)


def attend_kernel(place, kind, nw, before, rows, base_group, norm, vec, *refs):
    w_in, (q_o, k_o, v_o, att_o, p_o, w_o) = refs[:nw], refs[nw + before :]
    j = pl.program_id(0)
    w = w_o.at[0]
    if kind == "whole":
        w[...] = w_in[0][0]
    else:
        load_weight(place, kind, norm.shape[1] // place.count, w_in, w)
    x = norm[...]
    lanes = pl.ds(pl.multiple_of((base_group + j) * GROUP, GROUP), GROUP)
    q_o[0] = ((dot(x, w[:, 0:GROUP]) + vec[3:4, lanes]).astype(BF16) * 0.125).astype(BF16)
    k_o[0] = dot(x, w[:, GROUP : 2 * GROUP]).astype(BF16)
    v_o[0] = (dot(x, w[:, 2 * GROUP :]) + vec[4:5, lanes]).astype(BF16)
    s = rows.pad
    first = lax.broadcasted_iota(jnp.int32, (s, 128), 1) < HEAD
    live = lax.broadcasted_iota(jnp.int32, (s, 2 * s), 0) < rows.patches

    def image(i):
        at = pl.ds(pl.multiple_of(i * s, 16), s)
        for p in range(2):
            cols = pl.ds(128 * p, 128)
            q, k, v = q_o[0, at, cols], k_o[0, at, cols], v_o[0, at, cols]
            score = jnp.where(live, dot_cols(k, halves(q, first)), NEG)
            peak = jnp.max(score, axis=0, keepdims=True)
            e = jnp.exp(score - peak)
            probs = (e * (1.0 / jnp.sum(e, axis=0, keepdims=True))).astype(BF16)
            p_o[0, p, i] = probs
            o = dot_rows(probs, v)
            att_o[0, at, cols] = jnp.where(first, o[:s], o[s:]).astype(BF16)

    def step(i, carry):
        for u in range(3):
            image(i * 3 + u)
        return carry

    lax.fori_loop(0, rows.images // 3, step, 0)


def piece_specs(weight, blocks=1, first=0):
    if weight.kind == "whole":
        return [pl.BlockSpec((blocks, *weight.arrays[0].shape[1:]), lambda j: (first + j, 0, 0))]
    if weight.kind == "rows":
        z, _, r, w = weight.arrays[0].shape
        return [pl.BlockSpec((z, blocks, r, w), lambda j: (0, first + j, 0, 0))] * 4
    k, z, _, r, w = weight.arrays[0].shape
    return [pl.BlockSpec((k, z, blocks, r, w), lambda j: (0, 0, first + j, 0, 0))] * 2


def attend_call(place, rows, group, groups, norm, vec, weight, before=()):
    s = rows.pad
    width = norm.shape[1]
    row = pl.BlockSpec((1, rows.all, GROUP), lambda j: (group + j, 0, 0))
    out = jax.ShapeDtypeStruct((3, rows.all, GROUP), BF16)
    outs = [out] * 4 + [jax.ShapeDtypeStruct((3, 2, rows.images, s, 2 * s), BF16)]
    specs = [row] * 4 + [pl.BlockSpec((1, 2, rows.images, s, 2 * s), lambda j: (group + j, 0, 0, 0, 0))]
    outs.append(jax.ShapeDtypeStruct((3, width, 3 * GROUP), BF16))
    specs.append(pl.BlockSpec((1, width, 3 * GROUP), lambda j: (group + j, 0, 0)))
    args = [norm, vec, *weight.arrays, *before]
    first = len(args) - len(before)
    return pl.pallas_call(
        functools.partial(attend_kernel, place, weight.kind, len(weight.arrays), len(before), rows, group),
        grid=(groups,),
        in_specs=[whole(norm.shape), whole(vec.shape)]
        + piece_specs(weight)
        + [pl.BlockSpec(memory_space=pl.ANY)] * len(before),
        out_specs=specs,
        out_shape=outs,
        input_output_aliases={first + i: i for i in range(len(before))},
        compiler_params=params(),
        cost_estimate=cost(2 + 6 * groups),
        name="attend",
    )(*args)


def project_kernel(place, kind, nw, spot, vec, base, att, *refs):
    w_in, (resid_o, norm_o, w_o) = refs[:nw], refs[nw:]

    @pl.when(pl.program_id(0) == 0)
    def _():
        if kind == "whole":
            w_o[0] = w_in[0][0]
        else:
            load_weight(place, kind, base.shape[1] // place.count, w_in, w_o.at[0])

    both = jnp.concatenate([att[g] for g in range(att.shape[0])], axis=1)
    total = dot(both, w_o[0]) + base[...].astype(F32) + vec[5:6, :]
    resid_o[...] = total
    xhat, _ = norm_stats(total)
    norm_o[...] = (xhat * vec[6:7, :] + vec[7:8, :]).astype(BF16)


def project_call(place, rows, vec, base, att, weight, spot):
    width = base.shape[1]
    outs = [
        jax.ShapeDtypeStruct((rows.all, width), F32),
        jax.ShapeDtypeStruct((rows.all, width), BF16),
        jax.ShapeDtypeStruct((1, width, width), BF16),
    ]
    some = rows.images // 3
    pieces = [
        pl.BlockSpec(block.block_shape, lambda j, at=block.index_map(0): at)
        for block in piece_specs(weight, 1, spot)
    ]
    return pl.pallas_call(
        functools.partial(project_kernel, place, weight.kind, len(weight.arrays), spot),
        grid=(3,),
        in_specs=[whole(vec.shape), rows.block(width, some)]
        + [pl.BlockSpec((3, rows.pad * some, GROUP), lambda j: (0, j, 0))]
        + pieces,
        out_specs=[rows.block(width, some)] * 2 + [whole(outs[2].shape)],
        out_shape=outs,
        compiler_params=params(),
        cost_estimate=cost(7),
        name="project",
    )(vec, base, att, *weight.arrays)


def feed_kernel(place, kind, form, nw, rows, block, carried, norm, grad, vec, *refs):
    w_in, rest = refs[:nw], refs[nw:]
    if carried:
        (acc_in, gn_in), rest = rest[:2], rest[carried:]
    acc_o, gn_o, bias_o = rest[:3]
    j = pl.program_id(0)
    n = 1 if form == "whole" else 2
    grads_o, act_s, gp_s, rest = rest[3 : 3 + n], rest[3 + n], rest[4 + n], rest[5 + n :]
    if kind == "whole":
        w_up, w_down = w_in[0].at[0], w_in[0].at[1]
    else:
        w_up, w_down, rest = *rest[:2], rest[2:]
        r = norm.shape[1] // place.count
        load_weight(place, kind, r, w_in, w_up, 0)
        load_weight(place, kind, r, w_in, w_down, 1)

    @pl.when(j == 0)
    def _():
        if carried:
            acc_o[...] = acc_in[...]
            gn_o[...] = gn_in[...]
        else:
            acc_o[...] = jnp.zeros_like(acc_o)
            gn_o[...] = jnp.zeros_like(gn_o)

    bias = vec[pl.ds(9 + block + j, 1), :]
    step = rows.pad
    for b in range(rows.images):
        at = pl.ds(b * step, step)
        z = dot(norm[at, :], w_up[...]) + bias
        up = dot_cols(grad[at, :], w_down[...])
        act, slope = gelu_and_slope(z)
        act = act.astype(BF16)
        gp = (up * slope).astype(BF16)
        act_s[at, :] = act
        gp_s[at, :] = gp
        acc_o[at, :] += dot(act, w_down[...])
        gn_o[at, :] += dot_cols(gp, w_up[...])
    bias_o[0] = jnp.sum(gp_s[...].astype(F32), axis=0, keepdims=True)
    for i, (left, right) in enumerate(((norm, gp_s), (act_s, grad))):
        value = dot_rows(left[...], right[...]).astype(BF16)
        if form == "whole":
            grads_o[0][i] = value
        else:
            rest[0][...] = value
            store_grad(place, rest[0], *grads_o, i)


def grad_out(kind, blocks, width, r, per_step):
    if kind == "whole":
        return (
            [jax.ShapeDtypeStruct((blocks, width, width), BF16)],
            [pl.BlockSpec((per_step, width, width), lambda j: (j, 0, 0))],
        )
    if kind == "few":
        lead, w = (2, FAR), width
    else:
        lead, w = (2, 2, FAR), width // 2
    zero = (0,) * len(lead)
    return (
        [jax.ShapeDtypeStruct((*lead, blocks, r, w), BF16)] * 2,
        [pl.BlockSpec((*lead, per_step, r, w), lambda j: (*zero, j, 0, 0))] * 2,
    )


def feed_call(place, rows, block, blocks, spot, norm, grad, vec, weight, form, r, carried):
    width = norm.shape[1]
    acc = jax.ShapeDtypeStruct((rows.all, width), F32)
    outs, specs = grad_out(form, 2 * blocks, width, r, 2)
    scratch = [pltpu.VMEM((rows.all, width), BF16)] * 2
    scratch += [pltpu.VMEM((width, width), BF16)] * ((2 if weight.kind != "whole" else 0) + (form != "whole"))
    args = [norm, grad, vec, *weight.arrays, *carried]
    in_specs = [whole(norm.shape), whole(grad.shape), whole(vec.shape)] + piece_specs(weight, 2, spot)
    in_specs += [whole(acc.shape)] * len(carried)
    return pl.pallas_call(
        functools.partial(feed_kernel, place, weight.kind, form, len(weight.arrays), rows, block, len(carried)),
        grid=(blocks,),
        in_specs=in_specs,
        out_specs=[whole(acc.shape)] * 2 + [pl.BlockSpec((1, 1, width), lambda j: (j, 0, 0))] + specs,
        out_shape=[acc, acc, jax.ShapeDtypeStruct((blocks, 1, width), F32)] + outs,
        scratch_shapes=scratch,
        compiler_params=params(),
        cost_estimate=cost(15 * blocks),
        name="feed",
    )(*args)


def middle_kernel(rows, resid, acc, gn, grad, vec, w, out_o, low_o, da_o, sums_o):
    xhat, scale = norm_stats(resid[...])
    gain = vec[6:7, :]
    up = gn[...]
    g = grad[...].astype(F32)
    total = g + norm_back(up, xhat, scale, gain)
    lowered = total.astype(BF16)
    low_o[...] = lowered
    da_o[...] = dot_cols(lowered, w[0]).astype(BF16)
    sums = jnp.concatenate(
        [
            jnp.sum(total, axis=0, keepdims=True),
            jnp.sum(up * xhat, axis=0, keepdims=True),
            jnp.sum(up, axis=0, keepdims=True),
            jnp.sum(g, axis=0, keepdims=True),
        ],
        axis=0,
    )
    final = resid[...] + acc[...] + vec[8:9, :]
    j = pl.program_id(0)
    for i in range(rows.images):

        @pl.when(j == i)
        def _():
            sums_o[...] = sums if i == 0 else sums_o[...] + sums
            out_o[rows.patches * i : rows.patches * (i + 1), :] = final[: rows.patches]


def middle_call(rows, resid, acc, gn, grad, vec, weight):
    width = resid.shape[1]
    block = rows.block(width)
    outs = [
        jax.ShapeDtypeStruct((rows.raw, width), BF16),
        jax.ShapeDtypeStruct((rows.all, width), BF16),
        jax.ShapeDtypeStruct((rows.all, width), BF16),
        jax.ShapeDtypeStruct((4, width), F32),
    ]

    def kernel(resid, acc, gn, grad, vec, w, out_o, low_o, da_o, sums_o, out_s):
        middle_kernel(rows, resid, acc, gn, grad, vec, w, out_s, low_o, da_o, sums_o)

        @pl.when(pl.program_id(0) == rows.images - 1)
        def _():
            out_o[...] = out_s[...].astype(BF16)

    return pl.pallas_call(
        kernel,
        grid=(rows.images,),
        in_specs=[block] * 4 + [whole(vec.shape), whole(weight.shape)],
        out_specs=[whole(outs[0].shape), block, block, whole(outs[3].shape)],
        out_shape=outs,
        scratch_shapes=[pltpu.VMEM((rows.raw, width), F32)],
        compiler_params=params(),
        cost_estimate=cost(12),
        name="middle",
    )(resid, acc, gn, grad, vec, weight)


STEP = 2


def attend_back_kernel(place, kind, rows, projects, norm, da, *refs):
    g, j = pl.program_id(0), pl.program_id(1)
    q_i, k_i, v_i, p_i, refs = *refs[:4], refs[4:]
    if projects:
        (lowered, *atts), refs = refs[: 1 + projects], refs[1 + projects :]
    d_o, bias_o = refs[:2]
    if kind == "whole":
        (grads_o,) = refs[2:]
    else:
        keep, send, g_s = refs[2:]
    s = rows.pad
    some = rows.images // STEP
    first = lax.broadcasted_iota(jnp.int32, (s, 128), 1) < HEAD

    def emit(value, spot):
        if kind == "whole":
            grads_o[spot] = value.astype(BF16)
        else:
            g_s[...] = value.astype(BF16)
            store_grad(place, g_s, keep, send, spot)

    for i in range(some):
        at = pl.ds(i * s, s)
        to = pl.ds(pl.multiple_of((j * some + i) * s, 16), s)
        for p in range(2):
            cols = pl.ds(128 * p, 128)
            q, k, v = q_i[0, at, cols], k_i[0, at, cols], v_i[0, at, cols]
            q2, da2 = halves(q, first), halves(da[at, cols], first)
            low_probs = p_i[0, p, i]
            d_o[0, to, pl.ds(2 * GROUP + 128 * p, 128)] = dot(low_probs, da2).astype(BF16)
            up = dot_cols(v, da2)
            probs = low_probs.astype(F32)
            inner = jnp.sum(probs * up, axis=0, keepdims=True)
            ds = (probs * (up - inner)).astype(BF16)
            d_o[0, to, pl.ds(GROUP + 128 * p, 128)] = dot(ds, q2).astype(BF16)
            dq = dot_rows(ds, k)
            d_o[0, to, cols] = (jnp.where(first, dq[:s], dq[s:]) * 0.125).astype(BF16)

    @pl.when(j == STEP - 1)
    def _():
        if projects:

            @pl.when(g == 0)
            def _():
                both = jnp.concatenate([a[b] for a in atts for b in range(a.shape[0])], axis=1)
                emit(dot_rows(both, lowered[...]), 0)

        bias_o[0] = jnp.sum(d_o[0].astype(F32), axis=0, keepdims=True)
        emit(dot_rows(norm[...], d_o[0]), g + (1 if projects else 0))


def attend_back_call(place, rows, group, groups, norm, q, k, v, probs, da, r, shape="few", project=()):
    width = norm.shape[1]
    s = rows.pad
    some = rows.images // STEP
    row = pl.BlockSpec((1, s * some, GROUP), lambda g, j: (group + g, j, 0))
    in_specs = [whole(norm.shape), pl.BlockSpec((s * some, GROUP), lambda g, j: (j, group + g)), row, row, row]
    in_specs += [pl.BlockSpec((1, 2, some, s, 2 * s), lambda g, j: (group + g, 0, j, 0, 0))]
    in_specs += [whole(a.shape) for a in project]
    kind = shape
    outs, specs = grad_out(kind, groups + (1 if project else 0), width, r, 1)
    specs = [whole(out.shape) for out in outs]
    return pl.pallas_call(
        functools.partial(attend_back_kernel, place, kind, rows, max(len(project) - 1, 0)),
        grid=(groups, STEP),
        in_specs=in_specs,
        out_specs=[
            pl.BlockSpec((1, rows.all, width), lambda g, j: (g, 0, 0)),
            pl.BlockSpec((1, 1, width), lambda g, j: (g, 0, 0)),
        ]
        + specs,
        out_shape=[
            jax.ShapeDtypeStruct((groups, rows.all, width), BF16),
            jax.ShapeDtypeStruct((groups, 1, width), F32),
        ]
        + outs,
        scratch_shapes=[] if kind == "whole" else [pltpu.VMEM((width, width), BF16)],
        compiler_params=params(),
        cost_estimate=cost(11 * groups),
        name="attend_back",
    )(norm, da, q, k, v, probs, *project)


def last_kernel(rows, counts, quarter, count, base, low, flags, vec, w, *refs):
    n = len(counts)
    dqkv, biases, two, feeds, (out_o, late_o, sums_o) = refs[:n], refs[n : 2 * n], refs[2 * n], refs[2 * n + 1 : -3], refs[-3:]
    cols = flag_column(rows, flags)
    gain = vec[1:2, :]
    parts = [d[b] for d, count in zip(dqkv, counts) for b in range(count)]
    up = dot_cols(parts[0], w[0])
    for g in range(1, len(parts)):
        up = up + dot_cols(parts[g], w[g])
    xhat, scale = norm_stats(base[...].astype(F32))
    total = low[...].astype(F32) + norm_back(up, xhat, scale, gain)
    row = lax.broadcasted_iota(jnp.int32, (rows.pad, 1), 0)
    j = pl.program_id(0)
    for i in range(rows.images):

        @pl.when(j == i)
        def _():
            chosen = jnp.logical_and(cols[: rows.pad, i : i + 1] > 0.5, row < rows.patches)
            sums = jnp.concatenate(
                [
                    jnp.sum(jnp.where(chosen, total, 0.0), axis=0, keepdims=True),
                    jnp.sum(up * xhat, axis=0, keepdims=True),
                    jnp.sum(up, axis=0, keepdims=True),
                ],
                axis=0,
            )
            sums_o[...] = sums if i == 0 else sums_o[...] + sums
            out_o[rows.patches * i : rows.patches * (i + 1), :] = jnp.where(chosen, 0.0, total)[: rows.patches]

    @pl.when(j == rows.images - 1)
    def _():
        groups = [b[g] for b, group_count in zip(biases, counts) for g in range(group_count)]
        query = jnp.concatenate([g[:, :GROUP] for g in groups], axis=1)
        value = jnp.concatenate([g[:, 2 * GROUP :] for g in groups], axis=1)
        hidden = [f[b] for f in feeds for b in range(f.shape[0])]
        width = base.shape[1]
        every = jnp.concatenate(
            [sums_o[...], query, value, two[...], *hidden, jnp.zeros((9 - quarter - 2, width), F32)], axis=0
        )
        r = width // count
        for k in range(late_o.shape[0]):
            at = k % count
            late_o[k] = every[:, at * r : (at + 1) * r]


def last_call(rows, count, copies, base, low, flags, vec, w, dqkv, biases, two, feeds):
    width = base.shape[1]
    block = rows.block(width)
    outs = [
        jax.ShapeDtypeStruct((rows.raw, width), F32),
        jax.ShapeDtypeStruct((copies * count, 16, width // count), F32),
    ]
    quarter = sum(f.shape[0] for f in feeds)
    small = [*biases, two, *feeds]
    return pl.pallas_call(
        functools.partial(last_kernel, rows, [d.shape[0] for d in dqkv], quarter, count),
        grid=(rows.images,),
        in_specs=[block, block, whole(flags.shape), whole(vec.shape), whole(w.shape)]
        + [pl.BlockSpec((d.shape[0], rows.pad, width), lambda j: (0, j, 0)) for d in dqkv]
        + [whole(v.shape) for v in small],
        out_specs=[whole(out.shape) for out in outs],
        out_shape=outs,
        scratch_shapes=[pltpu.VMEM((3, width), F32)],
        compiler_params=params(),
        cost_estimate=cost(1500),
        name="last",
    )(base, low, flags, vec, w, *dqkv, *small)


def local(
    count,
    tokens,
    mask_flags,
    mask_token,
    norm1_gain,
    norm1_bias,
    qkv_weight,
    query_bias,
    value_bias,
    proj_weight,
    proj_bias,
    norm2_gain,
    norm2_bias,
    fc1_weight,
    fc1_bias,
    fc2_weight,
    fc2_bias,
    out_grad,
):
    images, patches = mask_flags.shape
    rows = Rows(images, patches)
    r, width = proj_weight.shape
    place = Place(count) if r % 16 == 0 and count == 4 * FAR else None
    quarter = fc1_weight.shape[1] // width

    half = quarter // 2
    vectors = (mask_token, norm1_gain, norm1_bias, query_bias, value_bias, proj_bias, norm2_gain, norm2_bias, fc2_bias)
    kinds = len(vectors) + quarter

    def whole_gather(stack):
        return Weight("whole", [lax.all_gather(stack, "fsdp", axis=1, tiled=True)])

    def whole_scatter(sums):
        share = lax.psum_scatter(sums if place else sums.astype(F32), "fsdp", scatter_dimension=1, tiled=True)
        return share if place else lax.psum(share, "rep")

    flow = Flow()
    pad_in = (tokens, out_grad)
    if place:
        z, x, c = place.own()
        first, second, ff_0, ff_1 = pack_call(count, vectors, fc1_bias, qkv_weight, proj_weight, fc1_weight, fc2_weight)
        flow.begin("wa", gather_fast(place, first))
        pad_in = flow.send(*pad_in)
    else:
        qkv_blocks = qkv_weight.reshape(r, 3, 3, GROUP).transpose(2, 0, 1, 3).reshape(3, r, 3 * GROUP)
        up_blocks = fc1_weight.reshape(r, count, quarter, r).transpose(2, 0, 1, 3).reshape(quarter, r, width)
        down_blocks = fc2_weight.reshape(quarter, r, width)
        ff = jnp.stack([up_blocks, down_blocks], axis=1).reshape(2 * quarter, r, width)
        w_a, w_b = whole_gather(qkv_blocks[:1]), whole_gather(jnp.concatenate([qkv_blocks[1:], proj_weight[None]]))
        w_f0, w_f1 = whole_gather(ff[: 2 * half]), whole_gather(ff[2 * half :])
        small = jnp.concatenate([v[None] for v in vectors] + [fc1_bias.reshape(quarter, r)])
        came = lax.all_gather(small, "fsdp", axis=1, tiled=True)
        came = jnp.pad(came, ((0, 16 - kinds), (0, 0)))
    base, grad = pad_call(rows, *pad_in)
    if place:
        (base,) = flow.meet(["wa"], base)
        flow.begin("wb", gather_wide(place, second))
        flow.begin("wf0", gather_even(place, ff_0))
        (base,) = flow.send(base)
        (base,) = flow.turn(["wa"], base)
        (base,) = flow.meet(["wa"], base)
        w_a = flow.done["wa"]
        came = jnp.stack([part[:, 0, r:, :r] for part in w_a.arrays]).reshape(2, 2, FAR, -1, r)
        came = jnp.where(c == 0, came, came[::-1])
        came = jnp.where(x == 0, came, came[:, ::-1])
        came = jnp.where(z % 2 == 0, came, came.reshape(2, 2, 2, 2, -1, r)[:, :, :, ::-1].reshape(came.shape))
        came = jnp.where(z < 2, came, came.reshape(2, 2, 2, 2, -1, r)[:, :, ::-1].reshape(came.shape))
        came = came.transpose(3, 2, 1, 0, 4)
    vec = came.reshape(16, width).astype(F32)

    base, norm = norm_one_call(rows, base, mask_flags, vec)
    if place:
        norm, ff_1 = flow.meet(["wb"], norm, ff_1)
        w_f1 = whole_gather(ff_1)
        (norm,) = flow.send(norm)
    attends = attend_call(place, rows, 0, 1, norm, vec, w_a)
    if place:
        norm, *attends = flow.turn(["wb", "wf0"], norm, *attends)
        norm, *attends = flow.meet(["wb"], norm, *attends)
        w_b = flow.done["wb"]
    q, k, v, att, probs, wqkv = attend_call(place, rows, 1, 2, norm, vec, w_b, attends)
    if place:
        (att,) = flow.turn(["wf0"], att)
    resid, norm_two, w_proj = project_call(place, rows, vec, base, att, w_b, 2)
    if place:
        (norm_two,) = flow.turn(["wf0"], norm_two)
        (norm_two,) = flow.meet(["wf0"], norm_two)
        w_f0 = flow.done["wf0"]

    form = "wide" if place else "whole"
    acc, gn, gb_0, f0 = feed_call(place, rows, 0, half, 0, norm_two, grad, vec, w_f0, "whole", r, ())
    f0 = whole_scatter(f0)
    acc, gn, gb_1, *f1 = feed_call(place, rows, half, half, 0, norm_two, grad, vec, w_f1, form, r, (acc, gn))
    if place:
        flow.begin("f1", scatter_wide(place, *f1))
        acc, gn = flow.send(acc, gn)

    block_out, lowered, da, sums_two = middle_call(rows, resid, acc, gn, grad, vec, w_proj)
    if place:
        (da,) = flow.turn(["f1"], da)
    dqkv, qs, *sums_c = attend_back_call(
        place, rows, 0, 3, norm, q, k, v, probs, da, r, form, project=[lowered, att]
    )
    if place:
        flow.begin("c", scatter_wide(place, *sums_c))
        dqkv, f0 = flow.meet(["f1"], dqkv, f0)
        flow.begin("f0", send_twin(place, f0))
        (dqkv,) = flow.send(dqkv)
    input_grad, late = last_call(
        rows,
        count,
        2 if place else 1,
        base,
        lowered,
        mask_flags,
        vec,
        wqkv,
        [dqkv],
        [qs],
        sums_two,
        [gb_0, gb_1],
    )
    if place:
        late, input_grad = flow.turn(["c", "f1", "f0"], late, input_grad)
        late = lax.all_to_all(late, ("rep", "fsdp"), 0, 0, tiled=True)
        (late,) = flow.meet(["c"], late)
        flow.begin("fy", send_twin(place, flow.done["f1"]))
        (late,) = flow.send(late)
        (late,) = flow.meet(["c", "fy"], late)
        flow.begin("cy", send_twin(place, flow.done["c"]))
        (late,) = flow.send(late)
        (late,) = flow.meet(["cy"], late)
        shares = late.sum(axis=0)
        sums = [side for name in ("f0", "fy", "cy") for pair in zip(*flow.done[name]) for side in pair]
        g_qkv, g_proj, g_up, g_down = unpack_call(count, quarter, sums)
    else:
        shares = lax.psum(lax.psum_scatter(late, "fsdp", scatter_dimension=0, tiled=True), "rep")[0]
        sums_c = whole_scatter(sums_c[0])
        g_proj = sums_c[0]
        g_qkv = sums_c[1:].reshape(3, r, 3, GROUP).transpose(1, 2, 0, 3).reshape(r, 3 * width)
        g_ff = jnp.concatenate([f0, whole_scatter(f1[0])]).reshape(quarter, 2, r, width)
        g_up = g_ff[:, 0].reshape(quarter, r, count, r).transpose(1, 2, 0, 3).reshape(r, quarter * width)
        g_down = g_ff[:, 1].reshape(quarter * r, width)
    token_s, gain1_s, shift1_s, qb_s, vb_s, pb_s, gain2_s, shift2_s, db_s = [shares[i] for i in range(9)]
    ub_s = shares[9:kinds].reshape(-1)
    return (
        block_out,
        input_grad,
        token_s,
        gain1_s,
        shift1_s,
        g_qkv,
        qb_s,
        vb_s,
        g_proj,
        pb_s,
        gain2_s,
        shift2_s,
        g_up,
        ub_s,
        g_down,
        db_s,
    )


def solution(mesh):
    both, one = P(("rep", "fsdp"), None), P("fsdp")
    flat = P("fsdp", None)
    in_specs = (both, both, one, one, one, flat, one, one, flat, one, one, one, flat, one, flat, one, both)
    out_specs = (both, both, one, one, one, flat, one, one, flat, one, one, one, flat, one, flat, one)
    return jax.shard_map(
        functools.partial(local, mesh.shape["fsdp"]),
        mesh=mesh,
        in_specs=in_specs,
        out_specs=out_specs,
        check_vma=False,
    )
```

profile of v0, /device:TPU:0, one launch (start us, length us, event | category | flops | bytes accessed | tf_op | source)
XLA Modules:
  0.0 313.8 jit_solution(15527358109169742630)
XLA Ops:
  7.2 1.2 broadcast_in_dim.39.refs_9_
  8.4 2.5 pack.1
  10.9 3.1 collective-permute-start
  14.0 2.6 collective-permute-start.1
  16.6 5.2 %pad_rows.1 = (bf16[1248,768]{1,0:T(8,128)(2,1)}, bf16[1248,768]{1,0:T(8,128)(2,1)}) custom-call(bf16[1176,768]{1,0:T(8,128)(2,1)} %tokens, bf16[1176,768]{1,0:T(8,128)(2,1)} %grads), custom_call_target="tpu_custom_call" | custom-call | flops 57500000 | bytes 150000 | tf_op jit(solution)/shard_map/pad_rows/pallas_call | solution.py:327
  21.9 2.8 collective-permute-done.1
  25.5 1.5 collective-permute-start.3
  26.9 1.6 collective-permute-start.6
  28.6 1.4 collective-permute-start.7
  30.0 1.4 collective-permute-start.8
  31.3 3.1 collective-permute-done.3
  34.5 1.7 collective-permute-done.5.refs_3_
  37.9 5.1 %norm_one.1 = (bf16[1248,768]{1,0:T(8,128)(2,1)}, bf16[1248,768]{1,0:T(8,128)(2,1)}) custom-call(bf16[1248,768]{1,0:T(8,128)(2,1)} %get-tuple-element.212.tokens, s32[6,196]{1,0:T(8,128)} %flags.3, f32[16,768]{1,0:T(8,128)} %reshape.93.vec), custom_call_target="tpu_custom_call" | custom-call | flops 57500000 | bytes 150000 | tf_op jit(solution)/shard_map/norm_one/pallas_call | solution.py:341
  43.5 1.6 collective-permute-start.10
  45.1 1.4 collective-permute-start.11
  47.1 2.4 collective-permute-start.12
  49.4 1.0 collective-permute-start.13
  50.4 4.2 %collective-permute-done.12 = bf16[4,48,384]{2,1,0:T(8,128)(2,1)S(1)} collective-permute-done((bf16[4,48,384]{2,1,0:T(8,128)(2,1)S(1)}, bf16[4,48,384]{2,1,0:T(8,128)(2,1)S(1)}, u32[]{:S(2)}, u32[]{:S(2)}) %collective-permute-start.12) | collective-permute-done | bytes 147488 | tf_op jit(solution)/shard_map/ppermute | solution.py:52
  54.6 1.5 collective-permute-start.14
  56.2 8.6 %attend.2 = (bf16[3,1248,256]{2,1,0:T(8,128)(2,1)}, bf16[3,1248,256]{2,1,0:T(8,128)(2,1)}, bf16[3,1248,256]{2,1,0:T(8,128)(2,1)}, bf16[3,1248,256]{2,1,0:T(8,128...) custom-call(bf16[1248,768]{1,0:T(8,128)(2,1)} %get-tuple-element.259.norm, ...), custom_call_target="tpu_custom_call" | custom-call | flops 92000000 | bytes 240000 | tf_op jit(solution)/shard_map/attend/pallas_call | solution.py:493
  64.7 2.1 collective-permute-done.13
  66.8 2.8 collective-permute-done.9
  70.1 1.6 collective-permute-start.15
  71.7 1.5 collective-permute-start.16
  73.8 1.2 copy-done.2
  75.0 13.4 %attend.3 = (bf16[3,1248,256]{2,1,0:T(8,128)(2,1)}, bf16[3,1248,256]{2,1,0:T(8,128)(2,1)}, bf16[3,1248,256]{2,1,0:T(8,128)(2,1)}, bf16[3,1248,256]{2,1,0:T(8,128...) custom-call(bf16[1248,768]{1,0:T(8,128)(2,1)} %get-tuple-element.259, ...), custom_call_target="tpu_custom_call", output_to_operand_aliasing={{0}: (4, {}), {1}: (5, {}), {2}: (6, {}), {3}: (7, {}), {4}... | custom-call | flops 161000000 | bytes 420000 | tf_op jit(solution)/shard_map/attend/pallas_call | solution.py:493
  88.5 2.4 collective-permute-done.15
  90.9 1.4 collective-permute-start.18
  92.4 2.4 collective-permute-start.19
  94.8 6.8 %project.1 = (f32[1248,768]{1,0:T(8,128)}, bf16[1248,768]{1,0:T(8,128)(2,1)}, bf16[1,768,768]{2,1,0:T(8,128)(2,1)}) custom-call(f32[16,768]{1,0:T(8,128)} %reshape.93.vec, bf16[1248,768]{1,0:T(8,128)(2,1)} %get-tuple-element.213.base, bf16[3,1248,256]{2,1,0:T(8,128)(2,1)} %get-tuple-element.271.att.refs_5_, bf16[4,4,3,48,384]{4,3,2,1,0:T(8,128)(2,1)} %copy-done, ...), custom_call_target="tpu_custom_call" | custom-call | flops 80500000 | bytes 210000 | tf_op jit(solution)/shard_map/project/pallas_call | solution.py:537
  101.6 3.2 %collective-permute-done.19 = bf16[2,4,48,384]{3,2,1,0:T(8,128)(2,1)S(1)} collective-permute-done((bf16[2,4,48,384]{3,2,1,0:T(8,128)(2,1)S(1)}, bf16[2,4,48,384]{3,2,1,0:T(8,128)(2,1)S(1)}, u32[]{:S(2)}, u32[]{:S(2)}) %collective-permute-start.19) | collective-permute-done | bytes 294944 | tf_op jit(solution)/shard_map/ppermute | solution.py:49
  105.4 4.5 %collective-permute-done.20.refs_1_ = bf16[4,4,4,48,384]{4,3,2,1,0:T(8,128)(2,1)S(1)} collective-permute-done((bf16[4,4,4,48,384]{4,3,2,1,0:T(8,128)(2,1)S(1)}, bf16[4,4,4,48,384]{4,3,2,1,0:T(8,128)(2,1)S(1)}, u32[]{:S(2)}, u32[]{:S(2)}) %collective-permute-start.20) | collective-permute-done | bytes 2359328 | tf_op jit(solution)/shard_map/ppermute | solution.py:46
  109.9 1.4 copy-done.7
  111.3 28.5 %feed.2 = (f32[1248,768]{1,0:T(8,128)}, f32[1248,768]{1,0:T(8,128)}, f32[2,1,768]{2,1,0:T(1,128)}, bf16[4,768,768]{2,1,0:T(8,128)(2,1)}) custom-call(bf16[1248,768]{1,0:T(8,128)(2,1)} %get-tuple-element.281.norm, bf16[1248,768]{1,0:T(8,128)(2,1)} %get-tuple-element.282.grad, f32[16,768]{1,0:T(8,128)} %reshape.93.vec, bf16[4,4,4,48,384]{4,3,2,1,0:T(8,128)(2,1)} %copy-done.1, ...), custom_call_target="tpu_custom_call" | custom-call | flops 345000000 | bytes 900000 | tf_op jit(solution)/shard_map/feed/pallas_call | solution.py:625
  139.9 33.4 %feed.3 = (f32[1248,768]{1,0:T(8,128)}, f32[1248,768]{1,0:T(8,128)}, f32[2,1,768]{2,1,0:T(1,128)}, bf16[2,2,4,4,48,384]{5,4,3,2,1,0:T(8,128)(2,1)}, bf16[2,2,4,4,48,384]{5,4,3,2,1,0:T(8,128)(2,1)}) custom-call(bf16[1248,768]{1,0:T(8,128)(2,1)} %get-tuple-element.281.norm, bf16[1248,768]{1,0:T(8,128)(2,1)} %get-tuple-element.282.grad, ...), custom_call_target="tpu_custom_call" | custom-call | flops 345000000 | bytes 900000 | tf_op jit(solution)/shard_map/feed/pallas_call | solution.py:625
  173.3 12.3 %middle.1 = (bf16[1176,768]{1,0:T(8,128)(2,1)}, bf16[1248,768]{1,0:T(8,128)(2,1)}, bf16[1248,768]{1,0:T(8,128)(2,1)}, f32[4,768]{1,0:T(4,128)}) custom-call(f32[1248,768]{1,0:T(8,128)} %get-tuple-element.272.resid, f32[1248,768]{1,0:T(8,128)} %get-tuple-element.290.acc, f32[1248,768]{1,0:T(8,128)} %get-tuple-element.291.gn, ...), custom_call_target="tpu_custom_call" | custom-call | flops 138000000 | bytes 360000 | tf_op jit(solution)/shard_map/middle/pallas_call | solution.py:683
  187.0 1.6 collective-permute-start.22
  188.6 1.5 collective-permute-start.23
  190.5 28.8 %attend_back.1 = (bf16[3,1248,768]{2,1,0:T(8,128)(2,1)}, f32[3,1,768]{2,1,0:T(1,128)}, bf16[2,2,4,4,48,384]{5,4,3,2,1,0:T(8,128)(2,1)}, bf16[2,2,4,4,48,384]{5,4,3,2,1,0:T(8,128)(2,1)}) custom-call(bf16[1248,768]{1,0:T(8,128)(2,1)} %get-tuple-element.259.norm, bf16[1248,768]{1,0:T(8,128)(2,1)} %get-tuple-element.299.da, ...), custom_call_target="tpu_custom_call" | custom-call | flops 379500000 | bytes 990000 | tf_op jit(solution)/shard_map/attend_back/pallas_call | solution.py:761
  219.6 2.6 reduce-scatter.2.cloned.1.call-done.refs_0_
  222.1 1.8 fusion.5
  224.1 1.5 collective-permute-start.29
  225.6 2.3 collective-permute-start.26
  227.9 1.1 collective-permute-start.27
  229.0 1.5 collective-permute-start.28
  230.5 15.6 %last.1 = (f32[1176,768]{1,0:T(8,128)}, f32[32,16,48]{2,1,0:T(8,128)}) custom-call(bf16[1248,768]{1,0:T(8,128)(2,1)} %get-tuple-element.213.base, bf16[1248,768]{1,0:T(8,128)(2,1)} %get-tuple-element.304.refs_4_.low, s32[6,196]{1,0:T(8,128)} %flags.3, f32[16,768]{1,0:T(8,128)} %reshape.93.vec, bf16[3,768,768]{2,1,0:T(8,128)(2,1)} %get-tuple-element.322.w, ...), custom_call_target="tpu_custom_call" | custom-call | flops 17250000896 | bytes 45000000 | tf_op jit(solution)/shard_map/last/pallas_call | solution.py:836
  246.2 1.9 fusion.11
  248.3 1.3 collective-permute-start.30
  249.6 1.1 collective-permute-start.31
  250.7 1.1 collective-permute-start.32
  251.8 1.8 reshape.96
  253.6 4.2 %all-to-all-start = ((f32[32,1,768]{2,1,0:T(1,128)}), f32[32,1,768]{2,1,0:T(1,128)}, u32[]{:S(2)}, u32[]{:S(2)}) async-start(f32[32,1,768]{2,1,0:T(1,128)} %reshape.96), calls=%async_computation.1 | async-start | bytes 196608 | tf_op jit(solution)/shard_map/all_to_all | solution.py:976
  257.8 1.8 fusion.14.refs_2_
  259.6 18.6 %all-to-all-done = f32[32,1,768]{2,1,0:T(1,128)} async-done(((f32[32,1,768]{2,1,0:T(1,128)}), f32[32,1,768]{2,1,0:T(1,128)}, u32[]{:S(2)}, u32[]{:S(2)}) %all-to-all-start) | async-done | bytes 98336 | tf_op jit(solution)/shard_map/all_to_all | solution.py:976
  278.7 1.8 reduce
  280.7 1.8 fusion.2
  283.4 2.1 collective-permute-start.34
  285.5 1.5 collective-permute-start.35
  287.0 1.1 collective-permute-start.36
  288.1 2.8 collective-permute-done.33
  290.9 6.5 %collective-permute-done.34 = bf16[4,48,384]{2,1,0:T(8,128)(2,1)S(1)} collective-permute-done((bf16[4,48,384]{2,1,0:T(8,128)(2,1)S(1)}, bf16[4,48,384]{2,1,0:T(8,128)(2,1)S(1)}, u32[]{:S(2)}, u32[]{:S(2)}) %collective-permute-start.34) | collective-permute-done | bytes 147488 | tf_op jit(solution)/shard_map/ppermute | solution.py:52
  297.5 0.9 collective-permute-start.37
  298.4 4.3 %collective-permute-done.37.refs_5_ = bf16[4,48,384]{2,1,0:T(8,128)(2,1)S(1)} collective-permute-done((bf16[4,48,384]{2,1,0:T(8,128)(2,1)S(1)}, bf16[4,48,384]{2,1,0:T(8,128)(2,1)S(1)}, u32[]{:S(2)}, u32[]{:S(2)}) %collective-permute-start.37) | collective-permute-done | bytes 147488 | tf_op jit(solution)/shard_map/ppermute | solution.py:55
  304.0 2.8 unpack.1
  (120 shorter events, 10.7 us)
Async XLA Ops:
  7.2 132.7 %all-gather.2.cloned.1.call-start = ((), (), s32[]{:S(2)}) async-start(), calls=%async_computation.2 | async-start | bytes 5013504 | tf_op jit(solution)/shard_map/all_gather | solution.py:882
  10.9 10.9 %copy-start.13 = (bf16[4,48,768]{2,1,0:T(8,128)(2,1)S(1)}, bf16[4,48,768]{2,1,0:T(8,128)(2,1)}, u32[]{:S(2)}) copy-start(bf16[4,48,768]{2,1,0:T(8,128)(2,1)} %get-tuple-element.201) | copy-start | bytes 884740
  10.9 10.9 %collective-permute-start = (bf16[1,64,768]{2,1,0:T(8,128)(2,1)}, bf16[1,64,768]{2,1,0:T(8,128)(2,1)S(1)}, u32[]{:S(2)}, u32[]{:S(2)}) collective-permute-start(bf16[1,64,768]{2,1,0:T(8,128)(2,1)} %get-tuple-element.193), channel_id=1, source_target_pairs={{0,4},{1,5},{2,6},{3,7},{4,0},{5,1},{6,2},{7,3},{8,12},{9,13},{10,... | collective-permute-start | bytes 294920 | tf_op jit(solution)/shard_map/ppermute | solution.py:52
  14.0 10.6 %collective-permute-start.1 = (bf16[1,64,768]{2,1,0:T(8,128)(2,1)}, bf16[1,64,768]{2,1,0:T(8,128)(2,1)S(1)}, u32[]{:S(2)}, u32[]{:S(2)}) collective-permute-start(bf16[1,64,768]{2,1,0:T(8,128)(2,1)} %get-tuple-element.193), channel_id=1, source_target_pairs={{0,8},{1,9},{2,10},{3,11},{4,12},{5,13},{6,14},{7,15},{8,0},{9,1},... | collective-permute-start | bytes 294920 | tf_op jit(solution)/shard_map/ppermute | solution.py:52
  16.6 8.1 %collective-permute-start.2 = (bf16[1,64,768]{2,1,0:T(8,128)(2,1)}, bf16[1,64,768]{2,1,0:T(8,128)(2,1)S(1)}, u32[]{:S(2)}, u32[]{:S(2)}) collective-permute-start(bf16[1,64,768]{2,1,0:T(8,128)(2,1)} %get-tuple-element.193), channel_id=1, source_target_pairs={{0,12},{1,13},{2,14},{3,15},{4,8},{5,9},{6,10},{7,11},{8,4},{9,5},... | collective-permute-start | bytes 294920 | tf_op jit(solution)/shard_map/ppermute | solution.py:52
  16.6 5.3 %copy-start.16 = (bf16[3,48,768]{2,1,0:T(8,128)(2,1)S(1)}, bf16[3,48,768]{2,1,0:T(8,128)(2,1)}, u32[]{:S(2)}) copy-start(bf16[3,48,768]{2,1,0:T(8,128)(2,1)} %get-tuple-element.200) | copy-start | bytes 663556
  16.6 8.1 %copy-start.22 = (bf16[1,64,768]{2,1,0:T(8,128)(2,1)S(1)}, bf16[1,64,768]{2,1,0:T(8,128)(2,1)}, u32[]{:S(2)}) copy-start(bf16[1,64,768]{2,1,0:T(8,128)(2,1)} %get-tuple-element.193) | copy-start | bytes 294916
  25.5 9.0 %collective-permute-start.3 = (bf16[4,1,64,768]{3,2,0,1:T(8,128)(2,1)S(1)}, bf16[4,1,64,768]{3,2,0,1:T(8,128)(2,1)S(1)}, u32[]{:S(2)}, u32[]{:S(2)}) collective-permute-start(bf16[4,1,64,768]{3,2,0,1:T(8,128)(2,1)S(1)} %get-tuple-element.204), channel_id=1, source_target_pairs={{0,2},{1,3},{2,0},{3,1},{4,6},{5,7},{6,4},{7,5},{8,10},{9,11},{10,... | collective-permute-start | bytes 1179656 | tf_op jit(solution)/shard_map/ppermute | solution.py:49
  26.9 7.5 %collective-permute-start.4 = (bf16[4,1,64,768]{3,2,0,1:T(8,128)(2,1)S(1)}, bf16[4,1,64,768]{3,2,0,1:T(8,128)(2,1)S(1)}, u32[]{:S(2)}, u32[]{:S(2)}) collective-permute-start(bf16[4,1,64,768]{3,2,0,1:T(8,128)(2,1)S(1)} %get-tuple-element.204), channel_id=1, source_target_pairs={{0,1},{1,0},{2,3},{3,2},{4,5},{5,4},{6,7},{7,6},{8,9},{9,8},{10,11... | collective-permute-start | bytes 1179656 | tf_op jit(solution)/shard_map/ppermute | solution.py:46
  26.9 16.1 %collective-permute-start.6 = (bf16[3,48,384]{2,1,0:T(8,128)(2,1)S(1)}, bf16[3,48,384]{2,1,0:T(8,128)(2,1)S(1)}, u32[]{:S(2)}, u32[]{:S(2)}) collective-permute-start(bf16[3,48,384]{2,1,0:T(8,128)(2,1)S(1)} %constant_dynamic-slice_fusion.1), channel_id=1, source_target_pairs={{0,4},{1,5},{2,6},{3,7},{4,0},{5,1},{6,2},{7,3},{8,12},{9,13},{10,... | collective-permute-start | bytes 331784 | tf_op jit(solution)/shard_map/ppermute | solution.py:52
  28.6 14.5 %collective-permute-start.7 = (bf16[3,48,384]{2,1,0:T(8,128)(2,1)S(1)}, bf16[3,48,384]{2,1,0:T(8,128)(2,1)S(1)}, u32[]{:S(2)}, u32[]{:S(2)}) collective-permute-start(bf16[3,48,384]{2,1,0:T(8,128)(2,1)S(1)} %constant_dynamic-slice_fusion.1), channel_id=1, source_target_pairs={{0,8},{1,9},{2,10},{3,11},{4,12},{5,13},{6,14},{7,15},{8,0},{9,1},... | collective-permute-start | bytes 331784 | tf_op jit(solution)/shard_map/ppermute | solution.py:52
  30.0 13.1 %collective-permute-start.8 = (bf16[3,48,384]{2,1,0:T(8,128)(2,1)S(1)}, bf16[3,48,384]{2,1,0:T(8,128)(2,1)S(1)}, u32[]{:S(2)}, u32[]{:S(2)}) collective-permute-start(bf16[3,48,384]{2,1,0:T(8,128)(2,1)S(1)} %constant_dynamic-slice_fusion.1), channel_id=1, source_target_pairs={{0,12},{1,13},{2,14},{3,15},{4,8},{5,9},{6,10},{7,11},{8,4},{9,5},... | collective-permute-start | bytes 331784 | tf_op jit(solution)/shard_map/ppermute | solution.py:52
  34.4 8.7 %copy-start.10 = (bf16[4,1,64,768]{3,2,0,1:T(8,128)(2,1)}, bf16[4,1,64,768]{3,2,0,1:T(8,128)(2,1)S(1)}, u32[]{:S(2)}) copy-start(bf16[4,1,64,768]{3,2,0,1:T(8,128)(2,1)S(1)} %collective-permute-done.3) | copy-start | bytes 1179652
  34.4 8.7 %copy-start.11 = (bf16[4,1,64,768]{3,2,0,1:T(8,128)(2,1)}, bf16[4,1,64,768]{3,2,0,1:T(8,128)(2,1)S(1)}, u32[]{:S(2)}) copy-start(bf16[4,1,64,768]{3,2,0,1:T(8,128)(2,1)S(1)} %collective-permute-done.4) | copy-start | bytes 1179652
  34.4 1.8 collective-permute-start.5
  36.2 6.9 %copy-start.12 = (bf16[4,1,64,768]{3,2,1,0:T(8,128)(2,1)}, bf16[4,1,64,768]{3,2,1,0:T(8,128)(2,1)S(1)}, u32[]{:S(2)}) copy-start(bf16[4,1,64,768]{3,2,1,0:T(8,128)(2,1)S(1)} %collective-permute-done.5.refs_3_) | copy-start | bytes 1179652
  43.1 179.0 %reduce-scatter.2.cloned.1.call-start = ((), (), s32[]{:S(2)}) async-start(), calls=%async_computation.3 | async-start | bytes 5013504 | tf_op jit(solution)/shard_map/reduce_scatter | solution.py:885
  43.5 23.3 %collective-permute-start.10 = (bf16[4,3,48,384]{3,2,1,0:T(8,128)(2,1)S(1)}, bf16[4,3,48,384]{3,2,1,0:T(8,128)(2,1)S(1)}, u32[]{:S(2)}, u32[]{:S(2)}) collective-permute-start(bf16[4,3,48,384]{3,2,1,0:T(8,128)(2,1)S(1)} %get-tuple-element.225), channel_id=1, source_target_pairs={{0,16},{16,0},{1,17},{17,1},{2,18},{18,2},{3,19},{19,3},{4,20},{20... | collective-permute-start | bytes 1327112 | tf_op jit(solution)/shard_map/ppermute | solution.py:55
  45.1 21.7 %collective-permute-start.11 = (bf16[4,3,48,384]{3,2,1,0:T(8,128)(2,1)S(1)}, bf16[4,3,48,384]{3,2,1,0:T(8,128)(2,1)S(1)}, u32[]{:S(2)}, u32[]{:S(2)}) collective-permute-start(bf16[4,3,48,384]{3,2,1,0:T(8,128)(2,1)S(1)} %get-tuple-element.225), channel_id=1, source_target_pairs={{0,18},{1,19},{2,16},{3,17},{4,22},{5,23},{6,20},{7,21},{8,26},{9,... | collective-permute-start | bytes 1327112 | tf_op jit(solution)/shard_map/ppermute | solution.py:59
  46.5 23.1 %collective-permute-start.9 = (bf16[4,3,48,384]{3,2,1,0:T(8,128)(2,1)S(1)}, bf16[4,3,48,384]{3,2,1,0:T(8,128)(2,1)S(1)}, u32[]{:S(2)}, u32[]{:S(2)}) collective-permute-start(bf16[4,3,48,384]{3,2,1,0:T(8,128)(2,1)S(1)} %get-tuple-element.225), channel_id=1, source_target_pairs={{0,2},{1,3},{2,0},{3,1},{4,6},{5,7},{6,4},{7,5},{8,10},{9,11},{10,... | collective-permute-start | bytes 1327112 | tf_op jit(solution)/shard_map/ppermute | solution.py:49
  47.1 7.6 %collective-permute-start.12 = (bf16[4,48,384]{2,1,0:T(8,128)(2,1)S(1)}, bf16[4,48,384]{2,1,0:T(8,128)(2,1)S(1)}, u32[]{:S(2)}, u32[]{:S(2)}) collective-permute-start(bf16[4,48,384]{2,1,0:T(8,128)(2,1)S(1)} %constant_dynamic-slice_fusion), channel_id=1, source_target_pairs={{0,4},{1,5},{2,6},{3,7},{4,0},{5,1},{6,2},{7,3},{8,12},{9,13},{10,... | collective-permute-start | bytes 442376 | tf_op jit(solution)/shard_map/ppermute | solution.py:52
  49.4 17.4 %collective-permute-start.13 = (bf16[4,48,384]{2,1,0:T(8,128)(2,1)S(1)}, bf16[4,48,384]{2,1,0:T(8,128)(2,1)S(1)}, u32[]{:S(2)}, u32[]{:S(2)}) collective-permute-start(bf16[4,48,384]{2,1,0:T(8,128)(2,1)S(1)} %constant_dynamic-slice_fusion), channel_id=1, source_target_pairs={{0,8},{1,9},{2,10},{3,11},{4,12},{5,13},{6,14},{7,15},{8,0},{9,1},... | collective-permute-start | bytes 442376 | tf_op jit(solution)/shard_map/ppermute | solution.py:52
  54.6 12.2 %collective-permute-start.14 = (bf16[4,48,384]{2,1,0:T(8,128)(2,1)S(1)}, bf16[4,48,384]{2,1,0:T(8,128)(2,1)S(1)}, u32[]{:S(2)}, u32[]{:S(2)}) collective-permute-start(bf16[4,48,384]{2,1,0:T(8,128)(2,1)S(1)} %constant_dynamic-slice_fusion), channel_id=1, source_target_pairs={{0,12},{1,13},{2,14},{3,15},{4,8},{5,9},{6,10},{7,11},{8,4},{9,5},... | collective-permute-start | bytes 442376 | tf_op jit(solution)/shard_map/ppermute | solution.py:52
  70.1 3.8 %copy-start = (bf16[4,4,3,48,384]{4,3,2,1,0:T(8,128)(2,1)}, bf16[4,4,3,48,384]{4,3,2,1,0:T(8,128)(2,1)S(1)}, u32[]{:S(2)}) copy-start(bf16[4,4,3,48,384]{4,3,2,1,0:T(8,128)(2,1)S(1)} %pad_maximum_fusion.1.refs_0_) | copy-start | bytes 5308420
  70.1 3.8 %collective-permute-start.17 = (bf16[4,4,3,48,384]{4,3,2,1,0:T(8,128)(2,1)S(1)}, bf16[4,4,3,48,384]{4,3,2,1,0:T(8,128)(2,1)S(1)}, u32[]{:S(2)}, u32[]{:S(2)}) collective-permute-start(bf16[4,4,3,48,384]{4,3,2,1,0:T(8,128)(2,1)S(1)} %pad_maximum_fusion.1.refs_0_), channel_id=1, source_target_pairs={{0,1},{1,0},{2,3},{3,2},{4,5},{5,4},{6,7},{7,6},{8,9},{9,8},{10,11... | collective-permute-start | bytes 5308424 | tf_op jit(solution)/shard_map/ppermute | solution.py:46
  70.1 20.7 %collective-permute-start.15 = (bf16[4,4,48,384]{3,2,1,0:T(8,128)(2,1)S(1)}, bf16[4,4,48,384]{3,2,1,0:T(8,128)(2,1)S(1)}, u32[]{:S(2)}, u32[]{:S(2)}) collective-permute-start(bf16[4,4,48,384]{3,2,1,0:T(8,128)(2,1)S(1)} %get-tuple-element.250), channel_id=1, source_target_pairs={{0,2},{1,3},{2,0},{3,1},{4,6},{5,7},{6,4},{7,5},{8,10},{9,11},{10,... | collective-permute-start | bytes 1769480 | tf_op jit(solution)/shard_map/ppermute | solution.py:49
  71.7 19.2 %collective-permute-start.16 = (bf16[4,4,48,384]{3,2,1,0:T(8,128)(2,1)S(1)}, bf16[4,4,48,384]{3,2,1,0:T(8,128)(2,1)S(1)}, u32[]{:S(2)}, u32[]{:S(2)}) collective-permute-start(bf16[4,4,48,384]{3,2,1,0:T(8,128)(2,1)S(1)} %get-tuple-element.250), channel_id=1, source_target_pairs={{0,16},{16,0},{1,17},{17,1},{2,18},{18,2},{3,19},{19,3},{4,20},{20... | collective-permute-start | bytes 1769480 | tf_op jit(solution)/shard_map/ppermute | solution.py:55
  73.8 1.2 copy-start.2
  90.9 10.7 %collective-permute-start.18 = (bf16[2,4,48,384]{3,2,1,0:T(8,128)(2,1)S(1)}, bf16[2,4,48,384]{3,2,1,0:T(8,128)(2,1)S(1)}, u32[]{:S(2)}, u32[]{:S(2)}) collective-permute-start(bf16[2,4,48,384]{3,2,1,0:T(8,128)(2,1)S(1)} %slice.124), channel_id=1, source_target_pairs={{0,16},{16,0},{1,17},{17,1},{2,18},{18,2},{3,19},{19,3},{4,20},{20... | collective-permute-start | bytes 884744 | tf_op jit(solution)/shard_map/ppermute | solution.py:55
  92.4 12.5 %collective-permute-start.19 = (bf16[2,4,48,384]{3,2,1,0:T(8,128)(2,1)S(1)}, bf16[2,4,48,384]{3,2,1,0:T(8,128)(2,1)S(1)}, u32[]{:S(2)}, u32[]{:S(2)}) collective-permute-start(bf16[2,4,48,384]{3,2,1,0:T(8,128)(2,1)S(1)} %slice.125), channel_id=1, source_target_pairs={{0,2},{1,3},{2,0},{3,1},{4,6},{5,7},{6,4},{7,5},{8,10},{9,11},{10,... | collective-permute-start | bytes 884744 | tf_op jit(solution)/shard_map/ppermute | solution.py:49
  105.3 4.6 %copy-start.1 = (bf16[4,4,4,48,384]{4,3,2,1,0:T(8,128)(2,1)}, bf16[4,4,4,48,384]{4,3,2,1,0:T(8,128)(2,1)S(1)}, u32[]{:S(2)}) copy-start(bf16[4,4,4,48,384]{4,3,2,1,0:T(8,128)(2,1)S(1)} %pad_maximum_fusion.refs_0_) | copy-start | bytes 7077892
  105.3 4.6 %collective-permute-start.20 = (bf16[4,4,4,48,384]{4,3,2,1,0:T(8,128)(2,1)S(1)}, bf16[4,4,4,48,384]{4,3,2,1,0:T(8,128)(2,1)S(1)}, u32[]{:S(2)}, u32[]{:S(2)}) collective-permute-start(bf16[4,4,4,48,384]{4,3,2,1,0:T(8,128)(2,1)S(1)} %pad_maximum_fusion.refs_0_), channel_id=1, source_target_pairs={{0,1},{1,0},{2,3},{3,2},{4,5},{5,4},{6,7},{7,6},{8,9},{9,8},{10,11... | collective-permute-start | bytes 7077896 | tf_op jit(solution)/shard_map/ppermute | solution.py:46
  109.9 1.4 copy-start.7
  173.3 12.4 %collective-permute-start.21 = (bf16[2,2,4,4,48,384]{5,4,3,2,1,0:T(8,128)(2,1)}, bf16[2,2,4,4,48,384]{5,4,3,2,1,0:T(8,128)(2,1)S(1)}, u32[]{:S(2)}, u32[]{:S(2)}) collective-permute-start(bf16[2,2,4,4,48,384]{5,4,3,2,1,0:T(8,128)(2,1)} %get-tuple-element.295), channel_id=1, source_target_pairs={{0,1},{1,0},{2,3},{3,2},{4,5},{5,4},{6,7},{7,6},{8,9},{9,8},{10,11... | collective-permute-start | bytes 7077896 | tf_op jit(solution)/shard_map/ppermute | solution.py:46
  173.3 12.3 %copy-start.5 = (bf16[2,2,4,4,48,384]{5,4,3,2,1,0:T(8,128)(2,1)S(1)}, bf16[2,2,4,4,48,384]{5,4,3,2,1,0:T(8,128)(2,1)}, u32[]{:S(2)}) copy-start(bf16[2,2,4,4,48,384]{5,4,3,2,1,0:T(8,128)(2,1)} %get-tuple-element.294) | copy-start | bytes 7077892
  185.6 1.4 copy-start.6
  187.0 32.3 %collective-permute-start.22 = (bf16[4,4,48,384]{3,2,1,0:T(8,128)(2,1)S(1)}, bf16[4,4,48,384]{3,2,1,0:T(8,128)(2,1)S(1)}, u32[]{:S(2)}, u32[]{:S(2)}) collective-permute-start(bf16[4,4,48,384]{3,2,1,0:T(8,128)(2,1)S(1)} %get-tuple-element.306), channel_id=1, source_target_pairs={{0,2},{1,3},{2,0},{3,1},{4,6},{5,7},{6,4},{7,5},{8,10},{9,11},{10,... | collective-permute-start | bytes 1769480 | tf_op jit(solution)/shard_map/ppermute | solution.py:49
  188.6 30.7 %collective-permute-start.23 = (bf16[4,4,48,384]{3,2,1,0:T(8,128)(2,1)S(1)}, bf16[4,4,48,384]{3,2,1,0:T(8,128)(2,1)}, u32[]{:S(2)}, u32[]{:S(2)}) collective-permute-start(bf16[4,4,48,384]{3,2,1,0:T(8,128)(2,1)S(1)} %get-tuple-element.307), channel_id=1, source_target_pairs={{0,16},{16,0},{1,17},{17,1},{2,18},{18,2},{3,19},{19,3},{4,20},{20... | collective-permute-start | bytes 1769480 | tf_op jit(solution)/shard_map/ppermute | solution.py:55
  190.1 29.4 %collective-permute-start.24 = (bf16[4,4,48,384]{3,2,1,0:T(8,128)(2,1)S(1)}, bf16[4,4,48,384]{3,2,1,0:T(8,128)(2,1)}, u32[]{:S(2)}, u32[]{:S(2)}) collective-permute-start(bf16[4,4,48,384]{3,2,1,0:T(8,128)(2,1)S(1)} %get-tuple-element.308), channel_id=1, source_target_pairs={{0,18},{1,19},{2,16},{3,17},{4,22},{5,23},{6,20},{7,21},{8,26},{9,... | collective-permute-start | bytes 1769480 | tf_op jit(solution)/shard_map/ppermute | solution.py:59
  222.1 2.0 copy-start.14
  224.0 22.1 %collective-permute-start.25 = (bf16[2,2,4,4,48,384]{5,4,3,2,1,0:T(8,128)(2,1)}, bf16[2,2,4,4,48,384]{5,4,3,2,1,0:T(8,128)(2,1)S(1)}, u32[]{:S(2)}, u32[]{:S(2)}) collective-permute-start(bf16[2,2,4,4,48,384]{5,4,3,2,1,0:T(8,128)(2,1)} %get-tuple-element.317), channel_id=1, source_target_pairs={{0,1},{1,0},{2,3},{3,2},{4,5},{5,4},{6,7},{7,6},{8,9},{9,8},{10,11... | collective-permute-start | bytes 7077896 | tf_op jit(solution)/shard_map/ppermute | solution.py:46
  224.1 22.0 %collective-permute-start.29 = (bf16[4,48,768]{2,1,0:T(8,128)(2,1)S(1)}, bf16[4,48,768]{2,1,0:T(8,128)(2,1)S(1)}, u32[]{:S(2)}, u32[]{:S(2)}) collective-permute-start(bf16[4,48,768]{2,1,0:T(8,128)(2,1)S(1)} %copy-done.14), channel_id=1, source_target_pairs={{0,16},{16,0},{1,17},{17,1},{2,18},{18,2},{3,19},{19,3},{4,20},{20... | collective-permute-start | bytes 884744 | tf_op jit(solution)/shard_map/ppermute | solution.py:55
  225.6 20.5 %collective-permute-start.26 = (bf16[4,48,384]{2,1,0:T(8,128)(2,1)S(1)}, bf16[4,48,384]{2,1,0:T(8,128)(2,1)S(1)}, u32[]{:S(2)}, u32[]{:S(2)}) collective-permute-start(bf16[4,48,384]{2,1,0:T(8,128)(2,1)S(1)} %get-tuple-element.318), channel_id=1, source_target_pairs={{0,4},{1,5},{2,6},{3,7},{4,0},{5,1},{6,2},{7,3},{8,12},{9,13},{10,... | collective-permute-start | bytes 442376 | tf_op jit(solution)/shard_map/ppermute | solution.py:52
  227.9 18.2 %collective-permute-start.27 = (bf16[4,48,384]{2,1,0:T(8,128)(2,1)S(1)}, bf16[4,48,384]{2,1,0:T(8,128)(2,1)S(1)}, u32[]{:S(2)}, u32[]{:S(2)}) collective-permute-start(bf16[4,48,384]{2,1,0:T(8,128)(2,1)S(1)} %get-tuple-element.319), channel_id=1, source_target_pairs={{0,8},{1,9},{2,10},{3,11},{4,12},{5,13},{6,14},{7,15},{8,0},{9,1},... | collective-permute-start | bytes 442376 | tf_op jit(solution)/shard_map/ppermute | solution.py:52
  229.0 17.1 %collective-permute-start.28 = (bf16[4,48,384]{2,1,0:T(8,128)(2,1)S(1)}, bf16[4,48,384]{2,1,0:T(8,128)(2,1)S(1)}, u32[]{:S(2)}, u32[]{:S(2)}) collective-permute-start(bf16[4,48,384]{2,1,0:T(8,128)(2,1)S(1)} %get-tuple-element.320), channel_id=1, source_target_pairs={{0,12},{1,13},{2,14},{3,15},{4,8},{5,9},{6,10},{7,11},{8,4},{9,5},... | collective-permute-start | bytes 442376 | tf_op jit(solution)/shard_map/ppermute | solution.py:52
  230.5 15.7 %copy-start.3 = (bf16[2,2,4,4,48,384]{5,4,3,2,1,0:T(8,128)(2,1)S(1)}, bf16[2,2,4,4,48,384]{5,4,3,2,1,0:T(8,128)(2,1)}, u32[]{:S(2)}) copy-start(bf16[2,2,4,4,48,384]{5,4,3,2,1,0:T(8,128)(2,1)} %get-tuple-element.305) | copy-start | bytes 7077892
  246.1 2.0 copy-start.19
  246.1 1.9 copy-start.20
  246.1 1.9 copy-start.21
  246.1 1.9 copy-start.15
  246.1 2.2 copy-start.4
  248.3 32.3 %collective-permute-start.30 = (bf16[4,4,48,384]{3,2,1,0:T(8,128)(2,1)}, bf16[4,4,48,384]{3,2,1,0:T(8,128)(2,1)S(1)}, u32[]{:S(2)}, u32[]{:S(2)}) collective-permute-start(bf16[4,4,48,384]{3,2,1,0:T(8,128)(2,1)} %get-tuple-element.334), channel_id=1, source_target_pairs={{0,2},{1,3},{2,0},{3,1},{4,6},{5,7},{6,4},{7,5},{8,10},{9,11},{10,... | collective-permute-start | bytes 1769480 | tf_op jit(solution)/shard_map/ppermute | solution.py:49
  249.6 31.0 %collective-permute-start.31 = (bf16[4,4,48,384]{3,2,1,0:T(8,128)(2,1)}, bf16[4,4,48,384]{3,2,1,0:T(8,128)(2,1)}, u32[]{:S(2)}, u32[]{:S(2)}) collective-permute-start(bf16[4,4,48,384]{3,2,1,0:T(8,128)(2,1)} %get-tuple-element.335), channel_id=1, source_target_pairs={{0,16},{16,0},{1,17},{17,1},{2,18},{18,2},{3,19},{19,3},{4,20},{20... | collective-permute-start | bytes 1769480 | tf_op jit(solution)/shard_map/ppermute | solution.py:55
  250.7 29.9 %collective-permute-start.32 = (bf16[4,4,48,384]{3,2,1,0:T(8,128)(2,1)}, bf16[4,4,48,384]{3,2,1,0:T(8,128)(2,1)}, u32[]{:S(2)}, u32[]{:S(2)}) collective-permute-start(bf16[4,4,48,384]{3,2,1,0:T(8,128)(2,1)} %get-tuple-element.336), channel_id=1, source_target_pairs={{0,18},{1,19},{2,16},{3,17},{4,22},{5,23},{6,20},{7,21},{8,26},{9,... | collective-permute-start | bytes 1769480 | tf_op jit(solution)/shard_map/ppermute | solution.py:59
  253.6 24.6 %all-to-all-start = ((f32[32,1,768]{2,1,0:T(1,128)}), f32[32,1,768]{2,1,0:T(1,128)}, u32[]{:S(2)}, u32[]{:S(2)}) async-start(f32[32,1,768]{2,1,0:T(1,128)} %reshape.96), calls=%async_computation.1 | async-start | bytes 196608 | tf_op jit(solution)/shard_map/all_to_all | solution.py:976
  280.6 6.4 %copy-start.8 = (bf16[4,48,384]{2,1,0:T(8,128)(2,1)S(1)}, bf16[4,48,384]{2,1,0:T(8,128)(2,1)}, u32[]{:S(2)}) copy-start(bf16[4,48,384]{2,1,0:T(8,128)(2,1)} %fusion.14.refs_2_) | copy-start | bytes 442372
  282.5 8.3 %collective-permute-start.33 = (bf16[4,48,384]{2,1,0:T(8,128)(2,1)S(1)}, bf16[4,48,384]{2,1,0:T(8,128)(2,1)S(1)}, u32[]{:S(2)}, u32[]{:S(2)}) collective-permute-start(bf16[4,48,384]{2,1,0:T(8,128)(2,1)S(1)} %get-tuple-element.345), channel_id=1, source_target_pairs={{0,4},{1,5},{2,6},{3,7},{4,0},{5,1},{6,2},{7,3},{8,12},{9,13},{10,... | collective-permute-start | bytes 442376 | tf_op jit(solution)/shard_map/ppermute | solution.py:52
  283.4 14.0 %collective-permute-start.34 = (bf16[4,48,384]{2,1,0:T(8,128)(2,1)S(1)}, bf16[4,48,384]{2,1,0:T(8,128)(2,1)S(1)}, u32[]{:S(2)}, u32[]{:S(2)}) collective-permute-start(bf16[4,48,384]{2,1,0:T(8,128)(2,1)S(1)} %get-tuple-element.346), channel_id=1, source_target_pairs={{0,8},{1,9},{2,10},{3,11},{4,12},{5,13},{6,14},{7,15},{8,0},{9,1},... | collective-permute-start | bytes 442376 | tf_op jit(solution)/shard_map/ppermute | solution.py:52
  285.5 11.9 %collective-permute-start.35 = (bf16[4,48,384]{2,1,0:T(8,128)(2,1)S(1)}, bf16[4,48,384]{2,1,0:T(8,128)(2,1)S(1)}, u32[]{:S(2)}, u32[]{:S(2)}) collective-permute-start(bf16[4,48,384]{2,1,0:T(8,128)(2,1)S(1)} %get-tuple-element.347), channel_id=1, source_target_pairs={{0,12},{1,13},{2,14},{3,15},{4,8},{5,9},{6,10},{7,11},{8,4},{9,5},... | collective-permute-start | bytes 442376 | tf_op jit(solution)/shard_map/ppermute | solution.py:52
  287.0 10.4 %collective-permute-start.36 = (bf16[4,48,384]{2,1,0:T(8,128)(2,1)S(1)}, bf16[4,48,384]{2,1,0:T(8,128)(2,1)S(1)}, u32[]{:S(2)}, u32[]{:S(2)}) collective-permute-start(bf16[4,48,384]{2,1,0:T(8,128)(2,1)S(1)} %copy-done.8), channel_id=1, source_target_pairs={{0,16},{16,0},{1,17},{17,1},{2,18},{18,2},{3,19},{19,3},{4,20},{20... | collective-permute-start | bytes 442376 | tf_op jit(solution)/shard_map/ppermute | solution.py:55
  297.4 6.6 %copy-start.17 = (bf16[4,48,384]{2,1,0:T(8,128)(2,1)}, bf16[4,48,384]{2,1,0:T(8,128)(2,1)S(1)}, u32[]{:S(2)}) copy-start(bf16[4,48,384]{2,1,0:T(8,128)(2,1)S(1)} %collective-permute-done.36.refs_3_) | copy-start | bytes 442372
  297.5 6.5 %copy-start.9 = (bf16[4,48,384]{2,1,0:T(8,128)(2,1)}, bf16[4,48,384]{2,1,0:T(8,128)(2,1)S(1)}, u32[]{:S(2)}) copy-start(bf16[4,48,384]{2,1,0:T(8,128)(2,1)S(1)} %fusion.17.refs_4_) | copy-start | bytes 442372
  297.5 5.2 %collective-permute-start.37 = (bf16[4,48,384]{2,1,0:T(8,128)(2,1)S(1)}, bf16[4,48,384]{2,1,0:T(8,128)(2,1)S(1)}, u32[]{:S(2)}, u32[]{:S(2)}) collective-permute-start(bf16[4,48,384]{2,1,0:T(8,128)(2,1)S(1)} %fusion.17.refs_4_), channel_id=1, source_target_pairs={{0,16},{16,0},{1,17},{17,1},{2,18},{18,2},{3,19},{19,3},{4,20},{20... | collective-permute-start | bytes 442376 | tf_op jit(solution)/shard_map/ppermute | solution.py:55
  302.7 1.2 copy-start.18
Sparse Core Ops, SparseCore 0:
  43.2 70.9 all-gather.1
  140.0 82.1 reduce-scatter.1
where the time goes:
time: 318 us; the launch traced here: 314 us
  Pallas kernels  163 us (51%)
  waiting for transfers between devices  62.5 us (20%)
  starting transfers between devices  51.5 us (16%)
  between operations  14.8 us (5%)
  other arithmetic  11.8 us (4%)
  local copies, waits for them, and re-layouts  10.2 us (3%)
    pallas_call x2, Pallas kernels, feed_call(): pl.pallas_call(functools.partial(feed_kernel, place, weight.kind, form, l...  61.9 us
    pallas_call x1, Pallas kernels, attend_back_call(): pl.pallas_call(functools.partial(attend_back_kernel, place, kind, rows, m...  28.8 us
    ppermute x15, starting transfers between devices, along_z(): return lambda v: lax.ppermute(v, 'fsdp', self.swap(4 * d))  24.2 us
    pallas_call x2, Pallas kernels, attend_call(): pl.pallas_call(functools.partial(attend_kernel, place, weight.kind, len(w...  22 us
    all_to_all x1, waiting for transfers between devices, local(): late = lax.all_to_all(late, ('rep', 'fsdp'), 0, 0, tiled=True)  18.6 us
    ppermute x15, waiting for transfers between devices, along_z(): return lambda v: lax.ppermute(v, 'fsdp', self.swap(4 * d))  18.4 us
    pallas_call x1, Pallas kernels, last_call(): pl.pallas_call(functools.partial(last_kernel, rows, [d.shape[0] for d in...  15.6 us
    pallas_call x1, Pallas kernels, middle_call(): pl.pallas_call(kernel, grid=(rows.images,), in_specs=[block] * 4 + [whole...  12.3 us
  transfers between devices with their start and end apart: 41, of which 16 were waited for; matrix products, arithmetic and copies ran while one was open for 3% of the time, Pallas kernels for 50%

commit v1 on v0

--- a/solution.py
+++ b/solution.py
@@ -167,8 +167,8 @@
     def begin(self, name, steps):
         self.live[name] = (steps, next(steps), None)
 
-    def send(self, *arrays):
-        waiting = [name for name, (_, pairs, sent) in self.live.items() if sent is None]
+    def send(self, *arrays, but=()):
+        waiting = [name for name, (_, _, sent) in self.live.items() if sent is None and name not in but]
         flat = [v for name in waiting for _, v in self.live[name][1]]
         flat = list(lax.optimization_barrier(tuple(flat) + tuple(arrays)))
         for name in waiting:
@@ -635,6 +635,9 @@
     )(*args)
 
 
+PAIR = 2
+
+
 def middle_kernel(rows, resid, acc, gn, grad, vec, w, out_o, low_o, da_o, sums_o):
     xhat, scale = norm_stats(resid[...])
     gain = vec[6:7, :]
@@ -655,17 +658,19 @@
     )
     final = resid[...] + acc[...] + vec[8:9, :]
     j = pl.program_id(0)
-    for i in range(rows.images):
+    for i in range(rows.images // PAIR):
 
         @pl.when(j == i)
         def _():
             sums_o[...] = sums if i == 0 else sums_o[...] + sums
-            out_o[rows.patches * i : rows.patches * (i + 1), :] = final[: rows.patches]
+            for u in range(PAIR):
+                lo = rows.patches * (PAIR * i + u)
+                out_o[lo : lo + rows.patches, :] = final[rows.pad * u : rows.pad * u + rows.patches]
 
 
 def middle_call(rows, resid, acc, gn, grad, vec, weight):
     width = resid.shape[1]
-    block = rows.block(width)
+    block = rows.block(width, PAIR)
     outs = [
         jax.ShapeDtypeStruct((rows.raw, width), BF16),
         jax.ShapeDtypeStruct((rows.all, width), BF16),
@@ -676,13 +681,13 @@
     def kernel(resid, acc, gn, grad, vec, w, out_o, low_o, da_o, sums_o, out_s):
         middle_kernel(rows, resid, acc, gn, grad, vec, w, out_s, low_o, da_o, sums_o)
 
-        @pl.when(pl.program_id(0) == rows.images - 1)
+        @pl.when(pl.program_id(0) == rows.images // PAIR - 1)
         def _():
             out_o[...] = out_s[...].astype(BF16)
 
     return pl.pallas_call(
         kernel,
-        grid=(rows.images,),
+        grid=(rows.images // PAIR,),
         in_specs=[block] * 4 + [whole(vec.shape), whole(weight.shape)],
         out_specs=[whole(outs[0].shape), block, block, whole(outs[3].shape)],
         out_shape=outs,
@@ -792,11 +797,15 @@
     total = low[...].astype(F32) + norm_back(up, xhat, scale, gain)
     row = lax.broadcasted_iota(jnp.int32, (rows.pad, 1), 0)
     j = pl.program_id(0)
-    for i in range(rows.images):
+    for i in range(rows.images // PAIR):
 
         @pl.when(j == i)
         def _():
-            chosen = jnp.logical_and(cols[: rows.pad, i : i + 1] > 0.5, row < rows.patches)
+            flagged = [
+                jnp.logical_and(cols[: rows.pad, PAIR * i + u : PAIR * i + u + 1] > 0.5, row < rows.patches)
+                for u in range(PAIR)
+            ]
+            chosen = jnp.concatenate([jnp.where(f, 1.0, 0.0) for f in flagged], axis=0) > 0.5
             sums = jnp.concatenate(
                 [
                     jnp.sum(jnp.where(chosen, total, 0.0), axis=0, keepdims=True),
@@ -806,9 +815,12 @@
                 axis=0,
             )
             sums_o[...] = sums if i == 0 else sums_o[...] + sums
-            out_o[rows.patches * i : rows.patches * (i + 1), :] = jnp.where(chosen, 0.0, total)[: rows.patches]
-
-    @pl.when(j == rows.images - 1)
+            kept = jnp.where(chosen, 0.0, total)
+            for u in range(PAIR):
+                lo = rows.patches * (PAIR * i + u)
+                out_o[lo : lo + rows.patches, :] = kept[rows.pad * u : rows.pad * u + rows.patches]
+
+    @pl.when(j == rows.images // PAIR - 1)
     def _():
         groups = [b[g] for b, group_count in zip(biases, counts) for g in range(group_count)]
         query = jnp.concatenate([g[:, :GROUP] for g in groups], axis=1)
@@ -826,7 +838,7 @@
 
 def last_call(rows, count, copies, base, low, flags, vec, w, dqkv, biases, two, feeds):
     width = base.shape[1]
-    block = rows.block(width)
+    block = rows.block(width, PAIR)
     outs = [
         jax.ShapeDtypeStruct((rows.raw, width), F32),
         jax.ShapeDtypeStruct((copies * count, 16, width // count), F32),
@@ -835,9 +847,9 @@
     small = [*biases, two, *feeds]
     return pl.pallas_call(
         functools.partial(last_kernel, rows, [d.shape[0] for d in dqkv], quarter, count),
-        grid=(rows.images,),
+        grid=(rows.images // PAIR,),
         in_specs=[block, block, whole(flags.shape), whole(vec.shape), whole(w.shape)]
-        + [pl.BlockSpec((d.shape[0], rows.pad, width), lambda j: (0, j, 0)) for d in dqkv]
+        + [pl.BlockSpec((d.shape[0], PAIR * rows.pad, width), lambda j: (0, j, 0)) for d in dqkv]
         + [whole(v.shape) for v in small],
         out_specs=[whole(out.shape) for out in outs],
         out_shape=outs,
@@ -956,7 +968,7 @@
         flow.begin("c", scatter_wide(place, *sums_c))
         dqkv, f0 = flow.meet(["f1"], dqkv, f0)
         flow.begin("f0", send_twin(place, f0))
-        (dqkv,) = flow.send(dqkv)
+        (dqkv,) = flow.send(dqkv, but=("f1",))
     input_grad, late = last_call(
         rows,
         count,
@@ -972,9 +984,9 @@
         [gb_0, gb_1],
     )
     if place:
-        late, input_grad = flow.turn(["c", "f1", "f0"], late, input_grad)
+        late, input_grad = flow.turn(["c", "f0"], late, input_grad)
         late = lax.all_to_all(late, ("rep", "fsdp"), 0, 0, tiled=True)
-        (late,) = flow.meet(["c"], late)
+        (late,) = flow.meet(["c", "f1"], late)
         flow.begin("fy", send_twin(place, flow.done["f1"]))
         (late,) = flow.send(late)
         (late,) = flow.meet(["c", "fy"], late)

time: 318 us -> 314 us (0.987)
  no operation moved by 1% of the time
where the time goes in v1:
time: 314 us; the launch traced here: 309 us
  Pallas kernels  160 us (51%)
  waiting for transfers between devices  62.5 us (20%)
  starting transfers between devices  51.4 us (16%)
  between operations  14.8 us (5%)
  local copies, waits for them, and re-layouts  10.4 us (3%)
  other arithmetic  10.3 us (3%)
    pallas_call x2, Pallas kernels, feed_call(): pl.pallas_call(functools.partial(feed_kernel, place, weight.kind, form, l...  61.8 us
    pallas_call x1, Pallas kernels, attend_back_call(): pl.pallas_call(functools.partial(attend_back_kernel, place, kind, rows, m...  28.8 us
    ppermute x15, starting transfers between devices, along_z(): return lambda v: lax.ppermute(v, 'fsdp', self.swap(4 * d))  24.9 us
    pallas_call x2, Pallas kernels, attend_call(): pl.pallas_call(functools.partial(attend_kernel, place, weight.kind, len(w...  21.9 us
    ppermute x15, waiting for transfers between devices, along_z(): return lambda v: lax.ppermute(v, 'fsdp', self.swap(4 * d))  19.7 us
    all_to_all x1, waiting for transfers between devices, local(): late = lax.all_to_all(late, ('rep', 'fsdp'), 0, 0, tiled=True)  16.1 us
    pallas_call x1, Pallas kernels, last_call(): pl.pallas_call(functools.partial(last_kernel, rows, [d.shape[0] for d in...  13.3 us
    pallas_call x1, Pallas kernels, middle_call(): pl.pallas_call(kernel, grid=(rows.images // PAIR,), in_specs=[block] * 4...  11.6 us
  transfers between devices with their start and end apart: 41, of which 16 were waited for; matrix products, arithmetic and copies ran while one was open for 3% of the time, Pallas kernels for 50%

profile of v1, /device:TPU:0, one launch (start us, length us, event | category | flops | bytes accessed | tf_op | source)
XLA Modules:
  0.0 309.3 jit_solution(2553225439247291230)
XLA Ops:
  7.2 1.2 broadcast_in_dim.39.refs_9_
  8.4 2.5 pack.1
  10.9 3.1 collective-permute-start
  14.0 2.6 collective-permute-start.1
  16.6 5.2 %pad_rows.1 = (bf16[1248,768]{1,0:T(8,128)(2,1)}, bf16[1248,768]{1,0:T(8,128)(2,1)}) custom-call(bf16[1176,768]{1,0:T(8,128)(2,1)} %tokens, bf16[1176,768]{1,0:T(8,128)(2,1)} %grads), custom_call_target="tpu_custom_call" | custom-call | flops 57500000 | bytes 150000 | tf_op jit(solution)/shard_map/pad_rows/pallas_call | solution.py:327
  21.8 2.8 collective-permute-done.1
  25.4 1.5 collective-permute-start.3
  26.9 1.6 collective-permute-start.6
  28.6 1.4 collective-permute-start.7
  30.0 1.4 collective-permute-start.8
  31.3 3.1 collective-permute-done.3
  34.5 1.7 collective-permute-done.5.refs_3_
  37.1 0.8 reshape.93.vec
  37.9 5.1 %norm_one.1 = (bf16[1248,768]{1,0:T(8,128)(2,1)}, bf16[1248,768]{1,0:T(8,128)(2,1)}) custom-call(bf16[1248,768]{1,0:T(8,128)(2,1)} %get-tuple-element.212.tokens, s32[6,196]{1,0:T(8,128)} %flags.3, f32[16,768]{1,0:T(8,128)} %reshape.93.vec), custom_call_target="tpu_custom_call" | custom-call | flops 57500000 | bytes 150000 | tf_op jit(solution)/shard_map/norm_one/pallas_call | solution.py:341
  43.6 1.6 collective-permute-start.10
  45.2 1.4 collective-permute-start.11
  47.2 2.4 collective-permute-start.12
  49.5 1.0 collective-permute-start.13
  50.5 4.2 %collective-permute-done.12 = bf16[4,48,384]{2,1,0:T(8,128)(2,1)S(1)} collective-permute-done((bf16[4,48,384]{2,1,0:T(8,128)(2,1)S(1)}, bf16[4,48,384]{2,1,0:T(8,128)(2,1)S(1)}, u32[]{:S(2)}, u32[]{:S(2)}) %collective-permute-start.12) | collective-permute-done | bytes 147488 | tf_op jit(solution)/shard_map/ppermute | solution.py:52
  54.7 1.5 collective-permute-start.14
  56.3 8.5 %attend.2 = (bf16[3,1248,256]{2,1,0:T(8,128)(2,1)}, bf16[3,1248,256]{2,1,0:T(8,128)(2,1)}, bf16[3,1248,256]{2,1,0:T(8,128)(2,1)}, bf16[3,1248,256]{2,1,0:T(8,128...) custom-call(bf16[1248,768]{1,0:T(8,128)(2,1)} %get-tuple-element.259.norm, ...), custom_call_target="tpu_custom_call" | custom-call | flops 92000000 | bytes 240000 | tf_op jit(solution)/shard_map/attend/pallas_call | solution.py:493
  64.8 2.2 collective-permute-done.13
  66.9 2.8 collective-permute-done.9
  70.2 1.6 collective-permute-start.15
  71.8 1.5 collective-permute-start.16
  73.9 1.2 copy-done.2
  75.1 13.4 %attend.3 = (bf16[3,1248,256]{2,1,0:T(8,128)(2,1)}, bf16[3,1248,256]{2,1,0:T(8,128)(2,1)}, bf16[3,1248,256]{2,1,0:T(8,128)(2,1)}, bf16[3,1248,256]{2,1,0:T(8,128...) custom-call(bf16[1248,768]{1,0:T(8,128)(2,1)} %get-tuple-element.259, ...), custom_call_target="tpu_custom_call", output_to_operand_aliasing={{0}: (4, {}), {1}: (5, {}), {2}: (6, {}), {3}: (7, {}), {4}... | custom-call | flops 161000000 | bytes 420000 | tf_op jit(solution)/shard_map/attend/pallas_call | solution.py:493
  88.5 2.6 collective-permute-done.15
  91.2 1.4 collective-permute-start.18
  92.7 2.4 collective-permute-start.19
  95.1 6.8 %project.1 = (f32[1248,768]{1,0:T(8,128)}, bf16[1248,768]{1,0:T(8,128)(2,1)}, bf16[1,768,768]{2,1,0:T(8,128)(2,1)}) custom-call(f32[16,768]{1,0:T(8,128)} %reshape.93.vec, bf16[1248,768]{1,0:T(8,128)(2,1)} %get-tuple-element.213.base, bf16[3,1248,256]{2,1,0:T(8,128)(2,1)} %get-tuple-element.271.att.refs_5_, bf16[4,4,3,48,384]{4,3,2,1,0:T(8,128)(2,1)} %copy-done, ...), custom_call_target="tpu_custom_call" | custom-call | flops 80500000 | bytes 210000 | tf_op jit(solution)/shard_map/project/pallas_call | solution.py:537
  101.9 3.1 collective-permute-done.19
  105.5 4.5 %collective-permute-done.20.refs_1_ = bf16[4,4,4,48,384]{4,3,2,1,0:T(8,128)(2,1)S(1)} collective-permute-done((bf16[4,4,4,48,384]{4,3,2,1,0:T(8,128)(2,1)S(1)}, bf16[4,4,4,48,384]{4,3,2,1,0:T(8,128)(2,1)S(1)}, u32[]{:S(2)}, u32[]{:S(2)}) %collective-permute-start.20) | collective-permute-done | bytes 2359328 | tf_op jit(solution)/shard_map/ppermute | solution.py:46
  110.0 1.5 copy-done.7
  111.5 28.8 %feed.2 = (f32[1248,768]{1,0:T(8,128)}, f32[1248,768]{1,0:T(8,128)}, f32[2,1,768]{2,1,0:T(1,128)}, bf16[4,768,768]{2,1,0:T(8,128)(2,1)}) custom-call(bf16[1248,768]{1,0:T(8,128)(2,1)} %get-tuple-element.281.norm, bf16[1248,768]{1,0:T(8,128)(2,1)} %get-tuple-element.282.grad, f32[16,768]{1,0:T(8,128)} %reshape.93.vec, bf16[4,4,4,48,384]{4,3,2,1,0:T(8,128)(2,1)} %copy-done.1, ...), custom_call_target="tpu_custom_call" | custom-call | flops 345000000 | bytes 900000 | tf_op jit(solution)/shard_map/feed/pallas_call | solution.py:625
  140.3 33.1 %feed.3 = (f32[1248,768]{1,0:T(8,128)}, f32[1248,768]{1,0:T(8,128)}, f32[2,1,768]{2,1,0:T(1,128)}, bf16[2,2,4,4,48,384]{5,4,3,2,1,0:T(8,128)(2,1)}, bf16[2,2,4,4,48,384]{5,4,3,2,1,0:T(8,128)(2,1)}) custom-call(bf16[1248,768]{1,0:T(8,128)(2,1)} %get-tuple-element.281.norm, bf16[1248,768]{1,0:T(8,128)(2,1)} %get-tuple-element.282.grad, ...), custom_call_target="tpu_custom_call" | custom-call | flops 345000000 | bytes 900000 | tf_op jit(solution)/shard_map/feed/pallas_call | solution.py:625
  173.4 11.6 %middle.1 = (bf16[1176,768]{1,0:T(8,128)(2,1)}, bf16[1248,768]{1,0:T(8,128)(2,1)}, bf16[1248,768]{1,0:T(8,128)(2,1)}, f32[4,768]{1,0:T(4,128)}) custom-call(f32[1248,768]{1,0:T(8,128)} %get-tuple-element.272.resid, f32[1248,768]{1,0:T(8,128)} %get-tuple-element.290.acc, f32[1248,768]{1,0:T(8,128)} %get-tuple-element.291.gn, ...), custom_call_target="tpu_custom_call" | custom-call | flops 138000000 | bytes 360000 | tf_op jit(solution)/shard_map/middle/pallas_call | solution.py:688
  185.6 0.9 copy-done.6
  186.5 1.6 collective-permute-start.22
  188.1 1.7 collective-permute-start.23
  190.0 28.8 %attend_back.1 = (bf16[3,1248,768]{2,1,0:T(8,128)(2,1)}, f32[3,1,768]{2,1,0:T(1,128)}, bf16[2,2,4,4,48,384]{5,4,3,2,1,0:T(8,128)(2,1)}, bf16[2,2,4,4,48,384]{5,4,3,2,1,0:T(8,128)(2,1)}) custom-call(bf16[1248,768]{1,0:T(8,128)(2,1)} %get-tuple-element.259.norm, bf16[1248,768]{1,0:T(8,128)(2,1)} %get-tuple-element.302.da, ...), custom_call_target="tpu_custom_call" | custom-call | flops 379500000 | bytes 990000 | tf_op jit(solution)/shard_map/attend_back/pallas_call | solution.py:766
  219.1 3.5 %reduce-scatter.2.cloned.1.call-done.refs_0_ = bf16[4,48,768]{2,1,0:T(8,128)(2,1)} async-done(((bf16[4,768,768]{2,1,0:T(8,128)(2,1)}), bf16[4,48,768]{2,1,0:T(8,128)(2,1)}) %reduce-scatter.2.cloned.1.call-update) | async-done | bytes 294928 | tf_op jit(solution)/shard_map/reduce_scatter | solution.py:897
  222.6 1.4 collective-permute-start.26
  224.0 13.3 %last.1 = (f32[1176,768]{1,0:T(8,128)}, f32[32,16,48]{2,1,0:T(8,128)}) custom-call(bf16[1248,768]{1,0:T(8,128)(2,1)} %get-tuple-element.213.base, bf16[1248,768]{1,0:T(8,128)(2,1)} %get-tuple-element.307.refs_4_.low, s32[6,196]{1,0:T(8,128)} %flags.3, f32[16,768]{1,0:T(8,128)} %reshape.93.vec, bf16[3,768,768]{2,1,0:T(8,128)(2,1)} %get-tuple-element.319.w, ...), custom_call_target="tpu_custom_call" | custom-call | flops 17250000896 | bytes 45000000 | tf_op jit(solution)/shard_map/last/pallas_call | solution.py:848
  237.3 2.1 fusion.5
  240.2 1.5 fusion.11
  243.3 2.4 collective-permute-start.29
  245.7 1.2 collective-permute-start.30
  247.0 0.9 reshape.96
  247.9 3.8 %all-to-all-start = ((f32[32,1,768]{2,1,0:T(1,128)}), f32[32,1,768]{2,1,0:T(1,128)S(1)}, u32[]{:S(2)}, u32[]{:S(2)}) async-start(f32[32,1,768]{2,1,0:T(1,128)} %reshape.96), calls=%async_computation.1 | async-start | bytes 196608 | tf_op jit(solution)/shard_map/all_to_all | solution.py:988
  251.7 2.7 collective-permute-start.31
  254.4 1.5 collective-permute-start.32
  255.9 16.1 %all-to-all-done = f32[32,1,768]{2,1,0:T(1,128)S(1)} async-done(((f32[32,1,768]{2,1,0:T(1,128)}), f32[32,1,768]{2,1,0:T(1,128)S(1)}, u32[]{:S(2)}, u32[]{:S(2)}) %all-to-all-start) | async-done | bytes 98336 | tf_op jit(solution)/shard_map/all_to_all | solution.py:988
  272.4 0.9 reduce
  273.5 2.0 fusion.2
  275.6 1.1 fusion.14.refs_2_
  276.7 2.1 collective-permute-start.33
  278.8 1.0 collective-permute-start.34
  279.8 1.4 collective-permute-start.35
  281.3 1.0 collective-permute-start.36
  282.3 3.0 collective-permute-done.33
  285.2 7.5 %collective-permute-done.34 = bf16[4,48,384]{2,1,0:T(8,128)(2,1)S(1)} collective-permute-done((bf16[4,48,384]{2,1,0:T(8,128)(2,1)S(1)}, bf16[4,48,384]{2,1,0:T(8,128)(2,1)S(1)}, u32[]{:S(2)}, u32[]{:S(2)}) %collective-permute-start.34) | collective-permute-done | bytes 147488 | tf_op jit(solution)/shard_map/ppermute | solution.py:52
  293.6 4.5 %collective-permute-done.37.refs_5_ = bf16[4,48,384]{2,1,0:T(8,128)(2,1)S(1)} collective-permute-done((bf16[4,48,384]{2,1,0:T(8,128)(2,1)S(1)}, bf16[4,48,384]{2,1,0:T(8,128)(2,1)S(1)}, u32[]{:S(2)}, u32[]{:S(2)}) %collective-permute-start.37) | collective-permute-done | bytes 147488 | tf_op jit(solution)/shard_map/ppermute | solution.py:55
  299.3 2.8 unpack.1
  (114 shorter events, 10.7 us)
Async XLA Ops:
  7.2 133.1 %all-gather.2.cloned.1.call-start = ((), (), s32[]{:S(2)}) async-start(), calls=%async_computation.2 | async-start | bytes 5013504 | tf_op jit(solution)/shard_map/all_gather | solution.py:894
  10.9 10.9 %copy-start.13 = (bf16[4,48,768]{2,1,0:T(8,128)(2,1)S(1)}, bf16[4,48,768]{2,1,0:T(8,128)(2,1)}, u32[]{:S(2)}) copy-start(bf16[4,48,768]{2,1,0:T(8,128)(2,1)} %get-tuple-element.201) | copy-start | bytes 884740
  10.9 10.9 %collective-permute-start = (bf16[1,64,768]{2,1,0:T(8,128)(2,1)}, bf16[1,64,768]{2,1,0:T(8,128)(2,1)S(1)}, u32[]{:S(2)}, u32[]{:S(2)}) collective-permute-start(bf16[1,64,768]{2,1,0:T(8,128)(2,1)} %get-tuple-element.193), channel_id=1, source_target_pairs={{0,4},{1,5},{2,6},{3,7},{4,0},{5,1},{6,2},{7,3},{8,12},{9,13},{10,... | collective-permute-start | bytes 294920 | tf_op jit(solution)/shard_map/ppermute | solution.py:52
  14.0 10.6 %collective-permute-start.1 = (bf16[1,64,768]{2,1,0:T(8,128)(2,1)}, bf16[1,64,768]{2,1,0:T(8,128)(2,1)S(1)}, u32[]{:S(2)}, u32[]{:S(2)}) collective-permute-start(bf16[1,64,768]{2,1,0:T(8,128)(2,1)} %get-tuple-element.193), channel_id=1, source_target_pairs={{0,8},{1,9},{2,10},{3,11},{4,12},{5,13},{6,14},{7,15},{8,0},{9,1},... | collective-permute-start | bytes 294920 | tf_op jit(solution)/shard_map/ppermute | solution.py:52
  16.6 8.1 %collective-permute-start.2 = (bf16[1,64,768]{2,1,0:T(8,128)(2,1)}, bf16[1,64,768]{2,1,0:T(8,128)(2,1)S(1)}, u32[]{:S(2)}, u32[]{:S(2)}) collective-permute-start(bf16[1,64,768]{2,1,0:T(8,128)(2,1)} %get-tuple-element.193), channel_id=1, source_target_pairs={{0,12},{1,13},{2,14},{3,15},{4,8},{5,9},{6,10},{7,11},{8,4},{9,5},... | collective-permute-start | bytes 294920 | tf_op jit(solution)/shard_map/ppermute | solution.py:52
  16.6 5.2 %copy-start.16 = (bf16[3,48,768]{2,1,0:T(8,128)(2,1)S(1)}, bf16[3,48,768]{2,1,0:T(8,128)(2,1)}, u32[]{:S(2)}) copy-start(bf16[3,48,768]{2,1,0:T(8,128)(2,1)} %get-tuple-element.200) | copy-start | bytes 663556
  16.6 8.1 %copy-start.19 = (bf16[1,64,768]{2,1,0:T(8,128)(2,1)S(1)}, bf16[1,64,768]{2,1,0:T(8,128)(2,1)}, u32[]{:S(2)}) copy-start(bf16[1,64,768]{2,1,0:T(8,128)(2,1)} %get-tuple-element.193) | copy-start | bytes 294916
  25.4 9.0 %collective-permute-start.3 = (bf16[4,1,64,768]{3,2,0,1:T(8,128)(2,1)S(1)}, bf16[4,1,64,768]{3,2,0,1:T(8,128)(2,1)S(1)}, u32[]{:S(2)}, u32[]{:S(2)}) collective-permute-start(bf16[4,1,64,768]{3,2,0,1:T(8,128)(2,1)S(1)} %get-tuple-element.204), channel_id=1, source_target_pairs={{0,2},{1,3},{2,0},{3,1},{4,6},{5,7},{6,4},{7,5},{8,10},{9,11},{10,... | collective-permute-start | bytes 1179656 | tf_op jit(solution)/shard_map/ppermute | solution.py:49
  26.9 7.5 %collective-permute-start.4 = (bf16[4,1,64,768]{3,2,0,1:T(8,128)(2,1)S(1)}, bf16[4,1,64,768]{3,2,0,1:T(8,128)(2,1)S(1)}, u32[]{:S(2)}, u32[]{:S(2)}) collective-permute-start(bf16[4,1,64,768]{3,2,0,1:T(8,128)(2,1)S(1)} %get-tuple-element.204), channel_id=1, source_target_pairs={{0,1},{1,0},{2,3},{3,2},{4,5},{5,4},{6,7},{7,6},{8,9},{9,8},{10,11... | collective-permute-start | bytes 1179656 | tf_op jit(solution)/shard_map/ppermute | solution.py:46
  26.9 16.1 %collective-permute-start.6 = (bf16[3,48,384]{2,1,0:T(8,128)(2,1)S(1)}, bf16[3,48,384]{2,1,0:T(8,128)(2,1)S(1)}, u32[]{:S(2)}, u32[]{:S(2)}) collective-permute-start(bf16[3,48,384]{2,1,0:T(8,128)(2,1)S(1)} %constant_dynamic-slice_fusion.1), channel_id=1, source_target_pairs={{0,4},{1,5},{2,6},{3,7},{4,0},{5,1},{6,2},{7,3},{8,12},{9,13},{10,... | collective-permute-start | bytes 331784 | tf_op jit(solution)/shard_map/ppermute | solution.py:52
  28.6 14.5 %collective-permute-start.7 = (bf16[3,48,384]{2,1,0:T(8,128)(2,1)S(1)}, bf16[3,48,384]{2,1,0:T(8,128)(2,1)S(1)}, u32[]{:S(2)}, u32[]{:S(2)}) collective-permute-start(bf16[3,48,384]{2,1,0:T(8,128)(2,1)S(1)} %constant_dynamic-slice_fusion.1), channel_id=1, source_target_pairs={{0,8},{1,9},{2,10},{3,11},{4,12},{5,13},{6,14},{7,15},{8,0},{9,1},... | collective-permute-start | bytes 331784 | tf_op jit(solution)/shard_map/ppermute | solution.py:52
  30.0 13.1 %collective-permute-start.8 = (bf16[3,48,384]{2,1,0:T(8,128)(2,1)S(1)}, bf16[3,48,384]{2,1,0:T(8,128)(2,1)S(1)}, u32[]{:S(2)}, u32[]{:S(2)}) collective-permute-start(bf16[3,48,384]{2,1,0:T(8,128)(2,1)S(1)} %constant_dynamic-slice_fusion.1), channel_id=1, source_target_pairs={{0,12},{1,13},{2,14},{3,15},{4,8},{5,9},{6,10},{7,11},{8,4},{9,5},... | collective-permute-start | bytes 331784 | tf_op jit(solution)/shard_map/ppermute | solution.py:52
  34.4 8.7 %copy-start.10 = (bf16[4,1,64,768]{3,2,0,1:T(8,128)(2,1)}, bf16[4,1,64,768]{3,2,0,1:T(8,128)(2,1)S(1)}, u32[]{:S(2)}) copy-start(bf16[4,1,64,768]{3,2,0,1:T(8,128)(2,1)S(1)} %collective-permute-done.3) | copy-start | bytes 1179652
  34.4 8.7 %copy-start.11 = (bf16[4,1,64,768]{3,2,0,1:T(8,128)(2,1)}, bf16[4,1,64,768]{3,2,0,1:T(8,128)(2,1)S(1)}, u32[]{:S(2)}) copy-start(bf16[4,1,64,768]{3,2,0,1:T(8,128)(2,1)S(1)} %collective-permute-done.4) | copy-start | bytes 1179652
  34.4 1.8 collective-permute-start.5
  36.2 6.9 %copy-start.12 = (bf16[4,1,64,768]{3,2,1,0:T(8,128)(2,1)}, bf16[4,1,64,768]{3,2,1,0:T(8,128)(2,1)S(1)}, u32[]{:S(2)}) copy-start(bf16[4,1,64,768]{3,2,1,0:T(8,128)(2,1)S(1)} %collective-permute-done.5.refs_3_) | copy-start | bytes 1179652
  43.1 179.4 %reduce-scatter.2.cloned.1.call-start = ((), (), s32[]{:S(2)}) async-start(), calls=%async_computation.3 | async-start | bytes 5013504 | tf_op jit(solution)/shard_map/reduce_scatter | solution.py:897
  43.6 23.3 %collective-permute-start.10 = (bf16[4,3,48,384]{3,2,1,0:T(8,128)(2,1)S(1)}, bf16[4,3,48,384]{3,2,1,0:T(8,128)(2,1)S(1)}, u32[]{:S(2)}, u32[]{:S(2)}) collective-permute-start(bf16[4,3,48,384]{3,2,1,0:T(8,128)(2,1)S(1)} %get-tuple-element.225), channel_id=1, source_target_pairs={{0,16},{16,0},{1,17},{17,1},{2,18},{18,2},{3,19},{19,3},{4,20},{20... | collective-permute-start | bytes 1327112 | tf_op jit(solution)/shard_map/ppermute | solution.py:55
  45.2 21.8 %collective-permute-start.11 = (bf16[4,3,48,384]{3,2,1,0:T(8,128)(2,1)S(1)}, bf16[4,3,48,384]{3,2,1,0:T(8,128)(2,1)S(1)}, u32[]{:S(2)}, u32[]{:S(2)}) collective-permute-start(bf16[4,3,48,384]{3,2,1,0:T(8,128)(2,1)S(1)} %get-tuple-element.225), channel_id=1, source_target_pairs={{0,18},{1,19},{2,16},{3,17},{4,22},{5,23},{6,20},{7,21},{8,26},{9,... | collective-permute-start | bytes 1327112 | tf_op jit(solution)/shard_map/ppermute | solution.py:59
  46.6 23.1 %collective-permute-start.9 = (bf16[4,3,48,384]{3,2,1,0:T(8,128)(2,1)S(1)}, bf16[4,3,48,384]{3,2,1,0:T(8,128)(2,1)S(1)}, u32[]{:S(2)}, u32[]{:S(2)}) collective-permute-start(bf16[4,3,48,384]{3,2,1,0:T(8,128)(2,1)S(1)} %get-tuple-element.225), channel_id=1, source_target_pairs={{0,2},{1,3},{2,0},{3,1},{4,6},{5,7},{6,4},{7,5},{8,10},{9,11},{10,... | collective-permute-start | bytes 1327112 | tf_op jit(solution)/shard_map/ppermute | solution.py:49
  47.2 7.6 %collective-permute-start.12 = (bf16[4,48,384]{2,1,0:T(8,128)(2,1)S(1)}, bf16[4,48,384]{2,1,0:T(8,128)(2,1)S(1)}, u32[]{:S(2)}, u32[]{:S(2)}) collective-permute-start(bf16[4,48,384]{2,1,0:T(8,128)(2,1)S(1)} %constant_dynamic-slice_fusion), channel_id=1, source_target_pairs={{0,4},{1,5},{2,6},{3,7},{4,0},{5,1},{6,2},{7,3},{8,12},{9,13},{10,... | collective-permute-start | bytes 442376 | tf_op jit(solution)/shard_map/ppermute | solution.py:52
  49.5 17.4 %collective-permute-start.13 = (bf16[4,48,384]{2,1,0:T(8,128)(2,1)S(1)}, bf16[4,48,384]{2,1,0:T(8,128)(2,1)S(1)}, u32[]{:S(2)}, u32[]{:S(2)}) collective-permute-start(bf16[4,48,384]{2,1,0:T(8,128)(2,1)S(1)} %constant_dynamic-slice_fusion), channel_id=1, source_target_pairs={{0,8},{1,9},{2,10},{3,11},{4,12},{5,13},{6,14},{7,15},{8,0},{9,1},... | collective-permute-start | bytes 442376 | tf_op jit(solution)/shard_map/ppermute | solution.py:52
  54.7 12.2 %collective-permute-start.14 = (bf16[4,48,384]{2,1,0:T(8,128)(2,1)S(1)}, bf16[4,48,384]{2,1,0:T(8,128)(2,1)S(1)}, u32[]{:S(2)}, u32[]{:S(2)}) collective-permute-start(bf16[4,48,384]{2,1,0:T(8,128)(2,1)S(1)} %constant_dynamic-slice_fusion), channel_id=1, source_target_pairs={{0,12},{1,13},{2,14},{3,15},{4,8},{5,9},{6,10},{7,11},{8,4},{9,5},... | collective-permute-start | bytes 442376 | tf_op jit(solution)/shard_map/ppermute | solution.py:52
  70.2 3.8 %copy-start = (bf16[4,4,3,48,384]{4,3,2,1,0:T(8,128)(2,1)}, bf16[4,4,3,48,384]{4,3,2,1,0:T(8,128)(2,1)S(1)}, u32[]{:S(2)}) copy-start(bf16[4,4,3,48,384]{4,3,2,1,0:T(8,128)(2,1)S(1)} %pad_maximum_fusion.1.refs_0_) | copy-start | bytes 5308420
  70.2 3.8 %collective-permute-start.17 = (bf16[4,4,3,48,384]{4,3,2,1,0:T(8,128)(2,1)S(1)}, bf16[4,4,3,48,384]{4,3,2,1,0:T(8,128)(2,1)S(1)}, u32[]{:S(2)}, u32[]{:S(2)}) collective-permute-start(bf16[4,4,3,48,384]{4,3,2,1,0:T(8,128)(2,1)S(1)} %pad_maximum_fusion.1.refs_0_), channel_id=1, source_target_pairs={{0,1},{1,0},{2,3},{3,2},{4,5},{5,4},{6,7},{7,6},{8,9},{9,8},{10,11... | collective-permute-start | bytes 5308424 | tf_op jit(solution)/shard_map/ppermute | solution.py:46
  70.2 20.9 %collective-permute-start.15 = (bf16[4,4,48,384]{3,2,1,0:T(8,128)(2,1)S(1)}, bf16[4,4,48,384]{3,2,1,0:T(8,128)(2,1)S(1)}, u32[]{:S(2)}, u32[]{:S(2)}) collective-permute-start(bf16[4,4,48,384]{3,2,1,0:T(8,128)(2,1)S(1)} %get-tuple-element.250), channel_id=1, source_target_pairs={{0,2},{1,3},{2,0},{3,1},{4,6},{5,7},{6,4},{7,5},{8,10},{9,11},{10,... | collective-permute-start | bytes 1769480 | tf_op jit(solution)/shard_map/ppermute | solution.py:49
  71.8 19.3 %collective-permute-start.16 = (bf16[4,4,48,384]{3,2,1,0:T(8,128)(2,1)S(1)}, bf16[4,4,48,384]{3,2,1,0:T(8,128)(2,1)S(1)}, u32[]{:S(2)}, u32[]{:S(2)}) collective-permute-start(bf16[4,4,48,384]{3,2,1,0:T(8,128)(2,1)S(1)} %get-tuple-element.250), channel_id=1, source_target_pairs={{0,16},{16,0},{1,17},{17,1},{2,18},{18,2},{3,19},{19,3},{4,20},{20... | collective-permute-start | bytes 1769480 | tf_op jit(solution)/shard_map/ppermute | solution.py:55
  73.9 1.2 copy-start.2
  91.2 10.7 %collective-permute-start.18 = (bf16[2,4,48,384]{3,2,1,0:T(8,128)(2,1)S(1)}, bf16[2,4,48,384]{3,2,1,0:T(8,128)(2,1)S(1)}, u32[]{:S(2)}, u32[]{:S(2)}) collective-permute-start(bf16[2,4,48,384]{3,2,1,0:T(8,128)(2,1)S(1)} %slice.124), channel_id=1, source_target_pairs={{0,16},{16,0},{1,17},{17,1},{2,18},{18,2},{3,19},{19,3},{4,20},{20... | collective-permute-start | bytes 884744 | tf_op jit(solution)/shard_map/ppermute | solution.py:55
  92.7 12.3 %collective-permute-start.19 = (bf16[2,4,48,384]{3,2,1,0:T(8,128)(2,1)S(1)}, bf16[2,4,48,384]{3,2,1,0:T(8,128)(2,1)S(1)}, u32[]{:S(2)}, u32[]{:S(2)}) collective-permute-start(bf16[2,4,48,384]{3,2,1,0:T(8,128)(2,1)S(1)} %slice.125), channel_id=1, source_target_pairs={{0,2},{1,3},{2,0},{3,1},{4,6},{5,7},{6,4},{7,5},{8,10},{9,11},{10,... | collective-permute-start | bytes 884744 | tf_op jit(solution)/shard_map/ppermute | solution.py:49
  105.4 4.6 %copy-start.1 = (bf16[4,4,4,48,384]{4,3,2,1,0:T(8,128)(2,1)}, bf16[4,4,4,48,384]{4,3,2,1,0:T(8,128)(2,1)S(1)}, u32[]{:S(2)}) copy-start(bf16[4,4,4,48,384]{4,3,2,1,0:T(8,128)(2,1)S(1)} %pad_maximum_fusion.refs_0_) | copy-start | bytes 7077892
  105.4 4.6 %collective-permute-start.20 = (bf16[4,4,4,48,384]{4,3,2,1,0:T(8,128)(2,1)S(1)}, bf16[4,4,4,48,384]{4,3,2,1,0:T(8,128)(2,1)S(1)}, u32[]{:S(2)}, u32[]{:S(2)}) collective-permute-start(bf16[4,4,4,48,384]{4,3,2,1,0:T(8,128)(2,1)S(1)} %pad_maximum_fusion.refs_0_), channel_id=1, source_target_pairs={{0,1},{1,0},{2,3},{3,2},{4,5},{5,4},{6,7},{7,6},{8,9},{9,8},{10,11... | collective-permute-start | bytes 7077896 | tf_op jit(solution)/shard_map/ppermute | solution.py:46
  110.0 1.5 copy-start.7
  173.4 11.7 %collective-permute-start.21 = (bf16[2,2,4,4,48,384]{5,4,3,2,1,0:T(8,128)(2,1)}, bf16[2,2,4,4,48,384]{5,4,3,2,1,0:T(8,128)(2,1)S(1)}, u32[]{:S(2)}, u32[]{:S(2)}) collective-permute-start(bf16[2,2,4,4,48,384]{5,4,3,2,1,0:T(8,128)(2,1)} %get-tuple-element.295), channel_id=1, source_target_pairs={{0,1},{1,0},{2,3},{3,2},{4,5},{5,4},{6,7},{7,6},{8,9},{9,8},{10,11... | collective-permute-start | bytes 7077896 | tf_op jit(solution)/shard_map/ppermute | solution.py:46
  173.4 11.6 %copy-start.5 = (bf16[2,2,4,4,48,384]{5,4,3,2,1,0:T(8,128)(2,1)S(1)}, bf16[2,2,4,4,48,384]{5,4,3,2,1,0:T(8,128)(2,1)}, u32[]{:S(2)}) copy-start(bf16[2,2,4,4,48,384]{5,4,3,2,1,0:T(8,128)(2,1)} %get-tuple-element.294) | copy-start | bytes 7077892
  185.1 1.4 copy-start.6
  186.5 32.3 %collective-permute-start.22 = (bf16[4,4,48,384]{3,2,1,0:T(8,128)(2,1)S(1)}, bf16[4,4,48,384]{3,2,1,0:T(8,128)(2,1)S(1)}, u32[]{:S(2)}, u32[]{:S(2)}) collective-permute-start(bf16[4,4,48,384]{3,2,1,0:T(8,128)(2,1)S(1)} %get-tuple-element.299), channel_id=1, source_target_pairs={{0,2},{1,3},{2,0},{3,1},{4,6},{5,7},{6,4},{7,5},{8,10},{9,11},{10,... | collective-permute-start | bytes 1769480 | tf_op jit(solution)/shard_map/ppermute | solution.py:49
  188.1 30.7 %collective-permute-start.23 = (bf16[4,4,48,384]{3,2,1,0:T(8,128)(2,1)S(1)}, bf16[4,4,48,384]{3,2,1,0:T(8,128)(2,1)}, u32[]{:S(2)}, u32[]{:S(2)}) collective-permute-start(bf16[4,4,48,384]{3,2,1,0:T(8,128)(2,1)S(1)} %get-tuple-element.300), channel_id=1, source_target_pairs={{0,16},{16,0},{1,17},{17,1},{2,18},{18,2},{3,19},{19,3},{4,20},{20... | collective-permute-start | bytes 1769480 | tf_op jit(solution)/shard_map/ppermute | solution.py:55
  189.8 29.3 %collective-permute-start.24 = (bf16[4,4,48,384]{3,2,1,0:T(8,128)(2,1)S(1)}, bf16[4,4,48,384]{3,2,1,0:T(8,128)(2,1)}, u32[]{:S(2)}, u32[]{:S(2)}) collective-permute-start(bf16[4,4,48,384]{3,2,1,0:T(8,128)(2,1)S(1)} %get-tuple-element.301), channel_id=1, source_target_pairs={{0,18},{1,19},{2,16},{3,17},{4,22},{5,23},{6,20},{7,21},{8,26},{9,... | collective-permute-start | bytes 1769480 | tf_op jit(solution)/shard_map/ppermute | solution.py:59
  222.6 17.6 %collective-permute-start.25 = (bf16[2,2,4,4,48,384]{5,4,3,2,1,0:T(8,128)(2,1)}, bf16[2,2,4,4,48,384]{5,4,3,2,1,0:T(8,128)(2,1)S(1)}, u32[]{:S(2)}, u32[]{:S(2)}) collective-permute-start(bf16[2,2,4,4,48,384]{5,4,3,2,1,0:T(8,128)(2,1)} %get-tuple-element.317), channel_id=1, source_target_pairs={{0,1},{1,0},{2,3},{3,2},{4,5},{5,4},{6,7},{7,6},{8,9},{9,8},{10,11... | collective-permute-start | bytes 7077896 | tf_op jit(solution)/shard_map/ppermute | solution.py:46
  222.6 17.6 %collective-permute-start.26 = (bf16[4,48,768]{2,1,0:T(8,128)(2,1)}, bf16[4,48,768]{2,1,0:T(8,128)(2,1)S(1)}, u32[]{:S(2)}, u32[]{:S(2)}) collective-permute-start(bf16[4,48,768]{2,1,0:T(8,128)(2,1)} %reduce-scatter.2.cloned.1.call-done.refs_0_), channel_id=1, source_target_pairs={{0,16},{16,0},{1,17},{17,1},{2,18},{18,2},{3,19},{19,3},{4,20},{20... | collective-permute-start | bytes 884744 | tf_op jit(solution)/shard_map/ppermute | solution.py:55
  237.3 2.9 copy-start.3
  240.2 1.5 copy-start.14
  240.2 2.1 copy-start.4
  240.2 6.8 %copy-start.15 = (f32[32,16,48]{2,1,0:T(8,128)S(1)}, f32[32,16,48]{2,1,0:T(8,128)}, u32[]{:S(2)}) copy-start(f32[32,16,48]{2,1,0:T(8,128)} %get-tuple-element.337) | copy-start | bytes 294916
  242.2 31.3 %collective-permute-start.27 = (bf16[4,4,48,384]{3,2,1,0:T(8,128)(2,1)}, bf16[4,4,48,384]{3,2,1,0:T(8,128)(2,1)}, u32[]{:S(2)}, u32[]{:S(2)}) collective-permute-start(bf16[4,4,48,384]{3,2,1,0:T(8,128)(2,1)} %get-tuple-element.331), channel_id=1, source_target_pairs={{0,2},{1,3},{2,0},{3,1},{4,6},{5,7},{6,4},{7,5},{8,10},{9,11},{10,... | collective-permute-start | bytes 1769480 | tf_op jit(solution)/shard_map/ppermute | solution.py:49
  242.8 30.7 %collective-permute-start.28 = (bf16[4,4,48,384]{3,2,1,0:T(8,128)(2,1)}, bf16[4,4,48,384]{3,2,1,0:T(8,128)(2,1)}, u32[]{:S(2)}, u32[]{:S(2)}) collective-permute-start(bf16[4,4,48,384]{3,2,1,0:T(8,128)(2,1)} %get-tuple-element.332), channel_id=1, source_target_pairs={{0,16},{16,0},{1,17},{17,1},{2,18},{18,2},{3,19},{19,3},{4,20},{20... | collective-permute-start | bytes 1769480 | tf_op jit(solution)/shard_map/ppermute | solution.py:55
  243.3 30.2 %collective-permute-start.29 = (bf16[4,4,48,384]{3,2,1,0:T(8,128)(2,1)}, bf16[4,4,48,384]{3,2,1,0:T(8,128)(2,1)}, u32[]{:S(2)}, u32[]{:S(2)}) collective-permute-start(bf16[4,4,48,384]{3,2,1,0:T(8,128)(2,1)} %get-tuple-element.333), channel_id=1, source_target_pairs={{0,18},{1,19},{2,16},{3,17},{4,22},{5,23},{6,20},{7,21},{8,26},{9,... | collective-permute-start | bytes 1769480 | tf_op jit(solution)/shard_map/ppermute | solution.py:59
  245.7 8.7 %collective-permute-start.30 = (bf16[4,48,384]{2,1,0:T(8,128)(2,1)S(1)}, bf16[4,48,384]{2,1,0:T(8,128)(2,1)}, u32[]{:S(2)}, u32[]{:S(2)}) collective-permute-start(bf16[4,48,384]{2,1,0:T(8,128)(2,1)S(1)} %get-tuple-element.334), channel_id=1, source_target_pairs={{0,4},{1,5},{2,6},{3,7},{4,0},{5,1},{6,2},{7,3},{8,12},{9,13},{10,... | collective-permute-start | bytes 442376 | tf_op jit(solution)/shard_map/ppermute | solution.py:52
  247.9 24.0 %all-to-all-start = ((f32[32,1,768]{2,1,0:T(1,128)}), f32[32,1,768]{2,1,0:T(1,128)S(1)}, u32[]{:S(2)}, u32[]{:S(2)}) async-start(f32[32,1,768]{2,1,0:T(1,128)} %reshape.96), calls=%async_computation.1 | async-start | bytes 196608 | tf_op jit(solution)/shard_map/all_to_all | solution.py:988
  251.7 21.8 %collective-permute-start.31 = (bf16[4,48,384]{2,1,0:T(8,128)(2,1)}, bf16[4,48,384]{2,1,0:T(8,128)(2,1)}, u32[]{:S(2)}, u32[]{:S(2)}) collective-permute-start(bf16[4,48,384]{2,1,0:T(8,128)(2,1)} %get-tuple-element.335), channel_id=1, source_target_pairs={{0,8},{1,9},{2,10},{3,11},{4,12},{5,13},{6,14},{7,15},{8,0},{9,1},... | collective-permute-start | bytes 442376 | tf_op jit(solution)/shard_map/ppermute | solution.py:52
  254.4 19.1 %collective-permute-start.32 = (bf16[4,48,384]{2,1,0:T(8,128)(2,1)S(1)}, bf16[4,48,384]{2,1,0:T(8,128)(2,1)}, u32[]{:S(2)}, u32[]{:S(2)}) collective-permute-start(bf16[4,48,384]{2,1,0:T(8,128)(2,1)S(1)} %get-tuple-element.336), channel_id=1, source_target_pairs={{0,12},{1,13},{2,14},{3,15},{4,8},{5,9},{6,10},{7,11},{8,4},{9,5},... | collective-permute-start | bytes 442376 | tf_op jit(solution)/shard_map/ppermute | solution.py:52
  276.7 22.6 %copy-start.8 = (bf16[4,48,384]{2,1,0:T(8,128)(2,1)}, bf16[4,48,384]{2,1,0:T(8,128)(2,1)S(1)}, u32[]{:S(2)}) copy-start(bf16[4,48,384]{2,1,0:T(8,128)(2,1)S(1)} %fusion.14.refs_2_) | copy-start | bytes 442372
  276.7 8.5 %collective-permute-start.33 = (bf16[4,48,384]{2,1,0:T(8,128)(2,1)S(1)}, bf16[4,48,384]{2,1,0:T(8,128)(2,1)S(1)}, u32[]{:S(2)}, u32[]{:S(2)}) collective-permute-start(bf16[4,48,384]{2,1,0:T(8,128)(2,1)S(1)} %get-tuple-element.345), channel_id=1, source_target_pairs={{0,4},{1,5},{2,6},{3,7},{4,0},{5,1},{6,2},{7,3},{8,12},{9,13},{10,... | collective-permute-start | bytes 442376 | tf_op jit(solution)/shard_map/ppermute | solution.py:52
  278.8 14.0 %collective-permute-start.34 = (bf16[4,48,384]{2,1,0:T(8,128)(2,1)S(1)}, bf16[4,48,384]{2,1,0:T(8,128)(2,1)S(1)}, u32[]{:S(2)}, u32[]{:S(2)}) collective-permute-start(bf16[4,48,384]{2,1,0:T(8,128)(2,1)S(1)} %get-tuple-element.346), channel_id=1, source_target_pairs={{0,8},{1,9},{2,10},{3,11},{4,12},{5,13},{6,14},{7,15},{8,0},{9,1},... | collective-permute-start | bytes 442376 | tf_op jit(solution)/shard_map/ppermute | solution.py:52
  279.8 13.0 %collective-permute-start.35 = (bf16[4,48,384]{2,1,0:T(8,128)(2,1)S(1)}, bf16[4,48,384]{2,1,0:T(8,128)(2,1)S(1)}, u32[]{:S(2)}, u32[]{:S(2)}) collective-permute-start(bf16[4,48,384]{2,1,0:T(8,128)(2,1)S(1)} %get-tuple-element.347), channel_id=1, source_target_pairs={{0,12},{1,13},{2,14},{3,15},{4,8},{5,9},{6,10},{7,11},{8,4},{9,5},... | collective-permute-start | bytes 442376 | tf_op jit(solution)/shard_map/ppermute | solution.py:52
  281.3 11.5 %collective-permute-start.36 = (bf16[4,48,384]{2,1,0:T(8,128)(2,1)S(1)}, bf16[4,48,384]{2,1,0:T(8,128)(2,1)S(1)}, u32[]{:S(2)}, u32[]{:S(2)}) collective-permute-start(bf16[4,48,384]{2,1,0:T(8,128)(2,1)S(1)} %fusion.14.refs_2_), channel_id=1, source_target_pairs={{0,16},{16,0},{1,17},{17,1},{2,18},{18,2},{3,19},{19,3},{4,20},{20... | collective-permute-start | bytes 442376 | tf_op jit(solution)/shard_map/ppermute | solution.py:55
  292.8 6.6 %copy-start.17 = (bf16[4,48,384]{2,1,0:T(8,128)(2,1)}, bf16[4,48,384]{2,1,0:T(8,128)(2,1)S(1)}, u32[]{:S(2)}) copy-start(bf16[4,48,384]{2,1,0:T(8,128)(2,1)S(1)} %collective-permute-done.36.refs_3_) | copy-start | bytes 442372
  292.9 6.5 %copy-start.9 = (bf16[4,48,384]{2,1,0:T(8,128)(2,1)}, bf16[4,48,384]{2,1,0:T(8,128)(2,1)S(1)}, u32[]{:S(2)}) copy-start(bf16[4,48,384]{2,1,0:T(8,128)(2,1)S(1)} %fusion.17.refs_4_) | copy-start | bytes 442372
  292.9 5.2 %collective-permute-start.37 = (bf16[4,48,384]{2,1,0:T(8,128)(2,1)S(1)}, bf16[4,48,384]{2,1,0:T(8,128)(2,1)S(1)}, u32[]{:S(2)}, u32[]{:S(2)}) collective-permute-start(bf16[4,48,384]{2,1,0:T(8,128)(2,1)S(1)} %fusion.17.refs_4_), channel_id=1, source_target_pairs={{0,16},{16,0},{1,17},{17,1},{2,18},{18,2},{3,19},{19,3},{4,20},{20... | collective-permute-start | bytes 442376 | tf_op jit(solution)/shard_map/ppermute | solution.py:55
  298.1 1.3 copy-start.18
Sparse Core Ops, SparseCore 0:
  43.2 71.0 all-gather.1
  140.4 82.1 reduce-scatter.1

commit v2 on v1

--- a/solution.py
+++ b/solution.py
@@ -574,8 +574,8 @@
             gn_o[...] = jnp.zeros_like(gn_o)
 
     bias = vec[pl.ds(9 + block + j, 1), :]
-    step = rows.pad
-    for b in range(rows.images):
+    step = 3 * rows.pad
+    for b in range(rows.images // 3):
         at = pl.ds(b * step, step)
         z = dot(norm[at, :], w_up[...]) + bias
         up = dot_cols(grad[at, :], w_down[...])

time: 314 us -> 312 us (level)
  no operation moved by 1% of the time
where the time goes in v2:
time: 312 us; the launch traced here: 308 us
  Pallas kernels  159 us (51%)
  waiting for transfers between devices  62.8 us (20%)
  starting transfers between devices  50.7 us (16%)
  between operations  14.8 us (5%)
  local copies, waits for them, and re-layouts  10.4 us (3%)
  other arithmetic  10.3 us (3%)
    pallas_call x2, Pallas kernels, feed_call(): pl.pallas_call(functools.partial(feed_kernel, place, weight.kind, form, l...  60.3 us
    pallas_call x1, Pallas kernels, attend_back_call(): pl.pallas_call(functools.partial(attend_back_kernel, place, kind, rows, m...  28.9 us
    ppermute x15, starting transfers between devices, along_z(): return lambda v: lax.ppermute(v, 'fsdp', self.swap(4 * d))  24 us
    pallas_call x2, Pallas kernels, attend_call(): pl.pallas_call(functools.partial(attend_kernel, place, weight.kind, len(w...  21.9 us
    ppermute x15, waiting for transfers between devices, along_z(): return lambda v: lax.ppermute(v, 'fsdp', self.swap(4 * d))  19 us
    all_to_all x1, waiting for transfers between devices, local(): late = lax.all_to_all(late, ('rep', 'fsdp'), 0, 0, tiled=True)  16.8 us
    pallas_call x1, Pallas kernels, last_call(): pl.pallas_call(functools.partial(last_kernel, rows, [d.shape[0] for d in...  13.3 us
    pallas_call x1, Pallas kernels, middle_call(): pl.pallas_call(kernel, grid=(rows.images // PAIR,), in_specs=[block] * 4...  12 us
  transfers between devices with their start and end apart: 41, of which 16 were waited for; matrix products, arithmetic and copies ran while one was open for 3% of the time, Pallas kernels for 50%

profile of v2, /device:TPU:0, one launch (start us, length us, event | category | flops | bytes accessed | tf_op | source)
XLA Modules:
  0.0 307.8 jit_solution(15782581254295316084)
XLA Ops:
  7.2 1.2 broadcast_in_dim.39.refs_9_
  8.4 2.5 pack.1
  10.9 3.1 collective-permute-start
  14.0 2.6 collective-permute-start.1
  16.6 5.2 %pad_rows.1 = (bf16[1248,768]{1,0:T(8,128)(2,1)}, bf16[1248,768]{1,0:T(8,128)(2,1)}) custom-call(bf16[1176,768]{1,0:T(8,128)(2,1)} %tokens, bf16[1176,768]{1,0:T(8,128)(2,1)} %grads), custom_call_target="tpu_custom_call" | custom-call | flops 57500000 | bytes 150000 | tf_op jit(solution)/shard_map/pad_rows/pallas_call | solution.py:327
  21.8 2.8 collective-permute-done.1
  24.6 0.8 fusion.18
  25.4 1.5 collective-permute-start.3
  26.9 1.6 collective-permute-start.6
  28.6 1.4 collective-permute-start.7
  30.0 1.4 collective-permute-start.8
  31.3 3.1 %collective-permute-done.3 = bf16[4,1,64,768]{3,2,0,1:T(8,128)(2,1)S(1)} collective-permute-done((bf16[4,1,64,768]{3,2,0,1:T(8,128)(2,1)S(1)}, bf16[4,1,64,768]{3,2,0,1:T(8,128)(2,1)S(1)}, u32[]{:S(2)}, u32[]{:S(2)}) %collective-permute-start.3) | collective-permute-done | bytes 393248 | tf_op jit(solution)/shard_map/ppermute | solution.py:49
  34.5 1.7 collective-permute-done.5.refs_3_
  37.1 0.8 reshape.93.vec
  37.9 5.1 %norm_one.1 = (bf16[1248,768]{1,0:T(8,128)(2,1)}, bf16[1248,768]{1,0:T(8,128)(2,1)}) custom-call(bf16[1248,768]{1,0:T(8,128)(2,1)} %get-tuple-element.212.tokens, s32[6,196]{1,0:T(8,128)} %flags.3, f32[16,768]{1,0:T(8,128)} %reshape.93.vec), custom_call_target="tpu_custom_call" | custom-call | flops 57500000 | bytes 150000 | tf_op jit(solution)/shard_map/norm_one/pallas_call | solution.py:341
  43.6 1.6 collective-permute-start.10
  45.2 1.4 collective-permute-start.11
  47.2 2.4 collective-permute-start.12
  49.5 1.0 collective-permute-start.13
  50.5 4.2 %collective-permute-done.12 = bf16[4,48,384]{2,1,0:T(8,128)(2,1)S(1)} collective-permute-done((bf16[4,48,384]{2,1,0:T(8,128)(2,1)S(1)}, bf16[4,48,384]{2,1,0:T(8,128)(2,1)S(1)}, u32[]{:S(2)}, u32[]{:S(2)}) %collective-permute-start.12) | collective-permute-done | bytes 147488 | tf_op jit(solution)/shard_map/ppermute | solution.py:52
  54.7 1.5 collective-permute-start.14
  56.3 8.5 %attend.2 = (bf16[3,1248,256]{2,1,0:T(8,128)(2,1)}, bf16[3,1248,256]{2,1,0:T(8,128)(2,1)}, bf16[3,1248,256]{2,1,0:T(8,128)(2,1)}, bf16[3,1248,256]{2,1,0:T(8,128...) custom-call(bf16[1248,768]{1,0:T(8,128)(2,1)} %get-tuple-element.259.norm, ...), custom_call_target="tpu_custom_call" | custom-call | flops 92000000 | bytes 240000 | tf_op jit(solution)/shard_map/attend/pallas_call | solution.py:493
  64.8 2.2 collective-permute-done.13
  66.9 2.8 collective-permute-done.9
  70.2 1.6 collective-permute-start.15
  71.8 1.5 collective-permute-start.16
  73.9 1.2 copy-done.2
  75.1 13.4 %attend.3 = (bf16[3,1248,256]{2,1,0:T(8,128)(2,1)}, bf16[3,1248,256]{2,1,0:T(8,128)(2,1)}, bf16[3,1248,256]{2,1,0:T(8,128)(2,1)}, bf16[3,1248,256]{2,1,0:T(8,128...) custom-call(bf16[1248,768]{1,0:T(8,128)(2,1)} %get-tuple-element.259, ...), custom_call_target="tpu_custom_call", output_to_operand_aliasing={{0}: (4, {}), {1}: (5, {}), {2}: (6, {}), {3}: (7, {}), {4}... | custom-call | flops 161000000 | bytes 420000 | tf_op jit(solution)/shard_map/attend/pallas_call | solution.py:493
  88.5 2.6 collective-permute-done.15
  91.2 1.4 collective-permute-start.18
  92.7 2.4 collective-permute-start.19
  95.1 6.8 %project.1 = (f32[1248,768]{1,0:T(8,128)}, bf16[1248,768]{1,0:T(8,128)(2,1)}, bf16[1,768,768]{2,1,0:T(8,128)(2,1)}) custom-call(f32[16,768]{1,0:T(8,128)} %reshape.93.vec, bf16[1248,768]{1,0:T(8,128)(2,1)} %get-tuple-element.213.base, bf16[3,1248,256]{2,1,0:T(8,128)(2,1)} %get-tuple-element.271.att.refs_5_, bf16[4,4,3,48,384]{4,3,2,1,0:T(8,128)(2,1)} %copy-done, ...), custom_call_target="tpu_custom_call" | custom-call | flops 80500000 | bytes 210000 | tf_op jit(solution)/shard_map/project/pallas_call | solution.py:537
  101.9 3.1 collective-permute-done.19
  105.5 4.5 %collective-permute-done.20.refs_1_ = bf16[4,4,4,48,384]{4,3,2,1,0:T(8,128)(2,1)S(1)} collective-permute-done((bf16[4,4,4,48,384]{4,3,2,1,0:T(8,128)(2,1)S(1)}, bf16[4,4,4,48,384]{4,3,2,1,0:T(8,128)(2,1)S(1)}, u32[]{:S(2)}, u32[]{:S(2)}) %collective-permute-start.20) | collective-permute-done | bytes 2359328 | tf_op jit(solution)/shard_map/ppermute | solution.py:46
  110.0 1.5 copy-done.7
  111.5 28.0 %feed.2 = (f32[1248,768]{1,0:T(8,128)}, f32[1248,768]{1,0:T(8,128)}, f32[2,1,768]{2,1,0:T(1,128)}, bf16[4,768,768]{2,1,0:T(8,128)(2,1)}) custom-call(bf16[1248,768]{1,0:T(8,128)(2,1)} %get-tuple-element.281.norm, bf16[1248,768]{1,0:T(8,128)(2,1)} %get-tuple-element.282.grad, f32[16,768]{1,0:T(8,128)} %reshape.93.vec, bf16[4,4,4,48,384]{4,3,2,1,0:T(8,128)(2,1)} %copy-done.1, ...), custom_call_target="tpu_custom_call" | custom-call | flops 345000000 | bytes 900000 | tf_op jit(solution)/shard_map/feed/pallas_call | solution.py:625
  139.5 32.3 %feed.3 = (f32[1248,768]{1,0:T(8,128)}, f32[1248,768]{1,0:T(8,128)}, f32[2,1,768]{2,1,0:T(1,128)}, bf16[2,2,4,4,48,384]{5,4,3,2,1,0:T(8,128)(2,1)}, bf16[2,2,4,4,48,384]{5,4,3,2,1,0:T(8,128)(2,1)}) custom-call(bf16[1248,768]{1,0:T(8,128)(2,1)} %get-tuple-element.281.norm, bf16[1248,768]{1,0:T(8,128)(2,1)} %get-tuple-element.282.grad, ...), custom_call_target="tpu_custom_call" | custom-call | flops 345000000 | bytes 900000 | tf_op jit(solution)/shard_map/feed/pallas_call | solution.py:625
  171.9 12.0 %middle.1 = (bf16[1176,768]{1,0:T(8,128)(2,1)}, bf16[1248,768]{1,0:T(8,128)(2,1)}, bf16[1248,768]{1,0:T(8,128)(2,1)}, f32[4,768]{1,0:T(4,128)}) custom-call(f32[1248,768]{1,0:T(8,128)} %get-tuple-element.272.resid, f32[1248,768]{1,0:T(8,128)} %get-tuple-element.290.acc, f32[1248,768]{1,0:T(8,128)} %get-tuple-element.291.gn, ...), custom_call_target="tpu_custom_call" | custom-call | flops 138000000 | bytes 360000 | tf_op jit(solution)/shard_map/middle/pallas_call | solution.py:688
  184.4 0.9 copy-done.6
  185.4 1.5 collective-permute-start.22
  186.9 1.9 collective-permute-start.23
  188.9 28.9 %attend_back.1 = (bf16[3,1248,768]{2,1,0:T(8,128)(2,1)}, f32[3,1,768]{2,1,0:T(1,128)}, bf16[2,2,4,4,48,384]{5,4,3,2,1,0:T(8,128)(2,1)}, bf16[2,2,4,4,48,384]{5,4,3,2,1,0:T(8,128)(2,1)}) custom-call(bf16[1248,768]{1,0:T(8,128)(2,1)} %get-tuple-element.259.norm, bf16[1248,768]{1,0:T(8,128)(2,1)} %get-tuple-element.302.da, ...), custom_call_target="tpu_custom_call" | custom-call | flops 379500000 | bytes 990000 | tf_op jit(solution)/shard_map/attend_back/pallas_call | solution.py:766
  218.0 3.8 %reduce-scatter.2.cloned.1.call-done.refs_0_ = bf16[4,48,768]{2,1,0:T(8,128)(2,1)} async-done(((bf16[4,768,768]{2,1,0:T(8,128)(2,1)}), bf16[4,48,768]{2,1,0:T(8,128)(2,1)}) %reduce-scatter.2.cloned.1.call-update) | async-done | bytes 294928 | tf_op jit(solution)/shard_map/reduce_scatter | solution.py:897
  221.8 1.4 collective-permute-start.26
  223.3 13.3 %last.1 = (f32[1176,768]{1,0:T(8,128)}, f32[32,16,48]{2,1,0:T(8,128)}) custom-call(bf16[1248,768]{1,0:T(8,128)(2,1)} %get-tuple-element.213.base, bf16[1248,768]{1,0:T(8,128)(2,1)} %get-tuple-element.307.refs_4_.low, s32[6,196]{1,0:T(8,128)} %flags.3, f32[16,768]{1,0:T(8,128)} %reshape.93.vec, bf16[3,768,768]{2,1,0:T(8,128)(2,1)} %get-tuple-element.319.w, ...), custom_call_target="tpu_custom_call" | custom-call | flops 17250000896 | bytes 45000000 | tf_op jit(solution)/shard_map/last/pallas_call | solution.py:848
  236.6 2.1 fusion.5
  239.5 1.5 fusion.11
  242.6 2.4 collective-permute-start.29
  245.4 0.9 reshape.96
  246.3 3.9 %all-to-all-start = ((f32[32,1,768]{2,1,0:T(1,128)}), f32[32,1,768]{2,1,0:T(1,128)S(1)}, u32[]{:S(2)}, u32[]{:S(2)}) async-start(f32[32,1,768]{2,1,0:T(1,128)} %reshape.96), calls=%async_computation.1 | async-start | bytes 196608 | tf_op jit(solution)/shard_map/all_to_all | solution.py:988
  250.2 2.7 collective-permute-start.31
  252.9 1.5 collective-permute-start.32
  254.4 16.8 %all-to-all-done = f32[32,1,768]{2,1,0:T(1,128)S(1)} async-done(((f32[32,1,768]{2,1,0:T(1,128)}), f32[32,1,768]{2,1,0:T(1,128)S(1)}, u32[]{:S(2)}, u32[]{:S(2)}) %all-to-all-start) | async-done | bytes 98336 | tf_op jit(solution)/shard_map/all_to_all | solution.py:988
  271.7 0.9 reduce
  272.8 2.0 fusion.2
  274.8 1.1 fusion.14.refs_2_
  275.9 1.4 collective-permute-start.33
  277.4 1.2 collective-permute-start.34
  278.5 1.9 collective-permute-start.35
  280.4 1.1 collective-permute-start.36
  281.5 2.8 collective-permute-done.33
  284.3 7.0 %collective-permute-done.34 = bf16[4,48,384]{2,1,0:T(8,128)(2,1)S(1)} collective-permute-done((bf16[4,48,384]{2,1,0:T(8,128)(2,1)S(1)}, bf16[4,48,384]{2,1,0:T(8,128)(2,1)S(1)}, u32[]{:S(2)}, u32[]{:S(2)}) %collective-permute-start.34) | collective-permute-done | bytes 147488 | tf_op jit(solution)/shard_map/ppermute | solution.py:52
  292.1 4.6 %collective-permute-done.37.refs_5_ = bf16[4,48,384]{2,1,0:T(8,128)(2,1)S(1)} collective-permute-done((bf16[4,48,384]{2,1,0:T(8,128)(2,1)S(1)}, bf16[4,48,384]{2,1,0:T(8,128)(2,1)S(1)}, u32[]{:S(2)}, u32[]{:S(2)}) %collective-permute-start.37) | collective-permute-done | bytes 147488 | tf_op jit(solution)/shard_map/ppermute | solution.py:55
  297.9 2.8 unpack.1
  (114 shorter events, 10.3 us)
Async XLA Ops:
  7.2 132.4 %all-gather.2.cloned.1.call-start = ((), (), s32[]{:S(2)}) async-start(), calls=%async_computation.2 | async-start | bytes 5013504 | tf_op jit(solution)/shard_map/all_gather | solution.py:894
  10.9 10.9 %copy-start.13 = (bf16[4,48,768]{2,1,0:T(8,128)(2,1)S(1)}, bf16[4,48,768]{2,1,0:T(8,128)(2,1)}, u32[]{:S(2)}) copy-start(bf16[4,48,768]{2,1,0:T(8,128)(2,1)} %get-tuple-element.201) | copy-start | bytes 884740
  10.9 10.9 %collective-permute-start = (bf16[1,64,768]{2,1,0:T(8,128)(2,1)}, bf16[1,64,768]{2,1,0:T(8,128)(2,1)S(1)}, u32[]{:S(2)}, u32[]{:S(2)}) collective-permute-start(bf16[1,64,768]{2,1,0:T(8,128)(2,1)} %get-tuple-element.193), channel_id=1, source_target_pairs={{0,4},{1,5},{2,6},{3,7},{4,0},{5,1},{6,2},{7,3},{8,12},{9,13},{10,... | collective-permute-start | bytes 294920 | tf_op jit(solution)/shard_map/ppermute | solution.py:52
  14.0 10.6 %collective-permute-start.1 = (bf16[1,64,768]{2,1,0:T(8,128)(2,1)}, bf16[1,64,768]{2,1,0:T(8,128)(2,1)S(1)}, u32[]{:S(2)}, u32[]{:S(2)}) collective-permute-start(bf16[1,64,768]{2,1,0:T(8,128)(2,1)} %get-tuple-element.193), channel_id=1, source_target_pairs={{0,8},{1,9},{2,10},{3,11},{4,12},{5,13},{6,14},{7,15},{8,0},{9,1},... | collective-permute-start | bytes 294920 | tf_op jit(solution)/shard_map/ppermute | solution.py:52
  16.6 8.1 %collective-permute-start.2 = (bf16[1,64,768]{2,1,0:T(8,128)(2,1)}, bf16[1,64,768]{2,1,0:T(8,128)(2,1)S(1)}, u32[]{:S(2)}, u32[]{:S(2)}) collective-permute-start(bf16[1,64,768]{2,1,0:T(8,128)(2,1)} %get-tuple-element.193), channel_id=1, source_target_pairs={{0,12},{1,13},{2,14},{3,15},{4,8},{5,9},{6,10},{7,11},{8,4},{9,5},... | collective-permute-start | bytes 294920 | tf_op jit(solution)/shard_map/ppermute | solution.py:52
  16.6 5.2 %copy-start.16 = (bf16[3,48,768]{2,1,0:T(8,128)(2,1)S(1)}, bf16[3,48,768]{2,1,0:T(8,128)(2,1)}, u32[]{:S(2)}) copy-start(bf16[3,48,768]{2,1,0:T(8,128)(2,1)} %get-tuple-element.200) | copy-start | bytes 663556
  16.6 8.1 %copy-start.19 = (bf16[1,64,768]{2,1,0:T(8,128)(2,1)S(1)}, bf16[1,64,768]{2,1,0:T(8,128)(2,1)}, u32[]{:S(2)}) copy-start(bf16[1,64,768]{2,1,0:T(8,128)(2,1)} %get-tuple-element.193) | copy-start | bytes 294916
  25.4 9.0 %collective-permute-start.3 = (bf16[4,1,64,768]{3,2,0,1:T(8,128)(2,1)S(1)}, bf16[4,1,64,768]{3,2,0,1:T(8,128)(2,1)S(1)}, u32[]{:S(2)}, u32[]{:S(2)}) collective-permute-start(bf16[4,1,64,768]{3,2,0,1:T(8,128)(2,1)S(1)} %get-tuple-element.204), channel_id=1, source_target_pairs={{0,2},{1,3},{2,0},{3,1},{4,6},{5,7},{6,4},{7,5},{8,10},{9,11},{10,... | collective-permute-start | bytes 1179656 | tf_op jit(solution)/shard_map/ppermute | solution.py:49
  26.9 7.5 %collective-permute-start.4 = (bf16[4,1,64,768]{3,2,0,1:T(8,128)(2,1)S(1)}, bf16[4,1,64,768]{3,2,0,1:T(8,128)(2,1)S(1)}, u32[]{:S(2)}, u32[]{:S(2)}) collective-permute-start(bf16[4,1,64,768]{3,2,0,1:T(8,128)(2,1)S(1)} %get-tuple-element.204), channel_id=1, source_target_pairs={{0,1},{1,0},{2,3},{3,2},{4,5},{5,4},{6,7},{7,6},{8,9},{9,8},{10,11... | collective-permute-start | bytes 1179656 | tf_op jit(solution)/shard_map/ppermute | solution.py:46
  26.9 16.1 %collective-permute-start.6 = (bf16[3,48,384]{2,1,0:T(8,128)(2,1)S(1)}, bf16[3,48,384]{2,1,0:T(8,128)(2,1)S(1)}, u32[]{:S(2)}, u32[]{:S(2)}) collective-permute-start(bf16[3,48,384]{2,1,0:T(8,128)(2,1)S(1)} %constant_dynamic-slice_fusion.1), channel_id=1, source_target_pairs={{0,4},{1,5},{2,6},{3,7},{4,0},{5,1},{6,2},{7,3},{8,12},{9,13},{10,... | collective-permute-start | bytes 331784 | tf_op jit(solution)/shard_map/ppermute | solution.py:52
  28.6 14.5 %collective-permute-start.7 = (bf16[3,48,384]{2,1,0:T(8,128)(2,1)S(1)}, bf16[3,48,384]{2,1,0:T(8,128)(2,1)S(1)}, u32[]{:S(2)}, u32[]{:S(2)}) collective-permute-start(bf16[3,48,384]{2,1,0:T(8,128)(2,1)S(1)} %constant_dynamic-slice_fusion.1), channel_id=1, source_target_pairs={{0,8},{1,9},{2,10},{3,11},{4,12},{5,13},{6,14},{7,15},{8,0},{9,1},... | collective-permute-start | bytes 331784 | tf_op jit(solution)/shard_map/ppermute | solution.py:52
  30.0 13.1 %collective-permute-start.8 = (bf16[3,48,384]{2,1,0:T(8,128)(2,1)S(1)}, bf16[3,48,384]{2,1,0:T(8,128)(2,1)S(1)}, u32[]{:S(2)}, u32[]{:S(2)}) collective-permute-start(bf16[3,48,384]{2,1,0:T(8,128)(2,1)S(1)} %constant_dynamic-slice_fusion.1), channel_id=1, source_target_pairs={{0,12},{1,13},{2,14},{3,15},{4,8},{5,9},{6,10},{7,11},{8,4},{9,5},... | collective-permute-start | bytes 331784 | tf_op jit(solution)/shard_map/ppermute | solution.py:52
  34.4 8.7 %copy-start.10 = (bf16[4,1,64,768]{3,2,0,1:T(8,128)(2,1)}, bf16[4,1,64,768]{3,2,0,1:T(8,128)(2,1)S(1)}, u32[]{:S(2)}) copy-start(bf16[4,1,64,768]{3,2,0,1:T(8,128)(2,1)S(1)} %collective-permute-done.3) | copy-start | bytes 1179652
  34.4 8.7 %copy-start.11 = (bf16[4,1,64,768]{3,2,0,1:T(8,128)(2,1)}, bf16[4,1,64,768]{3,2,0,1:T(8,128)(2,1)S(1)}, u32[]{:S(2)}) copy-start(bf16[4,1,64,768]{3,2,0,1:T(8,128)(2,1)S(1)} %collective-permute-done.4) | copy-start | bytes 1179652
  34.4 1.8 collective-permute-start.5
  36.2 6.9 %copy-start.12 = (bf16[4,1,64,768]{3,2,1,0:T(8,128)(2,1)}, bf16[4,1,64,768]{3,2,1,0:T(8,128)(2,1)S(1)}, u32[]{:S(2)}) copy-start(bf16[4,1,64,768]{3,2,1,0:T(8,128)(2,1)S(1)} %collective-permute-done.5.refs_3_) | copy-start | bytes 1179652
  43.1 178.7 %reduce-scatter.2.cloned.1.call-start = ((), (), s32[]{:S(2)}) async-start(), calls=%async_computation.3 | async-start | bytes 5013504 | tf_op jit(solution)/shard_map/reduce_scatter | solution.py:897
  43.6 23.3 %collective-permute-start.10 = (bf16[4,3,48,384]{3,2,1,0:T(8,128)(2,1)S(1)}, bf16[4,3,48,384]{3,2,1,0:T(8,128)(2,1)S(1)}, u32[]{:S(2)}, u32[]{:S(2)}) collective-permute-start(bf16[4,3,48,384]{3,2,1,0:T(8,128)(2,1)S(1)} %get-tuple-element.225), channel_id=1, source_target_pairs={{0,16},{16,0},{1,17},{17,1},{2,18},{18,2},{3,19},{19,3},{4,20},{20... | collective-permute-start | bytes 1327112 | tf_op jit(solution)/shard_map/ppermute | solution.py:55
  45.2 21.8 %collective-permute-start.11 = (bf16[4,3,48,384]{3,2,1,0:T(8,128)(2,1)S(1)}, bf16[4,3,48,384]{3,2,1,0:T(8,128)(2,1)S(1)}, u32[]{:S(2)}, u32[]{:S(2)}) collective-permute-start(bf16[4,3,48,384]{3,2,1,0:T(8,128)(2,1)S(1)} %get-tuple-element.225), channel_id=1, source_target_pairs={{0,18},{1,19},{2,16},{3,17},{4,22},{5,23},{6,20},{7,21},{8,26},{9,... | collective-permute-start | bytes 1327112 | tf_op jit(solution)/shard_map/ppermute | solution.py:59
  46.6 23.1 %collective-permute-start.9 = (bf16[4,3,48,384]{3,2,1,0:T(8,128)(2,1)S(1)}, bf16[4,3,48,384]{3,2,1,0:T(8,128)(2,1)S(1)}, u32[]{:S(2)}, u32[]{:S(2)}) collective-permute-start(bf16[4,3,48,384]{3,2,1,0:T(8,128)(2,1)S(1)} %get-tuple-element.225), channel_id=1, source_target_pairs={{0,2},{1,3},{2,0},{3,1},{4,6},{5,7},{6,4},{7,5},{8,10},{9,11},{10,... | collective-permute-start | bytes 1327112 | tf_op jit(solution)/shard_map/ppermute | solution.py:49
  47.2 7.6 %collective-permute-start.12 = (bf16[4,48,384]{2,1,0:T(8,128)(2,1)S(1)}, bf16[4,48,384]{2,1,0:T(8,128)(2,1)S(1)}, u32[]{:S(2)}, u32[]{:S(2)}) collective-permute-start(bf16[4,48,384]{2,1,0:T(8,128)(2,1)S(1)} %constant_dynamic-slice_fusion), channel_id=1, source_target_pairs={{0,4},{1,5},{2,6},{3,7},{4,0},{5,1},{6,2},{7,3},{8,12},{9,13},{10,... | collective-permute-start | bytes 442376 | tf_op jit(solution)/shard_map/ppermute | solution.py:52
  49.5 17.4 %collective-permute-start.13 = (bf16[4,48,384]{2,1,0:T(8,128)(2,1)S(1)}, bf16[4,48,384]{2,1,0:T(8,128)(2,1)S(1)}, u32[]{:S(2)}, u32[]{:S(2)}) collective-permute-start(bf16[4,48,384]{2,1,0:T(8,128)(2,1)S(1)} %constant_dynamic-slice_fusion), channel_id=1, source_target_pairs={{0,8},{1,9},{2,10},{3,11},{4,12},{5,13},{6,14},{7,15},{8,0},{9,1},... | collective-permute-start | bytes 442376 | tf_op jit(solution)/shard_map/ppermute | solution.py:52
  54.7 12.2 %collective-permute-start.14 = (bf16[4,48,384]{2,1,0:T(8,128)(2,1)S(1)}, bf16[4,48,384]{2,1,0:T(8,128)(2,1)S(1)}, u32[]{:S(2)}, u32[]{:S(2)}) collective-permute-start(bf16[4,48,384]{2,1,0:T(8,128)(2,1)S(1)} %constant_dynamic-slice_fusion), channel_id=1, source_target_pairs={{0,12},{1,13},{2,14},{3,15},{4,8},{5,9},{6,10},{7,11},{8,4},{9,5},... | collective-permute-start | bytes 442376 | tf_op jit(solution)/shard_map/ppermute | solution.py:52
  70.2 3.8 %copy-start = (bf16[4,4,3,48,384]{4,3,2,1,0:T(8,128)(2,1)}, bf16[4,4,3,48,384]{4,3,2,1,0:T(8,128)(2,1)S(1)}, u32[]{:S(2)}) copy-start(bf16[4,4,3,48,384]{4,3,2,1,0:T(8,128)(2,1)S(1)} %pad_maximum_fusion.1.refs_0_) | copy-start | bytes 5308420
  70.2 3.8 %collective-permute-start.17 = (bf16[4,4,3,48,384]{4,3,2,1,0:T(8,128)(2,1)S(1)}, bf16[4,4,3,48,384]{4,3,2,1,0:T(8,128)(2,1)S(1)}, u32[]{:S(2)}, u32[]{:S(2)}) collective-permute-start(bf16[4,4,3,48,384]{4,3,2,1,0:T(8,128)(2,1)S(1)} %pad_maximum_fusion.1.refs_0_), channel_id=1, source_target_pairs={{0,1},{1,0},{2,3},{3,2},{4,5},{5,4},{6,7},{7,6},{8,9},{9,8},{10,11... | collective-permute-start | bytes 5308424 | tf_op jit(solution)/shard_map/ppermute | solution.py:46
  70.2 20.9 %collective-permute-start.15 = (bf16[4,4,48,384]{3,2,1,0:T(8,128)(2,1)S(1)}, bf16[4,4,48,384]{3,2,1,0:T(8,128)(2,1)S(1)}, u32[]{:S(2)}, u32[]{:S(2)}) collective-permute-start(bf16[4,4,48,384]{3,2,1,0:T(8,128)(2,1)S(1)} %get-tuple-element.250), channel_id=1, source_target_pairs={{0,2},{1,3},{2,0},{3,1},{4,6},{5,7},{6,4},{7,5},{8,10},{9,11},{10,... | collective-permute-start | bytes 1769480 | tf_op jit(solution)/shard_map/ppermute | solution.py:49
  71.8 19.3 %collective-permute-start.16 = (bf16[4,4,48,384]{3,2,1,0:T(8,128)(2,1)S(1)}, bf16[4,4,48,384]{3,2,1,0:T(8,128)(2,1)S(1)}, u32[]{:S(2)}, u32[]{:S(2)}) collective-permute-start(bf16[4,4,48,384]{3,2,1,0:T(8,128)(2,1)S(1)} %get-tuple-element.250), channel_id=1, source_target_pairs={{0,16},{16,0},{1,17},{17,1},{2,18},{18,2},{3,19},{19,3},{4,20},{20... | collective-permute-start | bytes 1769480 | tf_op jit(solution)/shard_map/ppermute | solution.py:55
  73.9 1.2 copy-start.2
  91.2 10.7 %collective-permute-start.18 = (bf16[2,4,48,384]{3,2,1,0:T(8,128)(2,1)S(1)}, bf16[2,4,48,384]{3,2,1,0:T(8,128)(2,1)S(1)}, u32[]{:S(2)}, u32[]{:S(2)}) collective-permute-start(bf16[2,4,48,384]{3,2,1,0:T(8,128)(2,1)S(1)} %slice.124), channel_id=1, source_target_pairs={{0,16},{16,0},{1,17},{17,1},{2,18},{18,2},{3,19},{19,3},{4,20},{20... | collective-permute-start | bytes 884744 | tf_op jit(solution)/shard_map/ppermute | solution.py:55
  92.7 12.3 %collective-permute-start.19 = (bf16[2,4,48,384]{3,2,1,0:T(8,128)(2,1)S(1)}, bf16[2,4,48,384]{3,2,1,0:T(8,128)(2,1)S(1)}, u32[]{:S(2)}, u32[]{:S(2)}) collective-permute-start(bf16[2,4,48,384]{3,2,1,0:T(8,128)(2,1)S(1)} %slice.125), channel_id=1, source_target_pairs={{0,2},{1,3},{2,0},{3,1},{4,6},{5,7},{6,4},{7,5},{8,10},{9,11},{10,... | collective-permute-start | bytes 884744 | tf_op jit(solution)/shard_map/ppermute | solution.py:49
  105.4 4.6 %copy-start.1 = (bf16[4,4,4,48,384]{4,3,2,1,0:T(8,128)(2,1)}, bf16[4,4,4,48,384]{4,3,2,1,0:T(8,128)(2,1)S(1)}, u32[]{:S(2)}) copy-start(bf16[4,4,4,48,384]{4,3,2,1,0:T(8,128)(2,1)S(1)} %pad_maximum_fusion.refs_0_) | copy-start | bytes 7077892
  105.4 4.6 %collective-permute-start.20 = (bf16[4,4,4,48,384]{4,3,2,1,0:T(8,128)(2,1)S(1)}, bf16[4,4,4,48,384]{4,3,2,1,0:T(8,128)(2,1)S(1)}, u32[]{:S(2)}, u32[]{:S(2)}) collective-permute-start(bf16[4,4,4,48,384]{4,3,2,1,0:T(8,128)(2,1)S(1)} %pad_maximum_fusion.refs_0_), channel_id=1, source_target_pairs={{0,1},{1,0},{2,3},{3,2},{4,5},{5,4},{6,7},{7,6},{8,9},{9,8},{10,11... | collective-permute-start | bytes 7077896 | tf_op jit(solution)/shard_map/ppermute | solution.py:46
  110.0 1.5 copy-start.7
  171.8 12.1 %collective-permute-start.21 = (bf16[2,2,4,4,48,384]{5,4,3,2,1,0:T(8,128)(2,1)}, bf16[2,2,4,4,48,384]{5,4,3,2,1,0:T(8,128)(2,1)S(1)}, u32[]{:S(2)}, u32[]{:S(2)}) collective-permute-start(bf16[2,2,4,4,48,384]{5,4,3,2,1,0:T(8,128)(2,1)} %get-tuple-element.295), channel_id=1, source_target_pairs={{0,1},{1,0},{2,3},{3,2},{4,5},{5,4},{6,7},{7,6},{8,9},{9,8},{10,11... | collective-permute-start | bytes 7077896 | tf_op jit(solution)/shard_map/ppermute | solution.py:46
  171.9 12.0 %copy-start.5 = (bf16[2,2,4,4,48,384]{5,4,3,2,1,0:T(8,128)(2,1)S(1)}, bf16[2,2,4,4,48,384]{5,4,3,2,1,0:T(8,128)(2,1)}, u32[]{:S(2)}) copy-start(bf16[2,2,4,4,48,384]{5,4,3,2,1,0:T(8,128)(2,1)} %get-tuple-element.294) | copy-start | bytes 7077892
  183.9 1.4 copy-start.6
  185.4 32.4 %collective-permute-start.22 = (bf16[4,4,48,384]{3,2,1,0:T(8,128)(2,1)S(1)}, bf16[4,4,48,384]{3,2,1,0:T(8,128)(2,1)S(1)}, u32[]{:S(2)}, u32[]{:S(2)}) collective-permute-start(bf16[4,4,48,384]{3,2,1,0:T(8,128)(2,1)S(1)} %get-tuple-element.299), channel_id=1, source_target_pairs={{0,2},{1,3},{2,0},{3,1},{4,6},{5,7},{6,4},{7,5},{8,10},{9,11},{10,... | collective-permute-start | bytes 1769480 | tf_op jit(solution)/shard_map/ppermute | solution.py:49
  186.9 30.9 %collective-permute-start.23 = (bf16[4,4,48,384]{3,2,1,0:T(8,128)(2,1)S(1)}, bf16[4,4,48,384]{3,2,1,0:T(8,128)(2,1)}, u32[]{:S(2)}, u32[]{:S(2)}) collective-permute-start(bf16[4,4,48,384]{3,2,1,0:T(8,128)(2,1)S(1)} %get-tuple-element.300), channel_id=1, source_target_pairs={{0,16},{16,0},{1,17},{17,1},{2,18},{18,2},{3,19},{19,3},{4,20},{20... | collective-permute-start | bytes 1769480 | tf_op jit(solution)/shard_map/ppermute | solution.py:55
  188.7 29.3 %collective-permute-start.24 = (bf16[4,4,48,384]{3,2,1,0:T(8,128)(2,1)S(1)}, bf16[4,4,48,384]{3,2,1,0:T(8,128)(2,1)}, u32[]{:S(2)}, u32[]{:S(2)}) collective-permute-start(bf16[4,4,48,384]{3,2,1,0:T(8,128)(2,1)S(1)} %get-tuple-element.301), channel_id=1, source_target_pairs={{0,18},{1,19},{2,16},{3,17},{4,22},{5,23},{6,20},{7,21},{8,26},{9,... | collective-permute-start | bytes 1769480 | tf_op jit(solution)/shard_map/ppermute | solution.py:59
  221.8 17.6 %collective-permute-start.25 = (bf16[2,2,4,4,48,384]{5,4,3,2,1,0:T(8,128)(2,1)}, bf16[2,2,4,4,48,384]{5,4,3,2,1,0:T(8,128)(2,1)S(1)}, u32[]{:S(2)}, u32[]{:S(2)}) collective-permute-start(bf16[2,2,4,4,48,384]{5,4,3,2,1,0:T(8,128)(2,1)} %get-tuple-element.317), channel_id=1, source_target_pairs={{0,1},{1,0},{2,3},{3,2},{4,5},{5,4},{6,7},{7,6},{8,9},{9,8},{10,11... | collective-permute-start | bytes 7077896 | tf_op jit(solution)/shard_map/ppermute | solution.py:46
  221.8 17.6 %collective-permute-start.26 = (bf16[4,48,768]{2,1,0:T(8,128)(2,1)}, bf16[4,48,768]{2,1,0:T(8,128)(2,1)S(1)}, u32[]{:S(2)}, u32[]{:S(2)}) collective-permute-start(bf16[4,48,768]{2,1,0:T(8,128)(2,1)} %reduce-scatter.2.cloned.1.call-done.refs_0_), channel_id=1, source_target_pairs={{0,16},{16,0},{1,17},{17,1},{2,18},{18,2},{3,19},{19,3},{4,20},{20... | collective-permute-start | bytes 884744 | tf_op jit(solution)/shard_map/ppermute | solution.py:55
  236.6 2.9 copy-start.3
  239.4 1.5 copy-start.14
  239.4 2.1 copy-start.4
  239.5 6.0 %copy-start.15 = (f32[32,16,48]{2,1,0:T(8,128)S(1)}, f32[32,16,48]{2,1,0:T(8,128)}, u32[]{:S(2)}) copy-start(f32[32,16,48]{2,1,0:T(8,128)} %get-tuple-element.337) | copy-start | bytes 294916
  241.5 31.3 %collective-permute-start.27 = (bf16[4,4,48,384]{3,2,1,0:T(8,128)(2,1)}, bf16[4,4,48,384]{3,2,1,0:T(8,128)(2,1)}, u32[]{:S(2)}, u32[]{:S(2)}) collective-permute-start(bf16[4,4,48,384]{3,2,1,0:T(8,128)(2,1)} %get-tuple-element.331), channel_id=1, source_target_pairs={{0,2},{1,3},{2,0},{3,1},{4,6},{5,7},{6,4},{7,5},{8,10},{9,11},{10,... | collective-permute-start | bytes 1769480 | tf_op jit(solution)/shard_map/ppermute | solution.py:49
  242.1 30.7 %collective-permute-start.28 = (bf16[4,4,48,384]{3,2,1,0:T(8,128)(2,1)}, bf16[4,4,48,384]{3,2,1,0:T(8,128)(2,1)}, u32[]{:S(2)}, u32[]{:S(2)}) collective-permute-start(bf16[4,4,48,384]{3,2,1,0:T(8,128)(2,1)} %get-tuple-element.332), channel_id=1, source_target_pairs={{0,16},{16,0},{1,17},{17,1},{2,18},{18,2},{3,19},{19,3},{4,20},{20... | collective-permute-start | bytes 1769480 | tf_op jit(solution)/shard_map/ppermute | solution.py:55
  242.6 30.2 %collective-permute-start.29 = (bf16[4,4,48,384]{3,2,1,0:T(8,128)(2,1)}, bf16[4,4,48,384]{3,2,1,0:T(8,128)(2,1)}, u32[]{:S(2)}, u32[]{:S(2)}) collective-permute-start(bf16[4,4,48,384]{3,2,1,0:T(8,128)(2,1)} %get-tuple-element.333), channel_id=1, source_target_pairs={{0,18},{1,19},{2,16},{3,17},{4,22},{5,23},{6,20},{7,21},{8,26},{9,... | collective-permute-start | bytes 1769480 | tf_op jit(solution)/shard_map/ppermute | solution.py:59
  245.0 8.0 %collective-permute-start.30 = (bf16[4,48,384]{2,1,0:T(8,128)(2,1)S(1)}, bf16[4,48,384]{2,1,0:T(8,128)(2,1)}, u32[]{:S(2)}, u32[]{:S(2)}) collective-permute-start(bf16[4,48,384]{2,1,0:T(8,128)(2,1)S(1)} %get-tuple-element.334), channel_id=1, source_target_pairs={{0,4},{1,5},{2,6},{3,7},{4,0},{5,1},{6,2},{7,3},{8,12},{9,13},{10,... | collective-permute-start | bytes 442376 | tf_op jit(solution)/shard_map/ppermute | solution.py:52
  246.3 24.9 %all-to-all-start = ((f32[32,1,768]{2,1,0:T(1,128)}), f32[32,1,768]{2,1,0:T(1,128)S(1)}, u32[]{:S(2)}, u32[]{:S(2)}) async-start(f32[32,1,768]{2,1,0:T(1,128)} %reshape.96), calls=%async_computation.1 | async-start | bytes 196608 | tf_op jit(solution)/shard_map/all_to_all | solution.py:988
  250.2 22.5 %collective-permute-start.31 = (bf16[4,48,384]{2,1,0:T(8,128)(2,1)}, bf16[4,48,384]{2,1,0:T(8,128)(2,1)}, u32[]{:S(2)}, u32[]{:S(2)}) collective-permute-start(bf16[4,48,384]{2,1,0:T(8,128)(2,1)} %get-tuple-element.335), channel_id=1, source_target_pairs={{0,8},{1,9},{2,10},{3,11},{4,12},{5,13},{6,14},{7,15},{8,0},{9,1},... | collective-permute-start | bytes 442376 | tf_op jit(solution)/shard_map/ppermute | solution.py:52
  252.9 19.8 %collective-permute-start.32 = (bf16[4,48,384]{2,1,0:T(8,128)(2,1)S(1)}, bf16[4,48,384]{2,1,0:T(8,128)(2,1)}, u32[]{:S(2)}, u32[]{:S(2)}) collective-permute-start(bf16[4,48,384]{2,1,0:T(8,128)(2,1)S(1)} %get-tuple-element.336), channel_id=1, source_target_pairs={{0,12},{1,13},{2,14},{3,15},{4,8},{5,9},{6,10},{7,11},{8,4},{9,5},... | collective-permute-start | bytes 442376 | tf_op jit(solution)/shard_map/ppermute | solution.py:52
  275.9 21.9 %copy-start.8 = (bf16[4,48,384]{2,1,0:T(8,128)(2,1)}, bf16[4,48,384]{2,1,0:T(8,128)(2,1)S(1)}, u32[]{:S(2)}) copy-start(bf16[4,48,384]{2,1,0:T(8,128)(2,1)S(1)} %fusion.14.refs_2_) | copy-start | bytes 442372
  275.9 8.4 %collective-permute-start.33 = (bf16[4,48,384]{2,1,0:T(8,128)(2,1)S(1)}, bf16[4,48,384]{2,1,0:T(8,128)(2,1)S(1)}, u32[]{:S(2)}, u32[]{:S(2)}) collective-permute-start(bf16[4,48,384]{2,1,0:T(8,128)(2,1)S(1)} %get-tuple-element.345), channel_id=1, source_target_pairs={{0,4},{1,5},{2,6},{3,7},{4,0},{5,1},{6,2},{7,3},{8,12},{9,13},{10,... | collective-permute-start | bytes 442376 | tf_op jit(solution)/shard_map/ppermute | solution.py:52
  277.4 14.0 %collective-permute-start.34 = (bf16[4,48,384]{2,1,0:T(8,128)(2,1)S(1)}, bf16[4,48,384]{2,1,0:T(8,128)(2,1)S(1)}, u32[]{:S(2)}, u32[]{:S(2)}) collective-permute-start(bf16[4,48,384]{2,1,0:T(8,128)(2,1)S(1)} %get-tuple-element.346), channel_id=1, source_target_pairs={{0,8},{1,9},{2,10},{3,11},{4,12},{5,13},{6,14},{7,15},{8,0},{9,1},... | collective-permute-start | bytes 442376 | tf_op jit(solution)/shard_map/ppermute | solution.py:52
  278.5 12.8 %collective-permute-start.35 = (bf16[4,48,384]{2,1,0:T(8,128)(2,1)S(1)}, bf16[4,48,384]{2,1,0:T(8,128)(2,1)S(1)}, u32[]{:S(2)}, u32[]{:S(2)}) collective-permute-start(bf16[4,48,384]{2,1,0:T(8,128)(2,1)S(1)} %get-tuple-element.347), channel_id=1, source_target_pairs={{0,12},{1,13},{2,14},{3,15},{4,8},{5,9},{6,10},{7,11},{8,4},{9,5},... | collective-permute-start | bytes 442376 | tf_op jit(solution)/shard_map/ppermute | solution.py:52
  280.4 10.9 %collective-permute-start.36 = (bf16[4,48,384]{2,1,0:T(8,128)(2,1)S(1)}, bf16[4,48,384]{2,1,0:T(8,128)(2,1)S(1)}, u32[]{:S(2)}, u32[]{:S(2)}) collective-permute-start(bf16[4,48,384]{2,1,0:T(8,128)(2,1)S(1)} %fusion.14.refs_2_), channel_id=1, source_target_pairs={{0,16},{16,0},{1,17},{17,1},{2,18},{18,2},{3,19},{19,3},{4,20},{20... | collective-permute-start | bytes 442376 | tf_op jit(solution)/shard_map/ppermute | solution.py:55
  291.3 6.6 %copy-start.17 = (bf16[4,48,384]{2,1,0:T(8,128)(2,1)}, bf16[4,48,384]{2,1,0:T(8,128)(2,1)S(1)}, u32[]{:S(2)}) copy-start(bf16[4,48,384]{2,1,0:T(8,128)(2,1)S(1)} %collective-permute-done.36.refs_3_) | copy-start | bytes 442372
  291.4 6.5 %copy-start.9 = (bf16[4,48,384]{2,1,0:T(8,128)(2,1)}, bf16[4,48,384]{2,1,0:T(8,128)(2,1)S(1)}, u32[]{:S(2)}) copy-start(bf16[4,48,384]{2,1,0:T(8,128)(2,1)S(1)} %fusion.17.refs_4_) | copy-start | bytes 442372
  291.4 5.2 %collective-permute-start.37 = (bf16[4,48,384]{2,1,0:T(8,128)(2,1)S(1)}, bf16[4,48,384]{2,1,0:T(8,128)(2,1)S(1)}, u32[]{:S(2)}, u32[]{:S(2)}) collective-permute-start(bf16[4,48,384]{2,1,0:T(8,128)(2,1)S(1)} %fusion.17.refs_4_), channel_id=1, source_target_pairs={{0,16},{16,0},{1,17},{17,1},{2,18},{18,2},{3,19},{19,3},{4,20},{20... | collective-permute-start | bytes 442376 | tf_op jit(solution)/shard_map/ppermute | solution.py:55
  296.6 1.3 copy-start.18
Sparse Core Ops, SparseCore 0:
  43.2 71.0 all-gather.1
  139.6 82.1 reduce-scatter.1

commit v3 on v2

--- a/solution.py
+++ b/solution.py
@@ -635,7 +635,7 @@
     )(*args)
 
 
-PAIR = 2
+PAIR = 3
 
 
 def middle_kernel(rows, resid, acc, gn, grad, vec, w, out_o, low_o, da_o, sums_o):

time: 312 us -> 312 us (level)
  no operation moved by 1% of the time
where the time goes in v3:
time: 312 us; the launch traced here: 308 us
  Pallas kernels  159 us (51%)
  waiting for transfers between devices  62.7 us (20%)
  starting transfers between devices  50.8 us (16%)
  between operations  14.8 us (5%)
  local copies, waits for them, and re-layouts  10.4 us (3%)
  other arithmetic  10.3 us (3%)
    pallas_call x2, Pallas kernels, feed_call(): pl.pallas_call(functools.partial(feed_kernel, place, weight.kind, form, l...  60.3 us
    pallas_call x1, Pallas kernels, attend_back_call(): pl.pallas_call(functools.partial(attend_back_kernel, place, kind, rows, m...  28.9 us
    ppermute x15, starting transfers between devices, along_z(): return lambda v: lax.ppermute(v, 'fsdp', self.swap(4 * d))  24.1 us
    pallas_call x2, Pallas kernels, attend_call(): pl.pallas_call(functools.partial(attend_kernel, place, weight.kind, len(w...  21.9 us
    ppermute x15, waiting for transfers between devices, along_z(): return lambda v: lax.ppermute(v, 'fsdp', self.swap(4 * d))  19.1 us
    all_to_all x1, waiting for transfers between devices, local(): late = lax.all_to_all(late, ('rep', 'fsdp'), 0, 0, tiled=True)  16.6 us
    pallas_call x1, Pallas kernels, last_call(): pl.pallas_call(functools.partial(last_kernel, rows, [d.shape[0] for d in...  13.5 us
    pallas_call x1, Pallas kernels, middle_call(): pl.pallas_call(kernel, grid=(rows.images // PAIR,), in_specs=[block] * 4...  12.1 us
  transfers between devices with their start and end apart: 41, of which 16 were waited for; matrix products, arithmetic and copies ran while one was open for 3% of the time, Pallas kernels for 50%

profile of v3, /device:TPU:0, one launch (start us, length us, event | category | flops | bytes accessed | tf_op | source)
XLA Modules:
  0.0 308.0 jit_solution(2237008425624792678)
XLA Ops:
  7.2 1.2 broadcast_in_dim.39.refs_9_
  8.4 2.5 pack.1
  10.9 3.1 collective-permute-start
  14.0 2.6 collective-permute-start.1
  16.6 5.2 %pad_rows.1 = (bf16[1248,768]{1,0:T(8,128)(2,1)}, bf16[1248,768]{1,0:T(8,128)(2,1)}) custom-call(bf16[1176,768]{1,0:T(8,128)(2,1)} %tokens, bf16[1176,768]{1,0:T(8,128)(2,1)} %grads), custom_call_target="tpu_custom_call" | custom-call | flops 57500000 | bytes 150000 | tf_op jit(solution)/shard_map/pad_rows/pallas_call | solution.py:327
  21.8 2.8 collective-permute-done.1
  24.6 0.8 fusion.18
  25.4 1.5 collective-permute-start.3
  26.9 1.6 collective-permute-start.6
  28.6 1.4 collective-permute-start.7
  30.0 1.4 collective-permute-start.8
  31.3 3.1 collective-permute-done.3
  34.5 1.7 collective-permute-done.5.refs_3_
  37.1 0.8 reshape.93.vec
  37.9 5.1 %norm_one.1 = (bf16[1248,768]{1,0:T(8,128)(2,1)}, bf16[1248,768]{1,0:T(8,128)(2,1)}) custom-call(bf16[1248,768]{1,0:T(8,128)(2,1)} %get-tuple-element.212.tokens, s32[6,196]{1,0:T(8,128)} %flags.3, f32[16,768]{1,0:T(8,128)} %reshape.93.vec), custom_call_target="tpu_custom_call" | custom-call | flops 57500000 | bytes 150000 | tf_op jit(solution)/shard_map/norm_one/pallas_call | solution.py:341
  43.6 1.6 collective-permute-start.10
  45.2 1.4 collective-permute-start.11
  47.2 2.4 collective-permute-start.12
  49.5 1.0 collective-permute-start.13
  50.5 4.2 %collective-permute-done.12 = bf16[4,48,384]{2,1,0:T(8,128)(2,1)S(1)} collective-permute-done((bf16[4,48,384]{2,1,0:T(8,128)(2,1)S(1)}, bf16[4,48,384]{2,1,0:T(8,128)(2,1)S(1)}, u32[]{:S(2)}, u32[]{:S(2)}) %collective-permute-start.12) | collective-permute-done | bytes 147488 | tf_op jit(solution)/shard_map/ppermute | solution.py:52
  54.7 1.5 collective-permute-start.14
  56.3 8.5 %attend.2 = (bf16[3,1248,256]{2,1,0:T(8,128)(2,1)}, bf16[3,1248,256]{2,1,0:T(8,128)(2,1)}, bf16[3,1248,256]{2,1,0:T(8,128)(2,1)}, bf16[3,1248,256]{2,1,0:T(8,128...) custom-call(bf16[1248,768]{1,0:T(8,128)(2,1)} %get-tuple-element.259.norm, ...), custom_call_target="tpu_custom_call" | custom-call | flops 92000000 | bytes 240000 | tf_op jit(solution)/shard_map/attend/pallas_call | solution.py:493
  64.8 2.2 collective-permute-done.13
  66.9 2.8 collective-permute-done.9
  70.2 1.6 collective-permute-start.15
  71.8 1.5 collective-permute-start.16
  73.9 1.2 copy-done.2
  75.1 13.4 %attend.3 = (bf16[3,1248,256]{2,1,0:T(8,128)(2,1)}, bf16[3,1248,256]{2,1,0:T(8,128)(2,1)}, bf16[3,1248,256]{2,1,0:T(8,128)(2,1)}, bf16[3,1248,256]{2,1,0:T(8,128...) custom-call(bf16[1248,768]{1,0:T(8,128)(2,1)} %get-tuple-element.259, ...), custom_call_target="tpu_custom_call", output_to_operand_aliasing={{0}: (4, {}), {1}: (5, {}), {2}: (6, {}), {3}: (7, {}), {4}... | custom-call | flops 161000000 | bytes 420000 | tf_op jit(solution)/shard_map/attend/pallas_call | solution.py:493
  88.5 2.6 collective-permute-done.15
  91.2 1.4 collective-permute-start.18
  92.7 2.4 collective-permute-start.19
  95.1 6.8 %project.1 = (f32[1248,768]{1,0:T(8,128)}, bf16[1248,768]{1,0:T(8,128)(2,1)}, bf16[1,768,768]{2,1,0:T(8,128)(2,1)}) custom-call(f32[16,768]{1,0:T(8,128)} %reshape.93.vec, bf16[1248,768]{1,0:T(8,128)(2,1)} %get-tuple-element.213.base, bf16[3,1248,256]{2,1,0:T(8,128)(2,1)} %get-tuple-element.271.att.refs_5_, bf16[4,4,3,48,384]{4,3,2,1,0:T(8,128)(2,1)} %copy-done, ...), custom_call_target="tpu_custom_call" | custom-call | flops 80500000 | bytes 210000 | tf_op jit(solution)/shard_map/project/pallas_call | solution.py:537
  101.9 3.1 collective-permute-done.19
  105.5 4.5 %collective-permute-done.20.refs_1_ = bf16[4,4,4,48,384]{4,3,2,1,0:T(8,128)(2,1)S(1)} collective-permute-done((bf16[4,4,4,48,384]{4,3,2,1,0:T(8,128)(2,1)S(1)}, bf16[4,4,4,48,384]{4,3,2,1,0:T(8,128)(2,1)S(1)}, u32[]{:S(2)}, u32[]{:S(2)}) %collective-permute-start.20) | collective-permute-done | bytes 2359328 | tf_op jit(solution)/shard_map/ppermute | solution.py:46
  110.0 1.5 copy-done.7
  111.5 28.0 %feed.2 = (f32[1248,768]{1,0:T(8,128)}, f32[1248,768]{1,0:T(8,128)}, f32[2,1,768]{2,1,0:T(1,128)}, bf16[4,768,768]{2,1,0:T(8,128)(2,1)}) custom-call(bf16[1248,768]{1,0:T(8,128)(2,1)} %get-tuple-element.281.norm, bf16[1248,768]{1,0:T(8,128)(2,1)} %get-tuple-element.282.grad, f32[16,768]{1,0:T(8,128)} %reshape.93.vec, bf16[4,4,4,48,384]{4,3,2,1,0:T(8,128)(2,1)} %copy-done.1, ...), custom_call_target="tpu_custom_call" | custom-call | flops 345000000 | bytes 900000 | tf_op jit(solution)/shard_map/feed/pallas_call | solution.py:625
  139.5 32.3 %feed.3 = (f32[1248,768]{1,0:T(8,128)}, f32[1248,768]{1,0:T(8,128)}, f32[2,1,768]{2,1,0:T(1,128)}, bf16[2,2,4,4,48,384]{5,4,3,2,1,0:T(8,128)(2,1)}, bf16[2,2,4,4,48,384]{5,4,3,2,1,0:T(8,128)(2,1)}) custom-call(bf16[1248,768]{1,0:T(8,128)(2,1)} %get-tuple-element.281.norm, bf16[1248,768]{1,0:T(8,128)(2,1)} %get-tuple-element.282.grad, ...), custom_call_target="tpu_custom_call" | custom-call | flops 345000000 | bytes 900000 | tf_op jit(solution)/shard_map/feed/pallas_call | solution.py:625
  171.9 12.1 %middle.1 = (bf16[1176,768]{1,0:T(8,128)(2,1)}, bf16[1248,768]{1,0:T(8,128)(2,1)}, bf16[1248,768]{1,0:T(8,128)(2,1)}, f32[4,768]{1,0:T(4,128)}) custom-call(f32[1248,768]{1,0:T(8,128)} %get-tuple-element.272.resid, f32[1248,768]{1,0:T(8,128)} %get-tuple-element.290.acc, f32[1248,768]{1,0:T(8,128)} %get-tuple-element.291.gn, ...), custom_call_target="tpu_custom_call" | custom-call | flops 138000000 | bytes 360000 | tf_op jit(solution)/shard_map/middle/pallas_call | solution.py:688
  184.5 0.9 copy-done.6
  185.4 1.5 collective-permute-start.22
  187.0 1.9 collective-permute-start.23
  188.9 28.9 %attend_back.1 = (bf16[3,1248,768]{2,1,0:T(8,128)(2,1)}, f32[3,1,768]{2,1,0:T(1,128)}, bf16[2,2,4,4,48,384]{5,4,3,2,1,0:T(8,128)(2,1)}, bf16[2,2,4,4,48,384]{5,4,3,2,1,0:T(8,128)(2,1)}) custom-call(bf16[1248,768]{1,0:T(8,128)(2,1)} %get-tuple-element.259.norm, bf16[1248,768]{1,0:T(8,128)(2,1)} %get-tuple-element.302.da, ...), custom_call_target="tpu_custom_call" | custom-call | flops 379500000 | bytes 990000 | tf_op jit(solution)/shard_map/attend_back/pallas_call | solution.py:766
  218.1 3.7 %reduce-scatter.2.cloned.1.call-done.refs_0_ = bf16[4,48,768]{2,1,0:T(8,128)(2,1)} async-done(((bf16[4,768,768]{2,1,0:T(8,128)(2,1)}), bf16[4,48,768]{2,1,0:T(8,128)(2,1)}) %reduce-scatter.2.cloned.1.call-update) | async-done | bytes 294928 | tf_op jit(solution)/shard_map/reduce_scatter | solution.py:897
  221.8 1.5 collective-permute-start.26
  223.2 13.5 %last.1 = (f32[1176,768]{1,0:T(8,128)}, f32[32,16,48]{2,1,0:T(8,128)}) custom-call(bf16[1248,768]{1,0:T(8,128)(2,1)} %get-tuple-element.213.base, bf16[1248,768]{1,0:T(8,128)(2,1)} %get-tuple-element.307.refs_4_.low, s32[6,196]{1,0:T(8,128)} %flags.3, f32[16,768]{1,0:T(8,128)} %reshape.93.vec, bf16[3,768,768]{2,1,0:T(8,128)(2,1)} %get-tuple-element.319.w, ...), custom_call_target="tpu_custom_call" | custom-call | flops 17250000896 | bytes 45000000 | tf_op jit(solution)/shard_map/last/pallas_call | solution.py:848
  236.7 2.1 fusion.5
  239.6 1.5 fusion.11
  242.7 2.4 collective-permute-start.29
  245.7 0.9 reshape.96
  246.5 3.9 %all-to-all-start = ((f32[32,1,768]{2,1,0:T(1,128)}), f32[32,1,768]{2,1,0:T(1,128)S(1)}, u32[]{:S(2)}, u32[]{:S(2)}) async-start(f32[32,1,768]{2,1,0:T(1,128)} %reshape.96), calls=%async_computation.1 | async-start | bytes 196608 | tf_op jit(solution)/shard_map/all_to_all | solution.py:988
  250.4 2.7 collective-permute-start.31
  253.2 1.5 collective-permute-start.32
  254.6 16.6 %all-to-all-done = f32[32,1,768]{2,1,0:T(1,128)S(1)} async-done(((f32[32,1,768]{2,1,0:T(1,128)}), f32[32,1,768]{2,1,0:T(1,128)S(1)}, u32[]{:S(2)}, u32[]{:S(2)}) %all-to-all-start) | async-done | bytes 98336 | tf_op jit(solution)/shard_map/all_to_all | solution.py:988
  271.8 0.9 reduce
  272.9 2.0 fusion.2
  274.9 1.1 fusion.14.refs_2_
  276.1 1.5 collective-permute-start.33
  277.6 1.0 collective-permute-start.34
  278.6 1.9 collective-permute-start.35
  280.5 1.1 collective-permute-start.36
  281.6 2.7 collective-permute-done.33
  284.4 7.2 %collective-permute-done.34 = bf16[4,48,384]{2,1,0:T(8,128)(2,1)S(1)} collective-permute-done((bf16[4,48,384]{2,1,0:T(8,128)(2,1)S(1)}, bf16[4,48,384]{2,1,0:T(8,128)(2,1)S(1)}, u32[]{:S(2)}, u32[]{:S(2)}) %collective-permute-start.34) | collective-permute-done | bytes 147488 | tf_op jit(solution)/shard_map/ppermute | solution.py:52
  292.3 4.6 %collective-permute-done.37.refs_5_ = bf16[4,48,384]{2,1,0:T(8,128)(2,1)S(1)} collective-permute-done((bf16[4,48,384]{2,1,0:T(8,128)(2,1)S(1)}, bf16[4,48,384]{2,1,0:T(8,128)(2,1)S(1)}, u32[]{:S(2)}, u32[]{:S(2)}) %collective-permute-start.37) | collective-permute-done | bytes 147488 | tf_op jit(solution)/shard_map/ppermute | solution.py:55
  298.1 2.8 unpack.1
  (114 shorter events, 10.3 us)
Async XLA Ops:
  7.2 132.4 %all-gather.2.cloned.1.call-start = ((), (), s32[]{:S(2)}) async-start(), calls=%async_computation.2 | async-start | bytes 5013504 | tf_op jit(solution)/shard_map/all_gather | solution.py:894
  10.9 10.9 %copy-start.13 = (bf16[4,48,768]{2,1,0:T(8,128)(2,1)S(1)}, bf16[4,48,768]{2,1,0:T(8,128)(2,1)}, u32[]{:S(2)}) copy-start(bf16[4,48,768]{2,1,0:T(8,128)(2,1)} %get-tuple-element.201) | copy-start | bytes 884740
  10.9 10.9 %collective-permute-start = (bf16[1,64,768]{2,1,0:T(8,128)(2,1)}, bf16[1,64,768]{2,1,0:T(8,128)(2,1)S(1)}, u32[]{:S(2)}, u32[]{:S(2)}) collective-permute-start(bf16[1,64,768]{2,1,0:T(8,128)(2,1)} %get-tuple-element.193), channel_id=1, source_target_pairs={{0,4},{1,5},{2,6},{3,7},{4,0},{5,1},{6,2},{7,3},{8,12},{9,13},{10,... | collective-permute-start | bytes 294920 | tf_op jit(solution)/shard_map/ppermute | solution.py:52
  14.0 10.6 %collective-permute-start.1 = (bf16[1,64,768]{2,1,0:T(8,128)(2,1)}, bf16[1,64,768]{2,1,0:T(8,128)(2,1)S(1)}, u32[]{:S(2)}, u32[]{:S(2)}) collective-permute-start(bf16[1,64,768]{2,1,0:T(8,128)(2,1)} %get-tuple-element.193), channel_id=1, source_target_pairs={{0,8},{1,9},{2,10},{3,11},{4,12},{5,13},{6,14},{7,15},{8,0},{9,1},... | collective-permute-start | bytes 294920 | tf_op jit(solution)/shard_map/ppermute | solution.py:52
  16.6 8.1 %collective-permute-start.2 = (bf16[1,64,768]{2,1,0:T(8,128)(2,1)}, bf16[1,64,768]{2,1,0:T(8,128)(2,1)S(1)}, u32[]{:S(2)}, u32[]{:S(2)}) collective-permute-start(bf16[1,64,768]{2,1,0:T(8,128)(2,1)} %get-tuple-element.193), channel_id=1, source_target_pairs={{0,12},{1,13},{2,14},{3,15},{4,8},{5,9},{6,10},{7,11},{8,4},{9,5},... | collective-permute-start | bytes 294920 | tf_op jit(solution)/shard_map/ppermute | solution.py:52
  16.6 5.2 %copy-start.16 = (bf16[3,48,768]{2,1,0:T(8,128)(2,1)S(1)}, bf16[3,48,768]{2,1,0:T(8,128)(2,1)}, u32[]{:S(2)}) copy-start(bf16[3,48,768]{2,1,0:T(8,128)(2,1)} %get-tuple-element.200) | copy-start | bytes 663556
  16.6 8.1 %copy-start.19 = (bf16[1,64,768]{2,1,0:T(8,128)(2,1)S(1)}, bf16[1,64,768]{2,1,0:T(8,128)(2,1)}, u32[]{:S(2)}) copy-start(bf16[1,64,768]{2,1,0:T(8,128)(2,1)} %get-tuple-element.193) | copy-start | bytes 294916
  25.4 9.0 %collective-permute-start.3 = (bf16[4,1,64,768]{3,2,0,1:T(8,128)(2,1)S(1)}, bf16[4,1,64,768]{3,2,0,1:T(8,128)(2,1)S(1)}, u32[]{:S(2)}, u32[]{:S(2)}) collective-permute-start(bf16[4,1,64,768]{3,2,0,1:T(8,128)(2,1)S(1)} %get-tuple-element.204), channel_id=1, source_target_pairs={{0,2},{1,3},{2,0},{3,1},{4,6},{5,7},{6,4},{7,5},{8,10},{9,11},{10,... | collective-permute-start | bytes 1179656 | tf_op jit(solution)/shard_map/ppermute | solution.py:49
  26.9 7.5 %collective-permute-start.4 = (bf16[4,1,64,768]{3,2,0,1:T(8,128)(2,1)S(1)}, bf16[4,1,64,768]{3,2,0,1:T(8,128)(2,1)S(1)}, u32[]{:S(2)}, u32[]{:S(2)}) collective-permute-start(bf16[4,1,64,768]{3,2,0,1:T(8,128)(2,1)S(1)} %get-tuple-element.204), channel_id=1, source_target_pairs={{0,1},{1,0},{2,3},{3,2},{4,5},{5,4},{6,7},{7,6},{8,9},{9,8},{10,11... | collective-permute-start | bytes 1179656 | tf_op jit(solution)/shard_map/ppermute | solution.py:46
  26.9 16.1 %collective-permute-start.6 = (bf16[3,48,384]{2,1,0:T(8,128)(2,1)S(1)}, bf16[3,48,384]{2,1,0:T(8,128)(2,1)S(1)}, u32[]{:S(2)}, u32[]{:S(2)}) collective-permute-start(bf16[3,48,384]{2,1,0:T(8,128)(2,1)S(1)} %constant_dynamic-slice_fusion.1), channel_id=1, source_target_pairs={{0,4},{1,5},{2,6},{3,7},{4,0},{5,1},{6,2},{7,3},{8,12},{9,13},{10,... | collective-permute-start | bytes 331784 | tf_op jit(solution)/shard_map/ppermute | solution.py:52
  28.6 14.5 %collective-permute-start.7 = (bf16[3,48,384]{2,1,0:T(8,128)(2,1)S(1)}, bf16[3,48,384]{2,1,0:T(8,128)(2,1)S(1)}, u32[]{:S(2)}, u32[]{:S(2)}) collective-permute-start(bf16[3,48,384]{2,1,0:T(8,128)(2,1)S(1)} %constant_dynamic-slice_fusion.1), channel_id=1, source_target_pairs={{0,8},{1,9},{2,10},{3,11},{4,12},{5,13},{6,14},{7,15},{8,0},{9,1},... | collective-permute-start | bytes 331784 | tf_op jit(solution)/shard_map/ppermute | solution.py:52
  30.0 13.1 %collective-permute-start.8 = (bf16[3,48,384]{2,1,0:T(8,128)(2,1)S(1)}, bf16[3,48,384]{2,1,0:T(8,128)(2,1)S(1)}, u32[]{:S(2)}, u32[]{:S(2)}) collective-permute-start(bf16[3,48,384]{2,1,0:T(8,128)(2,1)S(1)} %constant_dynamic-slice_fusion.1), channel_id=1, source_target_pairs={{0,12},{1,13},{2,14},{3,15},{4,8},{5,9},{6,10},{7,11},{8,4},{9,5},... | collective-permute-start | bytes 331784 | tf_op jit(solution)/shard_map/ppermute | solution.py:52
  34.4 8.7 %copy-start.10 = (bf16[4,1,64,768]{3,2,0,1:T(8,128)(2,1)}, bf16[4,1,64,768]{3,2,0,1:T(8,128)(2,1)S(1)}, u32[]{:S(2)}) copy-start(bf16[4,1,64,768]{3,2,0,1:T(8,128)(2,1)S(1)} %collective-permute-done.3) | copy-start | bytes 1179652
  34.4 8.7 %copy-start.11 = (bf16[4,1,64,768]{3,2,0,1:T(8,128)(2,1)}, bf16[4,1,64,768]{3,2,0,1:T(8,128)(2,1)S(1)}, u32[]{:S(2)}) copy-start(bf16[4,1,64,768]{3,2,0,1:T(8,128)(2,1)S(1)} %collective-permute-done.4) | copy-start | bytes 1179652
  34.4 1.8 collective-permute-start.5
  36.2 6.9 %copy-start.12 = (bf16[4,1,64,768]{3,2,1,0:T(8,128)(2,1)}, bf16[4,1,64,768]{3,2,1,0:T(8,128)(2,1)S(1)}, u32[]{:S(2)}) copy-start(bf16[4,1,64,768]{3,2,1,0:T(8,128)(2,1)S(1)} %collective-permute-done.5.refs_3_) | copy-start | bytes 1179652
  43.1 178.6 %reduce-scatter.2.cloned.1.call-start = ((), (), s32[]{:S(2)}) async-start(), calls=%async_computation.3 | async-start | bytes 5013504 | tf_op jit(solution)/shard_map/reduce_scatter | solution.py:897
  43.6 23.3 %collective-permute-start.10 = (bf16[4,3,48,384]{3,2,1,0:T(8,128)(2,1)S(1)}, bf16[4,3,48,384]{3,2,1,0:T(8,128)(2,1)S(1)}, u32[]{:S(2)}, u32[]{:S(2)}) collective-permute-start(bf16[4,3,48,384]{3,2,1,0:T(8,128)(2,1)S(1)} %get-tuple-element.225), channel_id=1, source_target_pairs={{0,16},{16,0},{1,17},{17,1},{2,18},{18,2},{3,19},{19,3},{4,20},{20... | collective-permute-start | bytes 1327112 | tf_op jit(solution)/shard_map/ppermute | solution.py:55
  45.2 21.8 %collective-permute-start.11 = (bf16[4,3,48,384]{3,2,1,0:T(8,128)(2,1)S(1)}, bf16[4,3,48,384]{3,2,1,0:T(8,128)(2,1)S(1)}, u32[]{:S(2)}, u32[]{:S(2)}) collective-permute-start(bf16[4,3,48,384]{3,2,1,0:T(8,128)(2,1)S(1)} %get-tuple-element.225), channel_id=1, source_target_pairs={{0,18},{1,19},{2,16},{3,17},{4,22},{5,23},{6,20},{7,21},{8,26},{9,... | collective-permute-start | bytes 1327112 | tf_op jit(solution)/shard_map/ppermute | solution.py:59
  46.6 23.1 %collective-permute-start.9 = (bf16[4,3,48,384]{3,2,1,0:T(8,128)(2,1)S(1)}, bf16[4,3,48,384]{3,2,1,0:T(8,128)(2,1)S(1)}, u32[]{:S(2)}, u32[]{:S(2)}) collective-permute-start(bf16[4,3,48,384]{3,2,1,0:T(8,128)(2,1)S(1)} %get-tuple-element.225), channel_id=1, source_target_pairs={{0,2},{1,3},{2,0},{3,1},{4,6},{5,7},{6,4},{7,5},{8,10},{9,11},{10,... | collective-permute-start | bytes 1327112 | tf_op jit(solution)/shard_map/ppermute | solution.py:49
  47.2 7.6 %collective-permute-start.12 = (bf16[4,48,384]{2,1,0:T(8,128)(2,1)S(1)}, bf16[4,48,384]{2,1,0:T(8,128)(2,1)S(1)}, u32[]{:S(2)}, u32[]{:S(2)}) collective-permute-start(bf16[4,48,384]{2,1,0:T(8,128)(2,1)S(1)} %constant_dynamic-slice_fusion), channel_id=1, source_target_pairs={{0,4},{1,5},{2,6},{3,7},{4,0},{5,1},{6,2},{7,3},{8,12},{9,13},{10,... | collective-permute-start | bytes 442376 | tf_op jit(solution)/shard_map/ppermute | solution.py:52
  49.5 17.4 %collective-permute-start.13 = (bf16[4,48,384]{2,1,0:T(8,128)(2,1)S(1)}, bf16[4,48,384]{2,1,0:T(8,128)(2,1)S(1)}, u32[]{:S(2)}, u32[]{:S(2)}) collective-permute-start(bf16[4,48,384]{2,1,0:T(8,128)(2,1)S(1)} %constant_dynamic-slice_fusion), channel_id=1, source_target_pairs={{0,8},{1,9},{2,10},{3,11},{4,12},{5,13},{6,14},{7,15},{8,0},{9,1},... | collective-permute-start | bytes 442376 | tf_op jit(solution)/shard_map/ppermute | solution.py:52
  54.7 12.2 %collective-permute-start.14 = (bf16[4,48,384]{2,1,0:T(8,128)(2,1)S(1)}, bf16[4,48,384]{2,1,0:T(8,128)(2,1)S(1)}, u32[]{:S(2)}, u32[]{:S(2)}) collective-permute-start(bf16[4,48,384]{2,1,0:T(8,128)(2,1)S(1)} %constant_dynamic-slice_fusion), channel_id=1, source_target_pairs={{0,12},{1,13},{2,14},{3,15},{4,8},{5,9},{6,10},{7,11},{8,4},{9,5},... | collective-permute-start | bytes 442376 | tf_op jit(solution)/shard_map/ppermute | solution.py:52
  70.2 3.8 %copy-start = (bf16[4,4,3,48,384]{4,3,2,1,0:T(8,128)(2,1)}, bf16[4,4,3,48,384]{4,3,2,1,0:T(8,128)(2,1)S(1)}, u32[]{:S(2)}) copy-start(bf16[4,4,3,48,384]{4,3,2,1,0:T(8,128)(2,1)S(1)} %pad_maximum_fusion.1.refs_0_) | copy-start | bytes 5308420
  70.2 3.8 %collective-permute-start.17 = (bf16[4,4,3,48,384]{4,3,2,1,0:T(8,128)(2,1)S(1)}, bf16[4,4,3,48,384]{4,3,2,1,0:T(8,128)(2,1)S(1)}, u32[]{:S(2)}, u32[]{:S(2)}) collective-permute-start(bf16[4,4,3,48,384]{4,3,2,1,0:T(8,128)(2,1)S(1)} %pad_maximum_fusion.1.refs_0_), channel_id=1, source_target_pairs={{0,1},{1,0},{2,3},{3,2},{4,5},{5,4},{6,7},{7,6},{8,9},{9,8},{10,11... | collective-permute-start | bytes 5308424 | tf_op jit(solution)/shard_map/ppermute | solution.py:46
  70.2 20.9 %collective-permute-start.15 = (bf16[4,4,48,384]{3,2,1,0:T(8,128)(2,1)S(1)}, bf16[4,4,48,384]{3,2,1,0:T(8,128)(2,1)S(1)}, u32[]{:S(2)}, u32[]{:S(2)}) collective-permute-start(bf16[4,4,48,384]{3,2,1,0:T(8,128)(2,1)S(1)} %get-tuple-element.250), channel_id=1, source_target_pairs={{0,2},{1,3},{2,0},{3,1},{4,6},{5,7},{6,4},{7,5},{8,10},{9,11},{10,... | collective-permute-start | bytes 1769480 | tf_op jit(solution)/shard_map/ppermute | solution.py:49
  71.8 19.3 %collective-permute-start.16 = (bf16[4,4,48,384]{3,2,1,0:T(8,128)(2,1)S(1)}, bf16[4,4,48,384]{3,2,1,0:T(8,128)(2,1)S(1)}, u32[]{:S(2)}, u32[]{:S(2)}) collective-permute-start(bf16[4,4,48,384]{3,2,1,0:T(8,128)(2,1)S(1)} %get-tuple-element.250), channel_id=1, source_target_pairs={{0,16},{16,0},{1,17},{17,1},{2,18},{18,2},{3,19},{19,3},{4,20},{20... | collective-permute-start | bytes 1769480 | tf_op jit(solution)/shard_map/ppermute | solution.py:55
  73.9 1.2 copy-start.2
  91.2 10.7 %collective-permute-start.18 = (bf16[2,4,48,384]{3,2,1,0:T(8,128)(2,1)S(1)}, bf16[2,4,48,384]{3,2,1,0:T(8,128)(2,1)S(1)}, u32[]{:S(2)}, u32[]{:S(2)}) collective-permute-start(bf16[2,4,48,384]{3,2,1,0:T(8,128)(2,1)S(1)} %slice.124), channel_id=1, source_target_pairs={{0,16},{16,0},{1,17},{17,1},{2,18},{18,2},{3,19},{19,3},{4,20},{20... | collective-permute-start | bytes 884744 | tf_op jit(solution)/shard_map/ppermute | solution.py:55
  92.7 12.3 %collective-permute-start.19 = (bf16[2,4,48,384]{3,2,1,0:T(8,128)(2,1)S(1)}, bf16[2,4,48,384]{3,2,1,0:T(8,128)(2,1)S(1)}, u32[]{:S(2)}, u32[]{:S(2)}) collective-permute-start(bf16[2,4,48,384]{3,2,1,0:T(8,128)(2,1)S(1)} %slice.125), channel_id=1, source_target_pairs={{0,2},{1,3},{2,0},{3,1},{4,6},{5,7},{6,4},{7,5},{8,10},{9,11},{10,... | collective-permute-start | bytes 884744 | tf_op jit(solution)/shard_map/ppermute | solution.py:49
  105.4 4.6 %copy-start.1 = (bf16[4,4,4,48,384]{4,3,2,1,0:T(8,128)(2,1)}, bf16[4,4,4,48,384]{4,3,2,1,0:T(8,128)(2,1)S(1)}, u32[]{:S(2)}) copy-start(bf16[4,4,4,48,384]{4,3,2,1,0:T(8,128)(2,1)S(1)} %pad_maximum_fusion.refs_0_) | copy-start | bytes 7077892
  105.4 4.6 %collective-permute-start.20 = (bf16[4,4,4,48,384]{4,3,2,1,0:T(8,128)(2,1)S(1)}, bf16[4,4,4,48,384]{4,3,2,1,0:T(8,128)(2,1)S(1)}, u32[]{:S(2)}, u32[]{:S(2)}) collective-permute-start(bf16[4,4,4,48,384]{4,3,2,1,0:T(8,128)(2,1)S(1)} %pad_maximum_fusion.refs_0_), channel_id=1, source_target_pairs={{0,1},{1,0},{2,3},{3,2},{4,5},{5,4},{6,7},{7,6},{8,9},{9,8},{10,11... | collective-permute-start | bytes 7077896 | tf_op jit(solution)/shard_map/ppermute | solution.py:46
  110.0 1.5 copy-start.7
  171.8 12.2 %collective-permute-start.21 = (bf16[2,2,4,4,48,384]{5,4,3,2,1,0:T(8,128)(2,1)}, bf16[2,2,4,4,48,384]{5,4,3,2,1,0:T(8,128)(2,1)S(1)}, u32[]{:S(2)}, u32[]{:S(2)}) collective-permute-start(bf16[2,2,4,4,48,384]{5,4,3,2,1,0:T(8,128)(2,1)} %get-tuple-element.295), channel_id=1, source_target_pairs={{0,1},{1,0},{2,3},{3,2},{4,5},{5,4},{6,7},{7,6},{8,9},{9,8},{10,11... | collective-permute-start | bytes 7077896 | tf_op jit(solution)/shard_map/ppermute | solution.py:46
  171.9 12.1 %copy-start.5 = (bf16[2,2,4,4,48,384]{5,4,3,2,1,0:T(8,128)(2,1)S(1)}, bf16[2,2,4,4,48,384]{5,4,3,2,1,0:T(8,128)(2,1)}, u32[]{:S(2)}) copy-start(bf16[2,2,4,4,48,384]{5,4,3,2,1,0:T(8,128)(2,1)} %get-tuple-element.294) | copy-start | bytes 7077892
  184.0 1.4 copy-start.6
  185.4 32.4 %collective-permute-start.22 = (bf16[4,4,48,384]{3,2,1,0:T(8,128)(2,1)S(1)}, bf16[4,4,48,384]{3,2,1,0:T(8,128)(2,1)S(1)}, u32[]{:S(2)}, u32[]{:S(2)}) collective-permute-start(bf16[4,4,48,384]{3,2,1,0:T(8,128)(2,1)S(1)} %get-tuple-element.299), channel_id=1, source_target_pairs={{0,2},{1,3},{2,0},{3,1},{4,6},{5,7},{6,4},{7,5},{8,10},{9,11},{10,... | collective-permute-start | bytes 1769480 | tf_op jit(solution)/shard_map/ppermute | solution.py:49
  187.0 30.8 %collective-permute-start.23 = (bf16[4,4,48,384]{3,2,1,0:T(8,128)(2,1)S(1)}, bf16[4,4,48,384]{3,2,1,0:T(8,128)(2,1)}, u32[]{:S(2)}, u32[]{:S(2)}) collective-permute-start(bf16[4,4,48,384]{3,2,1,0:T(8,128)(2,1)S(1)} %get-tuple-element.300), channel_id=1, source_target_pairs={{0,16},{16,0},{1,17},{17,1},{2,18},{18,2},{3,19},{19,3},{4,20},{20... | collective-permute-start | bytes 1769480 | tf_op jit(solution)/shard_map/ppermute | solution.py:55
  188.9 29.2 %collective-permute-start.24 = (bf16[4,4,48,384]{3,2,1,0:T(8,128)(2,1)S(1)}, bf16[4,4,48,384]{3,2,1,0:T(8,128)(2,1)}, u32[]{:S(2)}, u32[]{:S(2)}) collective-permute-start(bf16[4,4,48,384]{3,2,1,0:T(8,128)(2,1)S(1)} %get-tuple-element.301), channel_id=1, source_target_pairs={{0,18},{1,19},{2,16},{3,17},{4,22},{5,23},{6,20},{7,21},{8,26},{9,... | collective-permute-start | bytes 1769480 | tf_op jit(solution)/shard_map/ppermute | solution.py:59
  221.8 17.8 %collective-permute-start.25 = (bf16[2,2,4,4,48,384]{5,4,3,2,1,0:T(8,128)(2,1)}, bf16[2,2,4,4,48,384]{5,4,3,2,1,0:T(8,128)(2,1)S(1)}, u32[]{:S(2)}, u32[]{:S(2)}) collective-permute-start(bf16[2,2,4,4,48,384]{5,4,3,2,1,0:T(8,128)(2,1)} %get-tuple-element.317), channel_id=1, source_target_pairs={{0,1},{1,0},{2,3},{3,2},{4,5},{5,4},{6,7},{7,6},{8,9},{9,8},{10,11... | collective-permute-start | bytes 7077896 | tf_op jit(solution)/shard_map/ppermute | solution.py:46
  221.8 17.8 %collective-permute-start.26 = (bf16[4,48,768]{2,1,0:T(8,128)(2,1)}, bf16[4,48,768]{2,1,0:T(8,128)(2,1)S(1)}, u32[]{:S(2)}, u32[]{:S(2)}) collective-permute-start(bf16[4,48,768]{2,1,0:T(8,128)(2,1)} %reduce-scatter.2.cloned.1.call-done.refs_0_), channel_id=1, source_target_pairs={{0,16},{16,0},{1,17},{17,1},{2,18},{18,2},{3,19},{19,3},{4,20},{20... | collective-permute-start | bytes 884744 | tf_op jit(solution)/shard_map/ppermute | solution.py:55
  236.7 2.9 copy-start.3
  239.5 1.5 copy-start.14
  239.5 2.1 copy-start.4
  239.6 6.1 %copy-start.15 = (f32[32,16,48]{2,1,0:T(8,128)S(1)}, f32[32,16,48]{2,1,0:T(8,128)}, u32[]{:S(2)}) copy-start(f32[32,16,48]{2,1,0:T(8,128)} %get-tuple-element.337) | copy-start | bytes 294916
  241.6 31.3 %collective-permute-start.27 = (bf16[4,4,48,384]{3,2,1,0:T(8,128)(2,1)}, bf16[4,4,48,384]{3,2,1,0:T(8,128)(2,1)}, u32[]{:S(2)}, u32[]{:S(2)}) collective-permute-start(bf16[4,4,48,384]{3,2,1,0:T(8,128)(2,1)} %get-tuple-element.331), channel_id=1, source_target_pairs={{0,2},{1,3},{2,0},{3,1},{4,6},{5,7},{6,4},{7,5},{8,10},{9,11},{10,... | collective-permute-start | bytes 1769480 | tf_op jit(solution)/shard_map/ppermute | solution.py:49
  242.2 30.7 %collective-permute-start.28 = (bf16[4,4,48,384]{3,2,1,0:T(8,128)(2,1)}, bf16[4,4,48,384]{3,2,1,0:T(8,128)(2,1)}, u32[]{:S(2)}, u32[]{:S(2)}) collective-permute-start(bf16[4,4,48,384]{3,2,1,0:T(8,128)(2,1)} %get-tuple-element.332), channel_id=1, source_target_pairs={{0,16},{16,0},{1,17},{17,1},{2,18},{18,2},{3,19},{19,3},{4,20},{20... | collective-permute-start | bytes 1769480 | tf_op jit(solution)/shard_map/ppermute | solution.py:55
  242.7 30.2 %collective-permute-start.29 = (bf16[4,4,48,384]{3,2,1,0:T(8,128)(2,1)}, bf16[4,4,48,384]{3,2,1,0:T(8,128)(2,1)}, u32[]{:S(2)}, u32[]{:S(2)}) collective-permute-start(bf16[4,4,48,384]{3,2,1,0:T(8,128)(2,1)} %get-tuple-element.333), channel_id=1, source_target_pairs={{0,18},{1,19},{2,16},{3,17},{4,22},{5,23},{6,20},{7,21},{8,26},{9,... | collective-permute-start | bytes 1769480 | tf_op jit(solution)/shard_map/ppermute | solution.py:59
  245.1 8.1 %collective-permute-start.30 = (bf16[4,48,384]{2,1,0:T(8,128)(2,1)S(1)}, bf16[4,48,384]{2,1,0:T(8,128)(2,1)}, u32[]{:S(2)}, u32[]{:S(2)}) collective-permute-start(bf16[4,48,384]{2,1,0:T(8,128)(2,1)S(1)} %get-tuple-element.334), channel_id=1, source_target_pairs={{0,4},{1,5},{2,6},{3,7},{4,0},{5,1},{6,2},{7,3},{8,12},{9,13},{10,... | collective-permute-start | bytes 442376 | tf_op jit(solution)/shard_map/ppermute | solution.py:52
  246.5 24.7 %all-to-all-start = ((f32[32,1,768]{2,1,0:T(1,128)}), f32[32,1,768]{2,1,0:T(1,128)S(1)}, u32[]{:S(2)}, u32[]{:S(2)}) async-start(f32[32,1,768]{2,1,0:T(1,128)} %reshape.96), calls=%async_computation.1 | async-start | bytes 196608 | tf_op jit(solution)/shard_map/all_to_all | solution.py:988
  250.4 22.4 %collective-permute-start.31 = (bf16[4,48,384]{2,1,0:T(8,128)(2,1)}, bf16[4,48,384]{2,1,0:T(8,128)(2,1)}, u32[]{:S(2)}, u32[]{:S(2)}) collective-permute-start(bf16[4,48,384]{2,1,0:T(8,128)(2,1)} %get-tuple-element.335), channel_id=1, source_target_pairs={{0,8},{1,9},{2,10},{3,11},{4,12},{5,13},{6,14},{7,15},{8,0},{9,1},... | collective-permute-start | bytes 442376 | tf_op jit(solution)/shard_map/ppermute | solution.py:52
  253.2 19.7 %collective-permute-start.32 = (bf16[4,48,384]{2,1,0:T(8,128)(2,1)S(1)}, bf16[4,48,384]{2,1,0:T(8,128)(2,1)}, u32[]{:S(2)}, u32[]{:S(2)}) collective-permute-start(bf16[4,48,384]{2,1,0:T(8,128)(2,1)S(1)} %get-tuple-element.336), channel_id=1, source_target_pairs={{0,12},{1,13},{2,14},{3,15},{4,8},{5,9},{6,10},{7,11},{8,4},{9,5},... | collective-permute-start | bytes 442376 | tf_op jit(solution)/shard_map/ppermute | solution.py:52
  276.0 22.1 %copy-start.8 = (bf16[4,48,384]{2,1,0:T(8,128)(2,1)}, bf16[4,48,384]{2,1,0:T(8,128)(2,1)S(1)}, u32[]{:S(2)}) copy-start(bf16[4,48,384]{2,1,0:T(8,128)(2,1)S(1)} %fusion.14.refs_2_) | copy-start | bytes 442372
  276.1 8.3 %collective-permute-start.33 = (bf16[4,48,384]{2,1,0:T(8,128)(2,1)S(1)}, bf16[4,48,384]{2,1,0:T(8,128)(2,1)S(1)}, u32[]{:S(2)}, u32[]{:S(2)}) collective-permute-start(bf16[4,48,384]{2,1,0:T(8,128)(2,1)S(1)} %get-tuple-element.345), channel_id=1, source_target_pairs={{0,4},{1,5},{2,6},{3,7},{4,0},{5,1},{6,2},{7,3},{8,12},{9,13},{10,... | collective-permute-start | bytes 442376 | tf_op jit(solution)/shard_map/ppermute | solution.py:52
  277.6 14.0 %collective-permute-start.34 = (bf16[4,48,384]{2,1,0:T(8,128)(2,1)S(1)}, bf16[4,48,384]{2,1,0:T(8,128)(2,1)S(1)}, u32[]{:S(2)}, u32[]{:S(2)}) collective-permute-start(bf16[4,48,384]{2,1,0:T(8,128)(2,1)S(1)} %get-tuple-element.346), channel_id=1, source_target_pairs={{0,8},{1,9},{2,10},{3,11},{4,12},{5,13},{6,14},{7,15},{8,0},{9,1},... | collective-permute-start | bytes 442376 | tf_op jit(solution)/shard_map/ppermute | solution.py:52
  278.6 12.9 %collective-permute-start.35 = (bf16[4,48,384]{2,1,0:T(8,128)(2,1)S(1)}, bf16[4,48,384]{2,1,0:T(8,128)(2,1)S(1)}, u32[]{:S(2)}, u32[]{:S(2)}) collective-permute-start(bf16[4,48,384]{2,1,0:T(8,128)(2,1)S(1)} %get-tuple-element.347), channel_id=1, source_target_pairs={{0,12},{1,13},{2,14},{3,15},{4,8},{5,9},{6,10},{7,11},{8,4},{9,5},... | collective-permute-start | bytes 442376 | tf_op jit(solution)/shard_map/ppermute | solution.py:52
  280.5 11.1 %collective-permute-start.36 = (bf16[4,48,384]{2,1,0:T(8,128)(2,1)S(1)}, bf16[4,48,384]{2,1,0:T(8,128)(2,1)S(1)}, u32[]{:S(2)}, u32[]{:S(2)}) collective-permute-start(bf16[4,48,384]{2,1,0:T(8,128)(2,1)S(1)} %fusion.14.refs_2_), channel_id=1, source_target_pairs={{0,16},{16,0},{1,17},{17,1},{2,18},{18,2},{3,19},{19,3},{4,20},{20... | collective-permute-start | bytes 442376 | tf_op jit(solution)/shard_map/ppermute | solution.py:55
  291.6 6.6 %copy-start.17 = (bf16[4,48,384]{2,1,0:T(8,128)(2,1)}, bf16[4,48,384]{2,1,0:T(8,128)(2,1)S(1)}, u32[]{:S(2)}) copy-start(bf16[4,48,384]{2,1,0:T(8,128)(2,1)S(1)} %collective-permute-done.36.refs_3_) | copy-start | bytes 442372
  291.6 6.5 %copy-start.9 = (bf16[4,48,384]{2,1,0:T(8,128)(2,1)}, bf16[4,48,384]{2,1,0:T(8,128)(2,1)S(1)}, u32[]{:S(2)}) copy-start(bf16[4,48,384]{2,1,0:T(8,128)(2,1)S(1)} %fusion.17.refs_4_) | copy-start | bytes 442372
  291.7 5.2 %collective-permute-start.37 = (bf16[4,48,384]{2,1,0:T(8,128)(2,1)S(1)}, bf16[4,48,384]{2,1,0:T(8,128)(2,1)S(1)}, u32[]{:S(2)}, u32[]{:S(2)}) collective-permute-start(bf16[4,48,384]{2,1,0:T(8,128)(2,1)S(1)} %fusion.17.refs_4_), channel_id=1, source_target_pairs={{0,16},{16,0},{1,17},{17,1},{2,18},{18,2},{3,19},{19,3},{4,20},{20... | collective-permute-start | bytes 442376 | tf_op jit(solution)/shard_map/ppermute | solution.py:55
  296.9 1.3 copy-start.18
Sparse Core Ops, SparseCore 0:
  43.2 71.0 all-gather.1
  139.6 82.0 reduce-scatter.1
